TPU v7x, 128 devices: a whole 4x4x4 slice. The times are simulated.
128 devices in a mesh: row: 8 (over x_hi, y), col: 16 (over z, x_lo, core).
Axes of the slice: x: 4 (x_hi: 2, x_lo: 2; x = x_hi * 2 + x_lo), y: 4, z: 4, core: 2. Of those that a mesh axis runs over, the one named last changes fastest.
Arguments:
- left_matrix: bfloat16 [32768, 8192], P('row', 'col'), may hold values from -6 to 6
- left_pattern: int32 [256, 64], P('row', 'col'), may hold values from 0 to 1, as said below
- right_matrix: bfloat16 [8192, 16384], P('row', 'col'), may hold values from -0.25 to 0.25
- right_pattern: int32 [64, 128], P('row', 'col'), may hold values from 0 to 1, as said below
- keep_mask: int32 [256, 128], P('row', 'col'), may hold values 0 or 1
Outputs:
- partial_product: bfloat16 [32768, 16384], P('row', 'col')
Inputs may be any that keep to these rules, and one draw needn't show every extreme that they name: `left_pattern`: 1 where the block is present; in each aligned tile of 32 block rows by 4 block columns exactly 16 entries are 1. `right_pattern`: 1 where the block is present; in each aligned tile of 4 block rows by 8 block columns exactly 4 entries are 1. `keep_mask`: 1 where the product's block is kept.
All inputs are finite; a program needn't handle non-finite values.
Results may differ from a plain program's by a relative error of at most 0.001.
Values may be sent and summed in bfloat16 or wider, within the bound.
No kernel may reach another device: no remote copies, remote signals or barrier semaphores. Data moves between devices by JAX's collectives and lax.ppermute only.
A program may use at most 192 MiB of HBM per device.

v0:
```python
import jax
import jax.numpy as jnp
from jax import lax
from jax.sharding import PartitionSpec as P


def shortened(value):

    def short(part):
        return part.astype(jnp.bfloat16) if part.dtype == jnp.float32 else part

    return jax.tree.map(short, value)


def shifted(value, axis, steps):
    count = lax.axis_size(axis)
    pairs = [(source, (source + steps) % count) for source in range(count)]
    return lax.ppermute(value, axis, pairs)


def masked(tile, pattern):
    nrb, ncb = pattern.shape
    side_r = tile.shape[0] // nrb
    side_c = tile.shape[1] // ncb
    shaped = tile.reshape(nrb, side_r, ncb, side_c)
    return (shaped * pattern[:, None, :, None].astype(tile.dtype)).reshape(tile.shape)


def choose(flag, fresh, stale):
    return tuple((jnp.where(flag, new_part, old_part) for new_part, old_part in zip(fresh, stale)))


def narrow(pair, part, seg_rows, side):
    return (
        lax.dynamic_slice_in_dim(pair[0], part * seg_rows * side, seg_rows * side, 0),
        lax.dynamic_slice_in_dim(pair[1], part * seg_rows, seg_rows, 0),
    )


def product(left_pair, right_pair):
    left_m = masked(left_pair[0], left_pair[1])
    right_m = masked(right_pair[0], right_pair[1])
    return jnp.dot(left_m, right_m, preferred_element_type=jnp.float32)


def on_device(left_matrix, left_pattern, right_matrix, right_pattern, keep_mask):
    rows_n = lax.axis_size("row")
    cols_n = lax.axis_size("col")
    group = cols_n // rows_n
    levels = rows_n.bit_length() - 1
    row_at = lax.axis_index("row")
    col_at = lax.axis_index("col")
    seg_rows = left_pattern.shape[1]
    side = left_matrix.shape[1] // seg_rows
    part = col_at % group
    b_source = (right_matrix, right_pattern)
    a_source = (left_matrix, left_pattern)
    a_moved = a_source
    for level in range(levels):
        fresh = jax.tree.map(
            lambda part, own: part.astype(own.dtype),
            shifted(shortened(a_moved), "col", -(group << level)),
            a_moved,
        )
        a_moved = choose(row_at >> level & 1 == 1, fresh, a_moved)
    a_second = jax.tree.map(
        lambda part, own: part.astype(own.dtype),
        shifted(shortened(a_moved), "col", -group),
        a_moved,
    )
    offset = col_at // group
    b_moved = b_source
    for level in range(levels):
        fresh = jax.tree.map(
            lambda part, own: part.astype(own.dtype),
            shifted(shortened(b_moved), "row", -(1 << level)),
            b_moved,
        )
        b_moved = choose(offset >> level & 1 == 1, fresh, b_moved)
    b_first = b_moved
    b_second = jax.tree.map(
        lambda part, own: part.astype(own.dtype), shifted(shortened(b_first), "row", -1), b_first
    )
    b_first = narrow(b_first, part, seg_rows, side)
    b_second = narrow(b_second, part, seg_rows, side)
    total = product(a_moved, b_first) + product(a_second, b_second)
    return masked(total, keep_mask).astype(jnp.bfloat16)


def solution(mesh):
    in_specs = (P("row", "col"), P("row", "col"), P("row", "col"), P("row", "col"), P("row", "col"))
    out_specs = P("row", "col")
    return jax.shard_map(
        on_device, mesh=mesh, in_specs=in_specs, out_specs=out_specs, check_vma=False
    )
```

profile of v0, /device:TPU:52, one launch (start us, length us, event | category | flops | bytes accessed | tf_op | source)
XLA Modules:
  0.0 489.0 jit_solution(1744113827839149907)
XLA Ops:
  0.0 0.7 collective-permute-start
  0.7 91.9 %collective-permute-done = bf16[4096,512]{1,0:T(8,128)(2,1)} collective-permute-done((bf16[4096,512]{1,0:T(8,128)(2,1)}, bf16[4096,512]{1,0:T(8,128)(2,1)}, u32[]{:S(2)}, u32[]{:S(2)}) %collective-permute-start) | collective-permute-done | bytes 4194336 | tf_op jit(solution)/shard_map/ppermute | solution.py:18
  92.6 4.6 broadcast_select_fusion
  97.3 2.3 collective-permute-start.1
  99.6 0.5 collective-permute-start.6
  100.0 89.2 %collective-permute-done.1 = bf16[4096,512]{1,0:T(8,128)(2,1)} collective-permute-done((bf16[4096,512]{1,0:T(8,128)(2,1)}, bf16[4096,512]{1,0:T(8,128)(2,1)}, u32[]{:S(2)}, u32[]{:S(2)}) %collective-permute-start.1) | collective-permute-done | bytes 4194336 | tf_op jit(solution)/shard_map/ppermute | solution.py:18
  189.2 4.6 broadcast_select_fusion.1
  193.8 4.0 collective-permute-start.2
  197.8 0.0 collective-permute-done.6
  197.8 1.8 broadcast_select_fusion.3
  199.7 0.4 collective-permute-start.7
  200.1 1.0 copy-done
  201.0 48.0 %collective-permute-done.7 = bf16[1024,1024]{1,0:T(8,128)(2,1)} collective-permute-done((bf16[1024,1024]{1,0:T(8,128)(2,1)S(1)}, bf16[1024,1024]{1,0:T(8,128)(2,1)}, u32[]{:S(2)}, u32[]{:S(2)}) %collective-permute-start.7) | collective-permute-done | bytes 2097184 | tf_op jit(solution)/shard_map/ppermute | solution.py:18
  249.1 1.8 broadcast_select_fusion.4
  250.9 0.6 collective-permute-start.8
  251.5 35.5 %collective-permute-done.2 = bf16[4096,512]{1,0:T(8,128)(2,1)} collective-permute-done((bf16[4096,512]{1,0:T(8,128)(2,1)}, bf16[4096,512]{1,0:T(8,128)(2,1)}, u32[]{:S(2)}, u32[]{:S(2)}) %collective-permute-start.2) | collective-permute-done | bytes 4194336 | tf_op jit(solution)/shard_map/ppermute | solution.py:18
  286.9 4.7 broadcast_select_fusion.2
  291.6 3.5 collective-permute-start.12
  295.1 4.8 collective-permute-done.8
  299.9 1.5 broadcast_select_fusion.5
  301.4 0.0 collective-permute-start.14
  301.4 3.9 collective-permute-start.3
  305.4 0.0 collective-permute-start.9
  305.4 36.8 %collective-permute-done.9 = s32[8,8]{1,0:T(8,128)S(1)} collective-permute-done((s32[8,8]{1,0:T(8,128)S(1)}, s32[8,8]{1,0:T(8,128)S(1)}, u32[]{:S(2)}, u32[]{:S(2)}) %collective-permute-start.9) | collective-permute-done | bytes 288 | tf_op jit(solution)/shard_map/ppermute | solution.py:18
  342.2 85.7 %collective-permute-start.10 = (s32[8,8]{1,0:T(8,128)S(1)}, s32[8,8]{1,0:T(8,128)S(1)}, u32[]{:S(2)}, u32[]{:S(2)}) collective-permute-start(s32[8,8]{1,0:T(8,128)S(1)} %broadcast_select_fusion.6), channel_id=1, source_target_pairs={{0,96},{16,112},{32,0},{48,16},{64,32},{80,48},{96,64},{112,80},{1... | collective-permute-start | bytes 776 | tf_op jit(solution)/shard_map/ppermute | solution.py:18
  427.9 0.1 copy.8
  428.0 2.4 collective-permute-done.10
  430.4 2.1 collective-permute-start.11
  432.5 0.0 collective-permute-done.3
  432.5 3.7 collective-permute-start.4
  436.2 0.0 collective-permute-done.11
  436.2 3.6 collective-permute-start.15
  439.8 0.0 collective-permute-done.4
  439.8 2.2 collective-permute-start.5
  442.0 2.9 collective-permute-done.5
  444.9 2.9 collective-permute-start.13
  447.9 0.0 collective-permute-done.15
  447.9 0.1 copy.6
  448.0 1.8 collective-permute-done.13
  449.8 0.1 copy.7
  449.9 0.0 collective-permute-done.14
  449.9 0.2 mul.76
  450.1 1.1 mul.73
  451.2 10.4 %fusion.1 = f32[4096,1024]{1,0:T(8,128)} fusion(bf16[4096,512]{1,0:T(8,128)(2,1)} %collective-permute-done.12, bf16[512,8,4,128]{3,2,1,0:T(4,128)(2,1)S(1)} %bitcast.28, bf16[64,8,8,128]{3,2,1,0:T(8,128)(2,1)S(1)} %bitcast.30, bf16[1024,1024]{1,0:T(8,128)(2,1)S(1)} %collective-permute-done.14, s32[]{:T(128)S(6)} %select_n.119), kind=kOutput, calls=%fused_computation.3 | convolution fusion | flops 4299161600 | bytes 27262980 | tf_op jit(solution)/shard_map/dot_general | solution.py:43
  461.6 0.2 mul.70
  461.9 1.1 mul.65
  463.0 6.9 %mul.79 = f32[32,128,8,128]{3,2,1,0:T(8,128)} broadcast(f32[32,8]{1,0:T(8,128)S(1)} %copy.8), dimensions={0,2} | broadcast | bytes 16778240 | tf_op jit(solution)/shard_map/mul | solution.py:26
  469.9 19.1 %fusion = bf16[4096,1024]{1,0:T(8,128)(2,1)} fusion(f32[512,8,8,128]{3,2,1,0:T(8,128)} %bitcast.26, f32[4096,1024]{1,0:T(8,128)} %fusion.1, bf16[4096,512]{1,0:T(8,128)(2,1)} %broadcast_select_fusion.2, bf16[512,8,4,128]{3,2,1,0:T(4,128)(2,1)S(1)} %bitcast.27, bf16[64,8,8,128]{3,2,1,0:T(8,128)(2,1)S(1)} %bitcast.29, ...), kind=kOutput, calls=%fused_computation.1 | convolution fusion | flops 4311744512 | bytes 52428804 | tf_op jit(solution)/shard_map/dot_general | solution.py:43
  (20 shorter events, 0.1 us)
Async XLA Ops:
  0.0 92.6 %collective-permute-start = (bf16[4096,512]{1,0:T(8,128)(2,1)}, bf16[4096,512]{1,0:T(8,128)(2,1)}, u32[]{:S(2)}, u32[]{:S(2)}) collective-permute-start(bf16[4096,512]{1,0:T(8,128)(2,1)} %param.5), channel_id=1, source_target_pairs={{0,14},{1,15},{2,0},{3,1},{4,2},{5,3},{6,4},{7,5},{8,6},{9,7},{10,... | collective-permute-start | bytes 12582920 | tf_op jit(solution)/shard_map/ppermute | solution.py:18
  0.7 98.8 %copy-start.1 = (bf16[1024,1024]{1,0:T(8,128)(2,1)S(1)}, bf16[1024,1024]{1,0:T(8,128)(2,1)}, u32[]{:S(2)}) copy-start(bf16[1024,1024]{1,0:T(8,128)(2,1)} %param.7) | copy-start | bytes 6291460
  97.3 91.9 %collective-permute-start.1 = (bf16[4096,512]{1,0:T(8,128)(2,1)}, bf16[4096,512]{1,0:T(8,128)(2,1)}, u32[]{:S(2)}, u32[]{:S(2)}) collective-permute-start(bf16[4096,512]{1,0:T(8,128)(2,1)} %broadcast_select_fusion), channel_id=1, source_target_pairs={{0,12},{1,13},{2,14},{3,15},{4,0},{5,1},{6,2},{7,3},{8,4},{9,5},{1... | collective-permute-start | bytes 12582920 | tf_op jit(solution)/shard_map/ppermute | solution.py:18
  99.6 98.3 %collective-permute-start.6 = (bf16[1024,1024]{1,0:T(8,128)(2,1)S(1)}, bf16[1024,1024]{1,0:T(8,128)(2,1)}, u32[]{:S(2)}, u32[]{:S(2)}) collective-permute-start(bf16[1024,1024]{1,0:T(8,128)(2,1)S(1)} %copy-done.1), channel_id=1, source_target_pairs={{0,112},{16,0},{32,16},{48,32},{64,48},{80,64},{96,80},{112,96},{1... | collective-permute-start | bytes 6291464 | tf_op jit(solution)/shard_map/ppermute | solution.py:18
  193.8 93.1 %collective-permute-start.2 = (bf16[4096,512]{1,0:T(8,128)(2,1)}, bf16[4096,512]{1,0:T(8,128)(2,1)}, u32[]{:S(2)}, u32[]{:S(2)}) collective-permute-start(bf16[4096,512]{1,0:T(8,128)(2,1)} %broadcast_select_fusion.1), channel_id=1, source_target_pairs={{0,8},{1,9},{2,10},{3,11},{4,12},{5,13},{6,14},{7,15},{8,0},{9,1},... | collective-permute-start | bytes 12582920 | tf_op jit(solution)/shard_map/ppermute | solution.py:18
  199.7 1.4 copy-start
  199.7 49.4 %collective-permute-start.7 = (bf16[1024,1024]{1,0:T(8,128)(2,1)S(1)}, bf16[1024,1024]{1,0:T(8,128)(2,1)}, u32[]{:S(2)}, u32[]{:S(2)}) collective-permute-start(bf16[1024,1024]{1,0:T(8,128)(2,1)S(1)} %broadcast_select_fusion.3), channel_id=1, source_target_pairs={{0,96},{16,112},{32,0},{48,16},{64,32},{80,48},{96,64},{112,80},{1... | collective-permute-start | bytes 6291464 | tf_op jit(solution)/shard_map/ppermute | solution.py:18
  250.9 49.0 %collective-permute-start.8 = (bf16[1024,1024]{1,0:T(8,128)(2,1)S(1)}, bf16[1024,1024]{1,0:T(8,128)(2,1)}, u32[]{:S(2)}, u32[]{:S(2)}) collective-permute-start(bf16[1024,1024]{1,0:T(8,128)(2,1)S(1)} %broadcast_select_fusion.4), channel_id=1, source_target_pairs={{0,64},{16,80},{32,96},{48,112},{64,0},{80,16},{96,32},{112,48},{1... | collective-permute-start | bytes 6291464 | tf_op jit(solution)/shard_map/ppermute | solution.py:18
  291.6 9.8 %copy-start.4 = (s32[32,4]{0,1:T(4,128)S(1)}, s32[32,4]{0,1:T(4,128)}, u32[]{:S(2)}) copy-start(s32[32,4]{0,1:T(4,128)} %param.6) | copy-start | bytes 1540
  291.6 13.7 %copy-start.2 = (s32[8,8]{1,0:T(8,128)S(1)}, s32[8,8]{1,0:T(8,128)}, u32[]{:S(2)}) copy-start(s32[8,8]{1,0:T(8,128)} %param.8) | copy-start | bytes 772
  291.6 136.3 %copy-start.3 = (s32[32,8]{0,1:T(8,128)S(1)}, s32[32,8]{0,1:T(8,128)}, u32[]{:S(2)}) copy-start(s32[32,8]{0,1:T(8,128)} %param.9) | copy-start | bytes 3076
  291.6 158.2 %collective-permute-start.12 = (bf16[4096,512]{1,0:T(8,128)(2,1)}, bf16[4096,512]{1,0:T(8,128)(2,1)}, u32[]{:S(2)}, u32[]{:S(2)}) collective-permute-start(bf16[4096,512]{1,0:T(8,128)(2,1)} %broadcast_select_fusion.2), channel_id=1, source_target_pairs={{0,14},{1,15},{2,0},{3,1},{4,2},{5,3},{6,4},{7,5},{8,6},{9,7},{10,... | collective-permute-start | bytes 12582920 | tf_op jit(solution)/shard_map/ppermute | solution.py:18
  301.4 148.5 %collective-permute-start.14 = (bf16[1024,1024]{1,0:T(8,128)(2,1)}, bf16[1024,1024]{1,0:T(8,128)(2,1)S(1)}, u32[]{:S(2)}, u32[]{:S(2)}) collective-permute-start(bf16[1024,1024]{1,0:T(8,128)(2,1)} %broadcast_select_fusion.5), channel_id=1, source_target_pairs={{0,112},{16,0},{32,16},{48,32},{64,48},{80,64},{96,80},{112,96},{1... | collective-permute-start | bytes 6291464 | tf_op jit(solution)/shard_map/ppermute | solution.py:18
  301.4 131.1 %collective-permute-start.3 = (s32[32,4]{0,1:T(4,128)S(1)}, s32[32,4]{0,1:T(4,128)S(1)}, u32[]{:S(2)}, u32[]{:S(2)}) collective-permute-start(s32[32,4]{0,1:T(4,128)S(1)} %copy-done.4), channel_id=1, source_target_pairs={{0,14},{1,15},{2,0},{3,1},{4,2},{5,3},{6,4},{7,5},{8,6},{9,7},{10,... | collective-permute-start | bytes 1544 | tf_op jit(solution)/shard_map/ppermute | solution.py:18
  305.4 36.9 %collective-permute-start.9 = (s32[8,8]{1,0:T(8,128)S(1)}, s32[8,8]{1,0:T(8,128)S(1)}, u32[]{:S(2)}, u32[]{:S(2)}) collective-permute-start(s32[8,8]{1,0:T(8,128)S(1)} %copy-done.2), channel_id=1, source_target_pairs={{0,112},{16,0},{32,16},{48,32},{64,48},{80,64},{96,80},{112,96},{1... | collective-permute-start | bytes 776 | tf_op jit(solution)/shard_map/ppermute | solution.py:18
  342.2 88.2 %collective-permute-start.10 = (s32[8,8]{1,0:T(8,128)S(1)}, s32[8,8]{1,0:T(8,128)S(1)}, u32[]{:S(2)}, u32[]{:S(2)}) collective-permute-start(s32[8,8]{1,0:T(8,128)S(1)} %broadcast_select_fusion.6), channel_id=1, source_target_pairs={{0,96},{16,112},{32,0},{48,16},{64,32},{80,48},{96,64},{112,80},{1... | collective-permute-start | bytes 776 | tf_op jit(solution)/shard_map/ppermute | solution.py:18
  430.4 5.8 %collective-permute-start.11 = (s32[8,8]{1,0:T(8,128)S(1)}, s32[8,8]{1,0:T(8,128)S(1)}, u32[]{:S(2)}, u32[]{:S(2)}) collective-permute-start(s32[8,8]{1,0:T(8,128)S(1)} %broadcast_select_fusion.7), channel_id=1, source_target_pairs={{0,64},{16,80},{32,96},{48,112},{64,0},{80,16},{96,32},{112,48},{1... | collective-permute-start | bytes 776 | tf_op jit(solution)/shard_map/ppermute | solution.py:18
  432.5 7.3 %collective-permute-start.4 = (s32[32,4]{0,1:T(4,128)S(1)}, s32[32,4]{0,1:T(4,128)S(1)}, u32[]{:S(2)}, u32[]{:S(2)}) collective-permute-start(s32[32,4]{0,1:T(4,128)S(1)} %broadcast_select_fusion.9), channel_id=1, source_target_pairs={{0,12},{1,13},{2,14},{3,15},{4,0},{5,1},{6,2},{7,3},{8,4},{9,5},{1... | collective-permute-start | bytes 1544 | tf_op jit(solution)/shard_map/ppermute | solution.py:18
  436.2 11.7 %collective-permute-start.15 = (s32[8,8]{1,0:T(8,128)S(1)}, s32[8,8]{1,0:T(8,128)S(1)}, u32[]{:S(2)}, u32[]{:S(2)}) collective-permute-start(s32[8,8]{1,0:T(8,128)S(1)} %broadcast_select_fusion.8), channel_id=1, source_target_pairs={{0,112},{16,0},{32,16},{48,32},{64,48},{80,64},{96,80},{112,96},{1... | collective-permute-start | bytes 776 | tf_op jit(solution)/shard_map/ppermute | solution.py:18
  439.8 5.1 %collective-permute-start.5 = (s32[32,4]{0,1:T(4,128)S(1)}, s32[32,4]{0,1:T(4,128)S(1)}, u32[]{:S(2)}, u32[]{:S(2)}) collective-permute-start(s32[32,4]{0,1:T(4,128)S(1)} %broadcast_select_fusion.10), channel_id=1, source_target_pairs={{0,8},{1,9},{2,10},{3,11},{4,12},{5,13},{6,14},{7,15},{8,0},{9,1},... | collective-permute-start | bytes 1544 | tf_op jit(solution)/shard_map/ppermute | solution.py:18
  444.9 4.8 collective-permute-start.13
where the time goes:
time: 498 us; the launch traced here: 489 us
  waiting for transfers between devices  313 us (63%)
  starting transfers between devices  116 us (23%)
  matrix products  29.5 us (6%)
  other arithmetic  19.2 us (4%)
  local copies, waits for them, and re-layouts  10.8 us (2%)
    ppermute x16, waiting for transfers between devices, shifted(): return lax.ppermute(value, axis, pairs)  313 us
    ppermute x16, starting transfers between devices, shifted(): return lax.ppermute(value, axis, pairs)  116 us
    dot_general x2, matrix products, product(): return jnp.dot(left_m, right_m, preferred_element_type=jnp.float32)  29.5 us
    select_n x11, other arithmetic, choose(): jnp.where(flag, new_part, old_part)  19.1 us
  transfers between devices with their start and end apart: 16, of which 9 were waited for; matrix products, arithmetic and copies ran while one was open for 3% of the time, Pallas kernels for 0%

commit v1 on v0

v1 whole, which is shorter than its diff:
```python
import functools

import jax
import jax.numpy as jnp
from jax import lax
from jax.experimental import pallas as pl
from jax.experimental.pallas import tpu as pltpu
from jax.sharding import PartitionSpec as P

BLK = 128
MR = 32
KS = 4
NC = 8
LCAP = 16
RCAP = 4
META = 16
LROWS = LCAP * BLK
PAIRS = LCAP * RCAP
TILES = MR * NC
ZROWS = 256


def block_of(ref, block_row, block_col):
    return ref.at[
        pl.ds(pl.multiple_of(block_row * BLK, BLK), BLK),
        pl.ds(pl.multiple_of(block_col * BLK, BLK), BLK),
    ]


def spec(space):
    return pl.BlockSpec(memory_space=space)


def pack_left_kernel(pattern, left, out, pos, meta, sems):
    count = 0
    starts = []
    for k in range(KS):
        starts.append(count)
        for i in range(MR):
            pos[count] = k * MR + i
            count = count + pattern[k, i]
    starts.append(count)
    copies = []
    for a in range(LCAP):
        at = pos[a]
        copies.append(
            pltpu.make_async_copy(
                block_of(left, at & (MR - 1), at >> 5), out.at[pl.ds(a * BLK, BLK), :], sems.at[a]
            )
        )
        copies[-1].start()
    lane = lax.broadcasted_iota(jnp.int32, (META, BLK), 1)
    row = jnp.zeros((META, BLK), jnp.int32)
    for a in range(LCAP):
        row = jnp.where(lane == a, pos[a], row)
    for k in range(KS + 1):
        row = jnp.where(lane == LCAP + k, starts[k], row)
    meta[...] = row.astype(jnp.float32).astype(jnp.bfloat16)
    copies.append(pltpu.make_async_copy(meta, out.at[pl.ds(LROWS, META), :], sems.at[LCAP]))
    copies[-1].start()
    for copy in copies:
        copy.wait()


def pack_left(pattern, left):
    return pl.pallas_call(
        pack_left_kernel,
        out_shape=jax.ShapeDtypeStruct((LROWS + META, BLK), jnp.bfloat16),
        in_specs=[spec(pltpu.SMEM), spec(pltpu.HBM)],
        out_specs=spec(pl.ANY),
        scratch_shapes=[
            pltpu.SMEM((LCAP + 1,), jnp.int32),
            pltpu.VMEM((META, BLK), jnp.bfloat16),
            pltpu.SemaphoreType.DMA((LCAP + 1,)),
        ],
        compiler_params=pltpu.CompilerParams(vmem_limit_bytes=52 << 20),
        cost_estimate=pl.CostEstimate(flops=0, bytes_accessed=2 << 20, transcendentals=0),
        name="pack_left",
    )(pattern.T, left)


def pack_right_kernel(pattern, right, after, out, pos, meta, sems):
    del after
    part = lax.rem(lax.axis_index("col"), 2)
    count = 0
    for k in range(KS):
        for j in range(NC):
            pos[count] = k * NC + j
            count = count + pattern[part * KS + k, j]
    copies = []
    for b in range(RCAP):
        at = pos[b]
        copies.append(
            pltpu.make_async_copy(
                block_of(right, part * KS + (at >> 3), at & (NC - 1)),
                out.at[pl.ds(0, BLK), pl.ds(b * BLK, BLK)],
                sems.at[b],
            )
        )
        copies[-1].start()
    lane = lax.broadcasted_iota(jnp.int32, (META, RCAP * BLK), 1)
    row = jnp.zeros((META, RCAP * BLK), jnp.int32)
    for b in range(RCAP):
        row = jnp.where(lane == b, pos[b], row)
    meta[...] = row.astype(jnp.float32).astype(jnp.bfloat16)
    copies.append(pltpu.make_async_copy(meta, out.at[pl.ds(BLK, META), :], sems.at[RCAP]))
    copies[-1].start()
    for copy in copies:
        copy.wait()


def pack_right(pattern, right, after):
    return pl.pallas_call(
        pack_right_kernel,
        out_shape=jax.ShapeDtypeStruct((BLK + META, RCAP * BLK), jnp.bfloat16),
        in_specs=[spec(pltpu.SMEM), spec(pltpu.HBM), spec(pl.ANY)],
        out_specs=spec(pl.ANY),
        scratch_shapes=[
            pltpu.SMEM((RCAP + 1,), jnp.int32),
            pltpu.VMEM((META, RCAP * BLK), jnp.bfloat16),
            pltpu.SemaphoreType.DMA((RCAP + 1,)),
        ],
        compiler_params=pltpu.CompilerParams(vmem_limit_bytes=52 << 20),
        cost_estimate=pl.CostEstimate(flops=0, bytes_accessed=1 << 20, transcendentals=0),
        name="pack_right",
    )(pattern, right, after)


def piece(code):
    return (
        pl.ds(pl.multiple_of((code >> 2) * BLK, BLK), BLK),
        pl.ds(pl.multiple_of((code & 3) * BLK, BLK), BLK),
    )


def products(left, right, prod):
    chunk = 512
    rhs = right[...]
    for first in range(0, LROWS, chunk):
        rows = pl.ds(first, chunk)
        prod[rows, :] = jnp.dot(left[rows, :], rhs, preferred_element_type=jnp.float32)


def gather(left_at, right_at, kept, owner, prod, slot_of):
    total = 0
    for b in range(RCAP):
        at = right_at(b)
        j = at & (NC - 1)

        def meet(a, total, b=b, j=j):
            target = (left_at(a) & (MR - 1)) * NC + j
            code = a * RCAP + b
            wanted = kept(target)
            held = owner[target]
            fresh = jnp.logical_and(wanted, held == 0)

            @pl.when(fresh)
            def _():
                owner[target] = code + 1
                slot_of[total] = code * TILES + target

            @pl.when(jnp.logical_and(wanted, held != 0))
            def _():
                rows, cols = piece(held - 1)
                more_rows, more_cols = piece(code)
                prod[rows, cols] += prod[more_rows, more_cols]

            return total + fresh.astype(jnp.int32)

        k = at >> 3
        total = lax.fori_loop(left_at(LCAP + k), left_at(LCAP + 1 + k), meet, total)
    return total


def write(total, value, slot_of, stage, out, sems):
    def copy_out(slot, target):
        return pltpu.make_async_copy(
            stage.at[slot], block_of(out, target >> 3, target & (NC - 1)), sems.at[slot]
        )

    def send(slot, carry):
        entry = slot_of[slot]
        target = entry & (TILES - 1)
        stage[slot] = value(entry >> 8, target).astype(jnp.bfloat16)
        copy_out(slot, target).start()
        return carry

    def drain(slot, carry):
        copy_out(slot, slot_of[slot] & (TILES - 1)).wait()
        return carry

    lax.fori_loop(0, total, send, 0)
    lax.fori_loop(0, total, drain, 0)


def choose(flag, first, second, held):
    @pl.when(flag == 0)
    def _():
        held[...] = first[pl.ds(0, BLK), :]

    @pl.when(flag != 0)
    def _():
        held[...] = second[pl.ds(0, BLK), :]


def first_kernel(
    keep, left, r0, r1, out, prod, table,
    zero, zero_sems, right, stage, meta_v, meta, owner, slot_of, meta_sem, out_sems,
):
    zero[...] = jnp.zeros_like(zero)
    clears = [
        pltpu.make_async_copy(zero, out.at[pl.ds(n * ZROWS, ZROWS), :], zero_sems.at[n])
        for n in range(out.shape[0] // ZROWS)
    ]
    for copy in clears:
        copy.start()
    odd = lax.rem(lax.axis_index("row"), 2)
    line = lax.broadcasted_iota(jnp.int32, (META, BLK), 0)
    rows = left[pl.ds(LROWS, META), :].astype(jnp.float32)
    for n, ref in enumerate((r0, r1)):
        more = ref[pl.ds(BLK, META), pl.ds(0, BLK)].astype(jnp.float32)
        rows = jnp.where(line == 1 + n, more, rows)
    meta_v[...] = rows.astype(jnp.int32)
    meta_copy = pltpu.make_async_copy(meta_v, meta, meta_sem)
    meta_copy.start()
    for at in range(TILES):
        owner[at] = 0
    choose(odd, r0, r1, right)
    products(left, right, prod)
    meta_copy.wait()
    total = gather(
        lambda a: meta[0, a],
        lambda b: meta[1 + odd, b],
        lambda target: keep[target >> 3, target & (NC - 1)] != 0,
        owner,
        prod,
        slot_of,
    )

    def value(code, target):
        rows, cols = piece(code)
        return prod[rows, cols]

    for copy in clears:
        copy.wait()
    write(total, value, slot_of, stage, out, out_sems)
    for i in range(MR):
        for j in range(NC):
            table[i * NC + j] = jnp.where(keep[i, j] != 0, owner[i * NC + j], -1)
    for b in range(RCAP):
        table[TILES + b] = meta[2 - odd, b]


def first(keep, left, r0, r1):
    return pl.pallas_call(
        first_kernel,
        out_shape=(
            jax.ShapeDtypeStruct((MR * BLK, NC * BLK), jnp.bfloat16),
            jax.ShapeDtypeStruct((LROWS, RCAP * BLK), jnp.float32),
            jax.ShapeDtypeStruct((TILES + BLK,), jnp.int32),
        ),
        in_specs=[spec(pltpu.SMEM)] + [spec(pltpu.VMEM)] * 3,
        out_specs=[spec(pltpu.HBM), spec(pltpu.VMEM), spec(pltpu.SMEM)],
        scratch_shapes=[
            pltpu.VMEM((ZROWS, NC * BLK), jnp.bfloat16),
            pltpu.SemaphoreType.DMA((MR * BLK // ZROWS,)),
            pltpu.VMEM((BLK, RCAP * BLK), jnp.bfloat16),
            pltpu.VMEM((PAIRS, BLK, BLK), jnp.bfloat16),
            pltpu.VMEM((META, BLK), jnp.int32),
            pltpu.SMEM((META, BLK), jnp.int32),
            pltpu.SMEM((TILES,), jnp.int32),
            pltpu.SMEM((PAIRS,), jnp.int32),
            pltpu.SemaphoreType.DMA,
            pltpu.SemaphoreType.DMA((PAIRS,)),
        ],
        compiler_params=pltpu.CompilerParams(vmem_limit_bytes=32 << 20),
        cost_estimate=pl.CostEstimate(
            flops=10**10, bytes_accessed=14 << 20, transcendentals=0
        ),
        name="first",
    )(keep, left, r0, r1)


def last_kernel(
    table, left, r0, r1, before, zero, out,
    right, prod, stage, meta_v, meta, owner, slot_of, meta_sem, out_sems,
):
    del zero
    odd = lax.rem(lax.axis_index("row"), 2)
    meta_v[...] = left[pl.ds(LROWS, META), :].astype(jnp.float32).astype(jnp.int32)
    meta_copy = pltpu.make_async_copy(meta_v, meta, meta_sem)
    meta_copy.start()
    for at in range(TILES):
        owner[at] = 0
    choose(odd, r1, r0, right)
    products(left, right, prod)
    meta_copy.wait()
    total = gather(
        lambda a: meta[0, a],
        lambda b: table[TILES + b],
        lambda target: table[target] >= 0,
        owner,
        prod,
        slot_of,
    )

    def value(code, target):
        rows, cols = piece(code)
        held = table[target]
        old_rows, old_cols = piece(jnp.maximum(held - 1, 0))
        fresh = prod[rows, cols]
        return jnp.where(held > 0, fresh + before[old_rows, old_cols], fresh)

    write(total, value, slot_of, stage, out, out_sems)


def last(table, left, r0, r1, before, out):
    return pl.pallas_call(
        last_kernel,
        out_shape=jax.ShapeDtypeStruct(out.shape, out.dtype),
        in_specs=[spec(pltpu.SMEM)] + [spec(pltpu.VMEM)] * 4 + [spec(pltpu.HBM)],
        out_specs=spec(pltpu.HBM),
        scratch_shapes=[
            pltpu.VMEM((BLK, RCAP * BLK), jnp.bfloat16),
            pltpu.VMEM((LROWS, RCAP * BLK), jnp.float32),
            pltpu.VMEM((PAIRS, BLK, BLK), jnp.bfloat16),
            pltpu.VMEM((META, BLK), jnp.int32),
            pltpu.SMEM((META, BLK), jnp.int32),
            pltpu.SMEM((TILES,), jnp.int32),
            pltpu.SMEM((PAIRS,), jnp.int32),
            pltpu.SemaphoreType.DMA,
            pltpu.SemaphoreType.DMA((PAIRS,)),
        ],
        input_output_aliases={5: 0},
        compiler_params=pltpu.CompilerParams(vmem_limit_bytes=32 << 20),
        cost_estimate=pl.CostEstimate(
            flops=2 * PAIRS * BLK**3, bytes_accessed=4 << 20, transcendentals=0
        ),
        name="last",
    )(table, left, r0, r1, before, out)


def on_device(rows_n, cols_n, left_matrix, left_pattern, right_matrix, right_pattern, keep_mask):
    group = cols_n // rows_n

    def moved(value, target):
        pairs = []
        for r in range(rows_n):
            for c in range(cols_n):
                to_r, to_c = target(r, c)
                pairs.append((r * cols_n + c, to_r % rows_n * cols_n + to_c % cols_n))
        return lax.ppermute(value, ("row", "col"), pairs)

    lpack = pack_left(left_pattern, left_matrix)
    even = moved(lpack, lambda r, c: (r, c - group * (r + r % 2)))
    rpack = pack_right(right_pattern, right_matrix, lpack)
    r0 = moved(rpack, lambda r, c: (r - c // group, c))
    r1 = moved(rpack, lambda r, c: (r - c // group - 1, c))
    other = moved(even, lambda r, c: (r, c + group * (2 * (r % 2) - 1)))
    out, before, table = first(keep_mask, even, r0, r1)
    return last(table, other, r0, r1, before, out)


def solution(mesh):
    part = P("row", "col")
    return jax.shard_map(
        functools.partial(on_device, mesh.shape["row"], mesh.shape["col"]),
        mesh=mesh,
        in_specs=(part,) * 5,
        out_specs=part,
        check_vma=False,
    )
```

time: 498 us -> 39.6 us (0.08)
  the two profiles are of different devices: /device:TPU:52 before, /device:TPU:24 now
where the time goes in v1:
time: 39.6 us; the launch traced here: 39.3 us
  waiting for transfers between devices  14.3 us (36%)
  Pallas kernels  13.4 us (34%)
  starting transfers between devices  10.8 us (27%)
  local copies, waits for them, and re-layouts  0.78 us (2%)
    ppermute x4, waiting for transfers between devices, moved(): return lax.ppermute(value, ('row', 'col'), pairs)  14.3 us
    ppermute x4, starting transfers between devices, moved(): return lax.ppermute(value, ('row', 'col'), pairs)  10.8 us
    pallas_call x1, Pallas kernels, first(): pl.pallas_call(first_kernel, out_shape=(jax.ShapeDtypeStruct((MR * BLK, N...  6.57 us
    pallas_call x1, Pallas kernels, last(): pl.pallas_call(last_kernel, out_shape=jax.ShapeDtypeStruct(out.shape, out...  3.43 us
    pallas_call x1, Pallas kernels, pack_left(): pl.pallas_call(pack_left_kernel, out_shape=jax.ShapeDtypeStruct((LROWS +...  1.91 us
    pallas_call x1, Pallas kernels, pack_right(): pl.pallas_call(pack_right_kernel, out_shape=jax.ShapeDtypeStruct((BLK + M...  1.52 us
  transfers between devices with their start and end apart: 4, of which 2 were waited for; matrix products, arithmetic and copies ran while one was open for 0% of the time, Pallas kernels for 21%

profile of v1, /device:TPU:24, one launch (start us, length us, event | category | flops | bytes accessed | tf_op | source)
XLA Modules:
  0.0 39.3 jit_solution(6126623363113999371)
XLA Ops:
  0.0 0.0 copy-start
  0.0 0.0 copy-start.1
  0.0 0.7 %copy-done.1 = s32[32,4]{0,1:T(4,128)S(1)} copy-done((s32[32,4]{0,1:T(4,128)S(1)}, s32[32,4]{0,1:T(4,128)}, u32[]{:S(2)}) %copy-start.1) | copy-done | bytes 536
  0.7 0.0 copy-start.2
  0.7 1.9 %pack_left.1.after = bf16[2064,128]{1,0:T(8,128)(2,1)S(1)} custom-call(s32[4,32]{1,0:T(4,128)S(1)} %bitcast.1, bf16[4096,512]{1,0:T(8,128)(2,1)} %left.1), custom_call_target="tpu_custom_call" | custom-call | bytes 2097152 | tf_op jit(solution)/shard_map/pack_left/pallas_call | solution.py:66
  2.6 5.8 %collective-permute-start = (bf16[2064,128]{1,0:T(8,128)(2,1)S(1)}, bf16[2064,128]{1,0:T(8,128)(2,1)S(1)}, u32[]{:S(2)}, u32[]{:S(2)}) collective-permute-start(bf16[2064,128]{1,0:T(8,128)(2,1)S(1)} %pack_left.1.after), channel_id=1, source_target_pairs={{0,0},{1,1},{2,2},{3,3},{4,4},{5,5},{6,6},{7,7},{8,8},{9,9},{10,10... | collective-permute-start | bytes 1585160 | tf_op jit(solution)/shard_map/ppermute | solution.py:352
  8.4 0.0 copy-done
  8.4 1.5 %pack_right.1 = bf16[144,512]{1,0:T(8,128)(2,1)S(1)} custom-call(s32[8,8]{1,0:T(8,128)S(1)} %copy-done, bf16[1024,1024]{1,0:T(8,128)(2,1)} %right.1, bf16[2064,128]{1,0:T(8,128)(2,1)S(1)} %pack_left.1.after), custom_call_target="tpu_custom_call" | custom-call | bytes 1048576 | tf_op jit(solution)/shard_map/pack_right/pallas_call | solution.py:113
  9.9 2.8 %collective-permute-start.2 = (bf16[144,512]{1,0:T(8,128)(2,1)S(1)}, bf16[144,512]{1,0:T(8,128)(2,1)S(1)}, u32[]{:S(2)}, u32[]{:S(2)}) collective-permute-start(bf16[144,512]{1,0:T(8,128)(2,1)S(1)} %pack_right.1), channel_id=1, source_target_pairs={{0,112},{1,113},{2,98},{3,99},{4,84},{5,85},{6,70},{7,71},{8,56},{... | collective-permute-start | bytes 442376 | tf_op jit(solution)/shard_map/ppermute | solution.py:352
  12.8 0.7 %collective-permute-start.1 = (bf16[144,512]{1,0:T(8,128)(2,1)S(1)}, bf16[144,512]{1,0:T(8,128)(2,1)S(1)}, u32[]{:S(2)}, u32[]{:S(2)}) collective-permute-start(bf16[144,512]{1,0:T(8,128)(2,1)S(1)} %pack_right.1), channel_id=1, source_target_pairs={{0,0},{1,1},{2,114},{3,115},{4,100},{5,101},{6,86},{7,87},{8,72},{... | collective-permute-start | bytes 442376 | tf_op jit(solution)/shard_map/ppermute | solution.py:352
  13.4 0.0 copy-done.2
  13.5 0.1 copy.7.keep
  13.5 6.9 %collective-permute-done.left = bf16[2064,128]{1,0:T(8,128)(2,1)S(1)} collective-permute-done((bf16[2064,128]{1,0:T(8,128)(2,1)S(1)}, bf16[2064,128]{1,0:T(8,128)(2,1)S(1)}, u32[]{:S(2)}, u32[]{:S(2)}) %collective-permute-start) | collective-permute-done | bytes 528416 | tf_op jit(solution)/shard_map/ppermute | solution.py:352
  20.4 1.5 %collective-permute-start.3 = (bf16[2064,128]{1,0:T(8,128)(2,1)S(1)}, bf16[2064,128]{1,0:T(8,128)(2,1)S(1)}, u32[]{:S(2)}, u32[]{:S(2)}) collective-permute-start(bf16[2064,128]{1,0:T(8,128)(2,1)S(1)} %collective-permute-done.left), channel_id=1, source_target_pairs={{0,14},{1,15},{2,0},{3,1},{4,2},{5,3},{6,4},{7,5},{8,6},{9,7},{10,... | collective-permute-start | bytes 1585160 | tf_op jit(solution)/shard_map/ppermute | solution.py:352
  21.9 0.0 collective-permute-done.2.r1
  21.9 0.0 collective-permute-done.1.r0
  21.9 6.6 %first.1 = (bf16[4096,1024]{1,0:T(8,128)(2,1)}, f32[2048,512]{1,0:T(8,128)S(1)}, s32[384]{0:T(512)S(1)}) custom-call(s32[32,8]{1,0:T(8,128)S(1)} %copy.7.keep, bf16[2064,128]{1,0:T(8,128)(2,1)S(1)} %collective-permute-done.left, bf16[144,512]{1,0:T(8,128)(2,1)S(1)} %collective-permute-done.1.r0, bf16[144,512]{1,0:T(8,128)(2,1)S(1)} %collective-permute-done.2.r1), custom_call_target="tpu_custom_call" | custom-call | flops 10000000000 | bytes 14680064 | tf_op jit(solution)/shard_map/first/pallas_call | solution.py:255
  28.5 7.4 %collective-permute-done.3.left = bf16[2064,128]{1,0:T(8,128)(2,1)S(1)} collective-permute-done((bf16[2064,128]{1,0:T(8,128)(2,1)S(1)}, bf16[2064,128]{1,0:T(8,128)(2,1)S(1)}, u32[]{:S(2)}, u32[]{:S(2)}) %collective-permute-start.3) | collective-permute-done | bytes 528416 | tf_op jit(solution)/shard_map/ppermute | solution.py:352
  35.9 3.4 %last.1 = bf16[4096,1024]{1,0:T(8,128)(2,1)} custom-call(s32[384]{0:T(512)S(1)} %get-tuple-element.8.table, bf16[2064,128]{1,0:T(8,128)(2,1)S(1)} %collective-permute-done.3.left, bf16[144,512]{1,0:T(8,128)(2,1)S(1)} %collective-permute-done.1.r0, bf16[144,512]{1,0:T(8,128)(2,1)S(1)} %collective-permute-done.2.r1, ...), custom_call_target="tpu_custom_call", output_to_operand_aliasing={{}: (5, {})} | custom-call | flops 268435456 | bytes 4194304 | tf_op jit(solution)/shard_map/last/pallas_call | solution.py:318
Async XLA Ops:
  0.0 8.4 %copy-start = (s32[8,8]{1,0:T(8,128)S(1)}, s32[8,8]{1,0:T(8,128)}, u32[]{:S(2)}) copy-start(s32[8,8]{1,0:T(8,128)} %pattern.1) | copy-start | bytes 772
  0.0 0.7 %copy-start.1 = (s32[32,4]{0,1:T(4,128)S(1)}, s32[32,4]{0,1:T(4,128)}, u32[]{:S(2)}) copy-start(s32[32,4]{0,1:T(4,128)} %param.6) | copy-start | bytes 1540
  0.7 12.7 %copy-start.2 = (s32[32,8]{0,1:T(8,128)S(1)}, s32[32,8]{0,1:T(8,128)}, u32[]{:S(2)}) copy-start(s32[32,8]{0,1:T(8,128)} %param.9) | copy-start | bytes 3076
  2.6 17.8 %collective-permute-start = (bf16[2064,128]{1,0:T(8,128)(2,1)S(1)}, bf16[2064,128]{1,0:T(8,128)(2,1)S(1)}, u32[]{:S(2)}, u32[]{:S(2)}) collective-permute-start(bf16[2064,128]{1,0:T(8,128)(2,1)S(1)} %pack_left.1.after), channel_id=1, source_target_pairs={{0,0},{1,1},{2,2},{3,3},{4,4},{5,5},{6,6},{7,7},{8,8},{9,9},{10,10... | collective-permute-start | bytes 1585160 | tf_op jit(solution)/shard_map/ppermute | solution.py:352
  9.9 12.0 %collective-permute-start.2 = (bf16[144,512]{1,0:T(8,128)(2,1)S(1)}, bf16[144,512]{1,0:T(8,128)(2,1)S(1)}, u32[]{:S(2)}, u32[]{:S(2)}) collective-permute-start(bf16[144,512]{1,0:T(8,128)(2,1)S(1)} %pack_right.1), channel_id=1, source_target_pairs={{0,112},{1,113},{2,98},{3,99},{4,84},{5,85},{6,70},{7,71},{8,56},{... | collective-permute-start | bytes 442376 | tf_op jit(solution)/shard_map/ppermute | solution.py:352
  12.8 9.1 %collective-permute-start.1 = (bf16[144,512]{1,0:T(8,128)(2,1)S(1)}, bf16[144,512]{1,0:T(8,128)(2,1)S(1)}, u32[]{:S(2)}, u32[]{:S(2)}) collective-permute-start(bf16[144,512]{1,0:T(8,128)(2,1)S(1)} %pack_right.1), channel_id=1, source_target_pairs={{0,0},{1,1},{2,114},{3,115},{4,100},{5,101},{6,86},{7,87},{8,72},{... | collective-permute-start | bytes 442376 | tf_op jit(solution)/shard_map/ppermute | solution.py:352
  20.4 15.5 %collective-permute-start.3 = (bf16[2064,128]{1,0:T(8,128)(2,1)S(1)}, bf16[2064,128]{1,0:T(8,128)(2,1)S(1)}, u32[]{:S(2)}, u32[]{:S(2)}) collective-permute-start(bf16[2064,128]{1,0:T(8,128)(2,1)S(1)} %collective-permute-done.left), channel_id=1, source_target_pairs={{0,14},{1,15},{2,0},{3,1},{4,2},{5,3},{6,4},{7,5},{8,6},{9,7},{10,... | collective-permute-start | bytes 1585160 | tf_op jit(solution)/shard_map/ppermute | solution.py:352

commit v2 on v1

--- a/solution.py
+++ b/solution.py
@@ -15,6 +15,7 @@
 RCAP = 4
 META = 16
 LROWS = LCAP * BLK
+HALF = LROWS // 2
 PAIRS = LCAP * RCAP
 TILES = MR * NC
 ZROWS = 256
@@ -31,7 +32,7 @@
     return pl.BlockSpec(memory_space=space)
 
 
-def pack_left_kernel(pattern, left, out, pos, meta, sems):
+def pack_left_kernel(pattern, left, out, more, pos, meta, sems):
     count = 0
     starts = []
     for k in range(KS):
@@ -43,12 +44,17 @@
     copies = []
     for a in range(LCAP):
         at = pos[a]
-        copies.append(
-            pltpu.make_async_copy(
-                block_of(left, at & (MR - 1), at >> 5), out.at[pl.ds(a * BLK, BLK), :], sems.at[a]
+        block = block_of(left, at & (MR - 1), at >> 5)
+        first_row = a * BLK if a * BLK < HALF else a * BLK + META
+        copies.append(pltpu.make_async_copy(block, out.at[pl.ds(first_row, BLK), :], sems.at[a]))
+        copies[-1].start()
+        if a * BLK >= HALF:
+            copies.append(
+                pltpu.make_async_copy(
+                    block, more.at[pl.ds(a * BLK - HALF, BLK), :], sems.at[LCAP + a - LCAP // 2]
+                )
             )
-        )
-        copies[-1].start()
+            copies[-1].start()
     lane = lax.broadcasted_iota(jnp.int32, (META, BLK), 1)
     row = jnp.zeros((META, BLK), jnp.int32)
     for a in range(LCAP):
@@ -56,7 +62,7 @@
     for k in range(KS + 1):
         row = jnp.where(lane == LCAP + k, starts[k], row)
     meta[...] = row.astype(jnp.float32).astype(jnp.bfloat16)
-    copies.append(pltpu.make_async_copy(meta, out.at[pl.ds(LROWS, META), :], sems.at[LCAP]))
+    copies.append(pltpu.make_async_copy(meta, out.at[pl.ds(HALF, META), :], sems.at[LCAP + LCAP // 2]))
     copies[-1].start()
     for copy in copies:
         copy.wait()
@@ -65,13 +71,16 @@
 def pack_left(pattern, left):
     return pl.pallas_call(
         pack_left_kernel,
-        out_shape=jax.ShapeDtypeStruct((LROWS + META, BLK), jnp.bfloat16),
+        out_shape=(
+            jax.ShapeDtypeStruct((LROWS + META, BLK), jnp.bfloat16),
+            jax.ShapeDtypeStruct((HALF, BLK), jnp.bfloat16),
+        ),
         in_specs=[spec(pltpu.SMEM), spec(pltpu.HBM)],
-        out_specs=spec(pl.ANY),
+        out_specs=[spec(pl.ANY)] * 2,
         scratch_shapes=[
             pltpu.SMEM((LCAP + 1,), jnp.int32),
             pltpu.VMEM((META, BLK), jnp.bfloat16),
-            pltpu.SemaphoreType.DMA((LCAP + 1,)),
+            pltpu.SemaphoreType.DMA((LCAP + LCAP // 2 + 1,)),
         ],
         compiler_params=pltpu.CompilerParams(vmem_limit_bytes=52 << 20),
         cost_estimate=pl.CostEstimate(flops=0, bytes_accessed=2 << 20, transcendentals=0),
@@ -133,12 +142,14 @@
     )
 
 
-def products(left, right, prod):
+def products(halves, right, prod):
     chunk = 512
     rhs = right[...]
-    for first in range(0, LROWS, chunk):
-        rows = pl.ds(first, chunk)
-        prod[rows, :] = jnp.dot(left[rows, :], rhs, preferred_element_type=jnp.float32)
+    for n, (ref, begin) in enumerate(halves):
+        for first in range(0, HALF, chunk):
+            prod[pl.ds(n * HALF + first, chunk), :] = jnp.dot(
+                ref[pl.ds(begin + first, chunk), :], rhs, preferred_element_type=jnp.float32
+            )
 
 
 def gather(left_at, right_at, kept, owner, prod, slot_of):
@@ -216,17 +227,17 @@
         copy.start()
     odd = lax.rem(lax.axis_index("row"), 2)
     line = lax.broadcasted_iota(jnp.int32, (META, BLK), 0)
-    rows = left[pl.ds(LROWS, META), :].astype(jnp.float32)
+    rows = left[pl.ds(HALF, META), :].astype(jnp.float32)
     for n, ref in enumerate((r0, r1)):
-        more = ref[pl.ds(BLK, META), pl.ds(0, BLK)].astype(jnp.float32)
-        rows = jnp.where(line == 1 + n, more, rows)
+        right_row = ref[pl.ds(BLK, META), pl.ds(0, BLK)].astype(jnp.float32)
+        rows = jnp.where(line == 1 + n, right_row, rows)
     meta_v[...] = rows.astype(jnp.int32)
     meta_copy = pltpu.make_async_copy(meta_v, meta, meta_sem)
     meta_copy.start()
     for at in range(TILES):
         owner[at] = 0
     choose(odd, r0, r1, right)
-    products(left, right, prod)
+    products(((left, 0), (left, HALF + META)), right, prod)
     meta_copy.wait()
     total = gather(
         lambda a: meta[0, a],
@@ -282,18 +293,18 @@
 
 
 def last_kernel(
-    table, left, r0, r1, before, zero, out,
+    table, left, more, r0, r1, before, zero, out,
     right, prod, stage, meta_v, meta, owner, slot_of, meta_sem, out_sems,
 ):
     del zero
     odd = lax.rem(lax.axis_index("row"), 2)
-    meta_v[...] = left[pl.ds(LROWS, META), :].astype(jnp.float32).astype(jnp.int32)
+    meta_v[...] = left[pl.ds(HALF, META), :].astype(jnp.float32).astype(jnp.int32)
     meta_copy = pltpu.make_async_copy(meta_v, meta, meta_sem)
     meta_copy.start()
     for at in range(TILES):
         owner[at] = 0
     choose(odd, r1, r0, right)
-    products(left, right, prod)
+    products(((left, 0), (more, 0)), right, prod)
     meta_copy.wait()
     total = gather(
         lambda a: meta[0, a],
@@ -314,11 +325,11 @@
     write(total, value, slot_of, stage, out, out_sems)
 
 
-def last(table, left, r0, r1, before, out):
+def last(table, left, more, r0, r1, before, out):
     return pl.pallas_call(
         last_kernel,
         out_shape=jax.ShapeDtypeStruct(out.shape, out.dtype),
-        in_specs=[spec(pltpu.SMEM)] + [spec(pltpu.VMEM)] * 4 + [spec(pltpu.HBM)],
+        in_specs=[spec(pltpu.SMEM)] + [spec(pltpu.VMEM)] * 5 + [spec(pltpu.HBM)],
         out_specs=spec(pltpu.HBM),
         scratch_shapes=[
             pltpu.VMEM((BLK, RCAP * BLK), jnp.bfloat16),
@@ -331,34 +342,59 @@
             pltpu.SemaphoreType.DMA,
             pltpu.SemaphoreType.DMA((PAIRS,)),
         ],
-        input_output_aliases={5: 0},
+        input_output_aliases={6: 0},
         compiler_params=pltpu.CompilerParams(vmem_limit_bytes=32 << 20),
         cost_estimate=pl.CostEstimate(
             flops=2 * PAIRS * BLK**3, bytes_accessed=4 << 20, transcendentals=0
         ),
         name="last",
-    )(table, left, r0, r1, before, out)
+    )(table, left, more, r0, r1, before, out)
+
+
+def detour(r, c, cols_n, group):
+    core, chip = c % group, c // group
+    z, x = chip // 2, chip % 2
+    depth = cols_n // group // 2
+    step = (r + r % 2) // 2 % depth
+    source = (chip + r + 1 - r % 2) % (cols_n // group)
+    place = source // 2
+    if step == 0:
+        place = z
+    elif 2 * step != depth and 2 * (place - z) % (2 * depth) == depth:
+        place = (place + step) % depth
+    return source * group + core, (place * 2 + x) * group + core
 
 
 def on_device(rows_n, cols_n, left_matrix, left_pattern, right_matrix, right_pattern, keep_mask):
     group = cols_n // rows_n
 
+    def send(value, pairs):
+        pairs = [(a[0] * cols_n + a[1], b[0] * cols_n + b[1]) for a, b in pairs]
+        return lax.ppermute(value, ("row", "col"), pairs)
+
+    devices = [(r, c) for r in range(rows_n) for c in range(cols_n)]
+
     def moved(value, target):
         pairs = []
-        for r in range(rows_n):
-            for c in range(cols_n):
-                to_r, to_c = target(r, c)
-                pairs.append((r * cols_n + c, to_r % rows_n * cols_n + to_c % cols_n))
-        return lax.ppermute(value, ("row", "col"), pairs)
-
-    lpack = pack_left(left_pattern, left_matrix)
-    even = moved(lpack, lambda r, c: (r, c - group * (r + r % 2)))
-    rpack = pack_right(right_pattern, right_matrix, lpack)
+        for r, c in devices:
+            to_r, to_c = target(r, c)
+            pairs.append(((r, c), (to_r % rows_n, to_c % cols_n)))
+        return send(value, pairs)
+
+    whole, half = pack_left(left_pattern, left_matrix)
+    even = moved(whole, lambda r, c: (r, c - group * (r + r % 2)))
+    roads = {at: detour(*at, cols_n, group) for at in devices}
+    between = send(half, [((r, roads[r, c][0]), (r, roads[r, c][1])) for r, c in devices])
+    rpack = pack_right(right_pattern, right_matrix, whole)
     r0 = moved(rpack, lambda r, c: (r - c // group, c))
     r1 = moved(rpack, lambda r, c: (r - c // group - 1, c))
-    other = moved(even, lambda r, c: (r, c + group * (2 * (r % 2) - 1)))
+    passed = moved(
+        lax.slice_in_dim(even, 0, HALF + META),
+        lambda r, c: (r, c + group * (2 * (r % 2) - 1)),
+    )
+    more = send(between, [((r, roads[r, c][1]), (r, c)) for r, c in devices])
     out, before, table = first(keep_mask, even, r0, r1)
-    return last(table, other, r0, r1, before, out)
+    return last(table, passed, more, r0, r1, before, out)
 
 
 def solution(mesh):

time: 39.6 us -> 36.8 us (0.929)
  the two profiles are of different devices: /device:TPU:24 before, /device:TPU:52 now
where the time goes in v2:
time: 36.8 us; the launch traced here: 36.4 us
  starting transfers between devices  17.2 us (47%)
  Pallas kernels  13.5 us (37%)
  waiting for transfers between devices  4.87 us (13%)
  local copies, waits for them, and re-layouts  0.8 us (2%)
    ppermute x6, starting transfers between devices, send(): return lax.ppermute(value, ('row', 'col'), pairs)  17.2 us
    pallas_call x1, Pallas kernels, first(): pl.pallas_call(first_kernel, out_shape=(jax.ShapeDtypeStruct((MR * BLK, N...  6.52 us
    ppermute x6, waiting for transfers between devices, send(): return lax.ppermute(value, ('row', 'col'), pairs)  4.87 us
    pallas_call x1, Pallas kernels, last(): pl.pallas_call(last_kernel, out_shape=jax.ShapeDtypeStruct(out.shape, out...  3.35 us
    pallas_call x1, Pallas kernels, pack_left(): pl.pallas_call(pack_left_kernel, out_shape=(jax.ShapeDtypeStruct((LROWS +...  2.07 us
    pallas_call x1, Pallas kernels, pack_right(): pl.pallas_call(pack_right_kernel, out_shape=jax.ShapeDtypeStruct((BLK + M...  1.52 us
    unnamed x7, local copies, waits for them, and re-layouts  0.78 us
  transfers between devices with their start and end apart: 6, of which 1 were waited for; matrix products, arithmetic and copies ran while one was open for 0% of the time, Pallas kernels for 22%

profile of v2, /device:TPU:52, one launch (start us, length us, event | category | flops | bytes accessed | tf_op | source)
XLA Modules:
  0.0 36.4 jit_solution(16077584846764716814)
XLA Ops:
  0.0 0.0 copy-start
  0.0 0.0 copy-start.1
  0.0 0.7 %copy-done.1 = s32[32,4]{0,1:T(4,128)S(1)} copy-done((s32[32,4]{0,1:T(4,128)S(1)}, s32[32,4]{0,1:T(4,128)}, u32[]{:S(2)}) %copy-start.1) | copy-done | bytes 536
  0.7 0.0 copy-start.2
  0.7 2.1 %pack_left.1 = (bf16[2064,128]{1,0:T(8,128)(2,1)S(1)}, bf16[1024,128]{1,0:T(8,128)(2,1)S(1)}) custom-call(s32[4,32]{1,0:T(4,128)S(1)} %bitcast.1, bf16[4096,512]{1,0:T(8,128)(2,1)} %left.1), custom_call_target="tpu_custom_call" | custom-call | bytes 2097152 | tf_op jit(solution)/shard_map/pack_left/pallas_call | solution.py:72
  2.8 3.9 %collective-permute-start = (bf16[2064,128]{1,0:T(8,128)(2,1)S(1)}, bf16[2064,128]{1,0:T(8,128)(2,1)S(1)}, u32[]{:S(2)}, u32[]{:S(2)}) collective-permute-start(bf16[2064,128]{1,0:T(8,128)(2,1)S(1)} %get-tuple-element.10.after), channel_id=1, source_target_pairs={{0,0},{1,1},{2,2},{3,3},{4,4},{5,5},{6,6},{7,7},{8,8},{9,9},{10,10... | collective-permute-start | bytes 1585160 | tf_op jit(solution)/shard_map/ppermute | solution.py:373
  6.7 1.2 %collective-permute-start.4 = (bf16[1024,128]{1,0:T(8,128)(2,1)S(1)}, bf16[1024,128]{1,0:T(8,128)(2,1)S(1)}, u32[]{:S(2)}, u32[]{:S(2)}) collective-permute-start(bf16[1024,128]{1,0:T(8,128)(2,1)S(1)} %get-tuple-element.12), channel_id=1, source_target_pairs={{2,0},{3,1},{4,2},{5,3},{6,4},{7,5},{8,6},{9,7},{10,8},{11,9},{12,... | collective-permute-start | bytes 786440 | tf_op jit(solution)/shard_map/ppermute | solution.py:373
  7.9 0.0 copy-done
  7.9 1.5 %pack_right.1 = bf16[144,512]{1,0:T(8,128)(2,1)S(1)} custom-call(s32[8,8]{1,0:T(8,128)S(1)} %copy-done, bf16[1024,1024]{1,0:T(8,128)(2,1)} %right.1, bf16[2064,128]{1,0:T(8,128)(2,1)S(1)} %get-tuple-element.10.after), custom_call_target="tpu_custom_call" | custom-call | bytes 1048576 | tf_op jit(solution)/shard_map/pack_right/pallas_call | solution.py:122
  9.4 4.5 %collective-permute-start.2 = (bf16[144,512]{1,0:T(8,128)(2,1)S(1)}, bf16[144,512]{1,0:T(8,128)(2,1)S(1)}, u32[]{:S(2)}, u32[]{:S(2)}) collective-permute-start(bf16[144,512]{1,0:T(8,128)(2,1)S(1)} %pack_right.1), channel_id=1, source_target_pairs={{0,112},{1,113},{2,98},{3,99},{4,84},{5,85},{6,70},{7,71},{8,56},{... | collective-permute-start | bytes 442376 | tf_op jit(solution)/shard_map/ppermute | solution.py:373
  13.9 1.9 %collective-permute-start.1 = (bf16[144,512]{1,0:T(8,128)(2,1)S(1)}, bf16[144,512]{1,0:T(8,128)(2,1)S(1)}, u32[]{:S(2)}, u32[]{:S(2)}) collective-permute-start(bf16[144,512]{1,0:T(8,128)(2,1)S(1)} %pack_right.1), channel_id=1, source_target_pairs={{0,0},{1,1},{2,114},{3,115},{4,100},{5,101},{6,86},{7,87},{8,72},{... | collective-permute-start | bytes 442376 | tf_op jit(solution)/shard_map/ppermute | solution.py:373
  15.8 0.0 copy-done.2
  15.8 0.1 copy.7.keep
  15.9 0.0 collective-permute-done.4
  16.0 4.3 %collective-permute-start.5 = (bf16[1024,128]{1,0:T(8,128)(2,1)S(1)}, bf16[1024,128]{1,0:T(8,128)(2,1)S(1)}, u32[]{:S(2)}, u32[]{:S(2)}) collective-permute-start(bf16[1024,128]{1,0:T(8,128)(2,1)S(1)} %collective-permute-done.4), channel_id=1, source_target_pairs={{0,0},{1,1},{2,2},{3,3},{4,4},{5,5},{6,6},{7,7},{8,8},{9,9},{10,10... | collective-permute-start | bytes 786440 | tf_op jit(solution)/shard_map/ppermute | solution.py:373
  20.3 0.0 collective-permute-done.left
  20.3 1.4 %collective-permute-start.3 = (bf16[1040,128]{1,0:T(8,128)(2,1)S(1)}, bf16[1040,128]{1,0:T(8,128)(2,1)S(1)}, u32[]{:S(2)}, u32[]{:S(2)}) collective-permute-start(bf16[1040,128]{1,0:T(8,128)(2,1)S(1)} %slice.4), channel_id=1, source_target_pairs={{0,14},{1,15},{2,0},{3,1},{4,2},{5,3},{6,4},{7,5},{8,6},{9,7},{10,... | collective-permute-start | bytes 798728 | tf_op jit(solution)/shard_map/ppermute | solution.py:373
  21.7 0.0 collective-permute-done.2.r1
  21.7 4.8 %collective-permute-done.1.r0 = bf16[144,512]{1,0:T(8,128)(2,1)S(1)} collective-permute-done((bf16[144,512]{1,0:T(8,128)(2,1)S(1)}, bf16[144,512]{1,0:T(8,128)(2,1)S(1)}, u32[]{:S(2)}, u32[]{:S(2)}) %collective-permute-start.1) | collective-permute-done | bytes 147488 | tf_op jit(solution)/shard_map/ppermute | solution.py:373
  26.5 6.5 %first.1 = (bf16[4096,1024]{1,0:T(8,128)(2,1)}, f32[2048,512]{1,0:T(8,128)S(1)}, s32[384]{0:T(512)S(1)}) custom-call(s32[32,8]{1,0:T(8,128)S(1)} %copy.7.keep, bf16[2064,128]{1,0:T(8,128)(2,1)S(1)} %collective-permute-done.left, bf16[144,512]{1,0:T(8,128)(2,1)S(1)} %collective-permute-done.1.r0, bf16[144,512]{1,0:T(8,128)(2,1)S(1)} %collective-permute-done.2.r1), custom_call_target="tpu_custom_call" | custom-call | flops 10000000000 | bytes 14680064 | tf_op jit(solution)/shard_map/first/pallas_call | solution.py:266
  33.0 0.0 collective-permute-done.5.more
  33.0 0.0 collective-permute-done.3.left
  33.0 3.4 %last.1 = bf16[4096,1024]{1,0:T(8,128)(2,1)} custom-call(s32[384]{0:T(512)S(1)} %get-tuple-element.11.table, bf16[1040,128]{1,0:T(8,128)(2,1)S(1)} %collective-permute-done.3.left, bf16[1024,128]{1,0:T(8,128)(2,1)S(1)} %collective-permute-done.5.more, bf16[144,512]{1,0:T(8,128)(2,1)S(1)} %collective-permute-done.1.r0, ...), custom_call_target="tpu_custom_call", output_to_operand_aliasing={{}: (6, {})} | custom-call | flops 268435456 | bytes 4194304 | tf_op jit(solution)/shard_map/last/pallas_call | solution.py:329
  (1 shorter events, 0.0 us)
Async XLA Ops:
  0.0 7.9 %copy-start = (s32[8,8]{1,0:T(8,128)S(1)}, s32[8,8]{1,0:T(8,128)}, u32[]{:S(2)}) copy-start(s32[8,8]{1,0:T(8,128)} %pattern.1) | copy-start | bytes 772
  0.0 0.7 %copy-start.1 = (s32[32,4]{0,1:T(4,128)S(1)}, s32[32,4]{0,1:T(4,128)}, u32[]{:S(2)}) copy-start(s32[32,4]{0,1:T(4,128)} %param.6) | copy-start | bytes 1540
  0.7 15.1 %copy-start.2 = (s32[32,8]{0,1:T(8,128)S(1)}, s32[32,8]{0,1:T(8,128)}, u32[]{:S(2)}) copy-start(s32[32,8]{0,1:T(8,128)} %param.9) | copy-start | bytes 3076
  2.8 17.5 %collective-permute-start = (bf16[2064,128]{1,0:T(8,128)(2,1)S(1)}, bf16[2064,128]{1,0:T(8,128)(2,1)S(1)}, u32[]{:S(2)}, u32[]{:S(2)}) collective-permute-start(bf16[2064,128]{1,0:T(8,128)(2,1)S(1)} %get-tuple-element.10.after), channel_id=1, source_target_pairs={{0,0},{1,1},{2,2},{3,3},{4,4},{5,5},{6,6},{7,7},{8,8},{9,9},{10,10... | collective-permute-start | bytes 1585160 | tf_op jit(solution)/shard_map/ppermute | solution.py:373
  6.7 9.3 %collective-permute-start.4 = (bf16[1024,128]{1,0:T(8,128)(2,1)S(1)}, bf16[1024,128]{1,0:T(8,128)(2,1)S(1)}, u32[]{:S(2)}, u32[]{:S(2)}) collective-permute-start(bf16[1024,128]{1,0:T(8,128)(2,1)S(1)} %get-tuple-element.12), channel_id=1, source_target_pairs={{2,0},{3,1},{4,2},{5,3},{6,4},{7,5},{8,6},{9,7},{10,8},{11,9},{12,... | collective-permute-start | bytes 786440 | tf_op jit(solution)/shard_map/ppermute | solution.py:373
  9.4 12.3 %collective-permute-start.2 = (bf16[144,512]{1,0:T(8,128)(2,1)S(1)}, bf16[144,512]{1,0:T(8,128)(2,1)S(1)}, u32[]{:S(2)}, u32[]{:S(2)}) collective-permute-start(bf16[144,512]{1,0:T(8,128)(2,1)S(1)} %pack_right.1), channel_id=1, source_target_pairs={{0,112},{1,113},{2,98},{3,99},{4,84},{5,85},{6,70},{7,71},{8,56},{... | collective-permute-start | bytes 442376 | tf_op jit(solution)/shard_map/ppermute | solution.py:373
  13.9 12.6 %collective-permute-start.1 = (bf16[144,512]{1,0:T(8,128)(2,1)S(1)}, bf16[144,512]{1,0:T(8,128)(2,1)S(1)}, u32[]{:S(2)}, u32[]{:S(2)}) collective-permute-start(bf16[144,512]{1,0:T(8,128)(2,1)S(1)} %pack_right.1), channel_id=1, source_target_pairs={{0,0},{1,1},{2,114},{3,115},{4,100},{5,101},{6,86},{7,87},{8,72},{... | collective-permute-start | bytes 442376 | tf_op jit(solution)/shard_map/ppermute | solution.py:373
  16.0 17.1 %collective-permute-start.5 = (bf16[1024,128]{1,0:T(8,128)(2,1)S(1)}, bf16[1024,128]{1,0:T(8,128)(2,1)S(1)}, u32[]{:S(2)}, u32[]{:S(2)}) collective-permute-start(bf16[1024,128]{1,0:T(8,128)(2,1)S(1)} %collective-permute-done.4), channel_id=1, source_target_pairs={{0,0},{1,1},{2,2},{3,3},{4,4},{5,5},{6,6},{7,7},{8,8},{9,9},{10,10... | collective-permute-start | bytes 786440 | tf_op jit(solution)/shard_map/ppermute | solution.py:373
  20.3 12.7 %collective-permute-start.3 = (bf16[1040,128]{1,0:T(8,128)(2,1)S(1)}, bf16[1040,128]{1,0:T(8,128)(2,1)S(1)}, u32[]{:S(2)}, u32[]{:S(2)}) collective-permute-start(bf16[1040,128]{1,0:T(8,128)(2,1)S(1)} %slice.4), channel_id=1, source_target_pairs={{0,14},{1,15},{2,0},{3,1},{4,2},{5,3},{6,4},{7,5},{8,6},{9,7},{10,... | collective-permute-start | bytes 798728 | tf_op jit(solution)/shard_map/ppermute | solution.py:373

commit v3 on v2

--- a/solution.py
+++ b/solution.py
@@ -18,7 +18,6 @@
 HALF = LROWS // 2
 PAIRS = LCAP * RCAP
 TILES = MR * NC
-ZROWS = 256
 
 
 def block_of(ref, block_row, block_col):
@@ -32,107 +31,130 @@
     return pl.BlockSpec(memory_space=space)
 
 
-def pack_left_kernel(pattern, left, out, more, pos, meta, sems):
+def pack_kernel(lpat, rpat, left, right, lout, rout, lpos, rpos, lmeta, rmeta, sems, rsems):
+    part = lax.rem(lax.axis_index("col"), 2)
     count = 0
     starts = []
     for k in range(KS):
         starts.append(count)
         for i in range(MR):
-            pos[count] = k * MR + i
-            count = count + pattern[k, i]
+            lpos[count] = k * MR + i
+            count = count + lpat[k, i]
     starts.append(count)
     copies = []
     for a in range(LCAP):
-        at = pos[a]
-        block = block_of(left, at & (MR - 1), at >> 5)
+        at = lpos[a]
         first_row = a * BLK if a * BLK < HALF else a * BLK + META
-        copies.append(pltpu.make_async_copy(block, out.at[pl.ds(first_row, BLK), :], sems.at[a]))
+        copies.append(
+            pltpu.make_async_copy(
+                block_of(left, at & (MR - 1), at >> 5), lout.at[pl.ds(first_row, BLK), :], sems.at[a]
+            )
+        )
         copies[-1].start()
-        if a * BLK >= HALF:
-            copies.append(
-                pltpu.make_async_copy(
-                    block, more.at[pl.ds(a * BLK - HALF, BLK), :], sems.at[LCAP + a - LCAP // 2]
-                )
+    count = 0
+    for k in range(KS):
+        for j in range(NC):
+            rpos[count] = k * NC + j
+            count = count + rpat[part * KS + k, j]
+    for b in range(RCAP):
+        at = rpos[b]
+        copies.append(
+            pltpu.make_async_copy(
+                block_of(right, part * KS + (at >> 3), at & (NC - 1)),
+                rout.at[pl.ds(0, BLK), pl.ds(b * BLK, BLK)],
+                rsems.at[b],
             )
-            copies[-1].start()
+        )
+        copies[-1].start()
     lane = lax.broadcasted_iota(jnp.int32, (META, BLK), 1)
     row = jnp.zeros((META, BLK), jnp.int32)
     for a in range(LCAP):
-        row = jnp.where(lane == a, pos[a], row)
+        row = jnp.where(lane == a, lpos[a], row)
     for k in range(KS + 1):
         row = jnp.where(lane == LCAP + k, starts[k], row)
-    meta[...] = row.astype(jnp.float32).astype(jnp.bfloat16)
-    copies.append(pltpu.make_async_copy(meta, out.at[pl.ds(HALF, META), :], sems.at[LCAP + LCAP // 2]))
+    lmeta[...] = row.astype(jnp.float32).astype(jnp.bfloat16)
+    copies.append(pltpu.make_async_copy(lmeta, lout.at[pl.ds(HALF, META), :], sems.at[LCAP]))
+    copies[-1].start()
+    lane = lax.broadcasted_iota(jnp.int32, (META, RCAP * BLK), 1)
+    row = jnp.zeros((META, RCAP * BLK), jnp.int32)
+    for b in range(RCAP):
+        row = jnp.where(lane == b, rpos[b], row)
+    rmeta[...] = row.astype(jnp.float32).astype(jnp.bfloat16)
+    copies.append(pltpu.make_async_copy(rmeta, rout.at[pl.ds(BLK, META), :], rsems.at[RCAP]))
     copies[-1].start()
     for copy in copies:
         copy.wait()
 
 
-def pack_left(pattern, left):
+def pack(left_pattern, right_pattern, left, right):
     return pl.pallas_call(
-        pack_left_kernel,
+        pack_kernel,
         out_shape=(
             jax.ShapeDtypeStruct((LROWS + META, BLK), jnp.bfloat16),
-            jax.ShapeDtypeStruct((HALF, BLK), jnp.bfloat16),
+            jax.ShapeDtypeStruct((BLK + META, RCAP * BLK), jnp.bfloat16),
         ),
-        in_specs=[spec(pltpu.SMEM), spec(pltpu.HBM)],
+        in_specs=[spec(pltpu.SMEM), spec(pltpu.SMEM), spec(pltpu.HBM), spec(pltpu.HBM)],
         out_specs=[spec(pl.ANY)] * 2,
         scratch_shapes=[
             pltpu.SMEM((LCAP + 1,), jnp.int32),
+            pltpu.SMEM((RCAP + 1,), jnp.int32),
             pltpu.VMEM((META, BLK), jnp.bfloat16),
-            pltpu.SemaphoreType.DMA((LCAP + LCAP // 2 + 1,)),
+            pltpu.VMEM((META, RCAP * BLK), jnp.bfloat16),
+            pltpu.SemaphoreType.DMA((LCAP + 1,)),
+            pltpu.SemaphoreType.DMA((RCAP + 1,)),
         ],
         compiler_params=pltpu.CompilerParams(vmem_limit_bytes=52 << 20),
         cost_estimate=pl.CostEstimate(flops=0, bytes_accessed=2 << 20, transcendentals=0),
-        name="pack_left",
-    )(pattern.T, left)
-
-
-def pack_right_kernel(pattern, right, after, out, pos, meta, sems):
+        name="pack",
+    )(left_pattern.T, right_pattern, left, right)
+
+
+def second_half_kernel(whole, after, half):
     del after
-    part = lax.rem(lax.axis_index("col"), 2)
-    count = 0
-    for k in range(KS):
-        for j in range(NC):
-            pos[count] = k * NC + j
-            count = count + pattern[part * KS + k, j]
-    copies = []
-    for b in range(RCAP):
-        at = pos[b]
-        copies.append(
-            pltpu.make_async_copy(
-                block_of(right, part * KS + (at >> 3), at & (NC - 1)),
-                out.at[pl.ds(0, BLK), pl.ds(b * BLK, BLK)],
-                sems.at[b],
-            )
-        )
-        copies[-1].start()
-    lane = lax.broadcasted_iota(jnp.int32, (META, RCAP * BLK), 1)
-    row = jnp.zeros((META, RCAP * BLK), jnp.int32)
-    for b in range(RCAP):
-        row = jnp.where(lane == b, pos[b], row)
-    meta[...] = row.astype(jnp.float32).astype(jnp.bfloat16)
-    copies.append(pltpu.make_async_copy(meta, out.at[pl.ds(BLK, META), :], sems.at[RCAP]))
-    copies[-1].start()
+    half[...] = whole[pl.ds(HALF + META, HALF), :]
+
+
+def second_half(whole, after):
+    return pl.pallas_call(
+        second_half_kernel,
+        out_shape=jax.ShapeDtypeStruct((HALF, BLK), jnp.bfloat16),
+        in_specs=[spec(pltpu.VMEM), spec(pl.ANY)],
+        out_specs=spec(pltpu.VMEM),
+        cost_estimate=pl.CostEstimate(flops=0, bytes_accessed=1 << 19, transcendentals=0),
+        name="second_half",
+    )(whole, after)
+
+
+def blank_kernel(after, out, zero, sems):
+    del after
+    zero[...] = jnp.zeros_like(zero)
+    rows = zero.shape[0]
+    copies = [
+        pltpu.make_async_copy(zero, out.at[pl.ds(n * rows, rows), :], sems.at[n])
+        for n in range(out.shape[0] // rows)
+    ]
+    for copy in copies:
+        copy.start()
     for copy in copies:
         copy.wait()
 
 
-def pack_right(pattern, right, after):
+def blank(after, shape):
+    rows = 256
     return pl.pallas_call(
-        pack_right_kernel,
-        out_shape=jax.ShapeDtypeStruct((BLK + META, RCAP * BLK), jnp.bfloat16),
-        in_specs=[spec(pltpu.SMEM), spec(pltpu.HBM), spec(pl.ANY)],
-        out_specs=spec(pl.ANY),
+        blank_kernel,
+        out_shape=jax.ShapeDtypeStruct(shape, jnp.bfloat16),
+        in_specs=[spec(pl.ANY)],
+        out_specs=spec(pltpu.HBM),
         scratch_shapes=[
-            pltpu.SMEM((RCAP + 1,), jnp.int32),
-            pltpu.VMEM((META, RCAP * BLK), jnp.bfloat16),
-            pltpu.SemaphoreType.DMA((RCAP + 1,)),
+            pltpu.VMEM((rows, shape[1]), jnp.bfloat16),
+            pltpu.SemaphoreType.DMA((shape[0] // rows,)),
         ],
-        compiler_params=pltpu.CompilerParams(vmem_limit_bytes=52 << 20),
-        cost_estimate=pl.CostEstimate(flops=0, bytes_accessed=1 << 20, transcendentals=0),
-        name="pack_right",
-    )(pattern, right, after)
+        cost_estimate=pl.CostEstimate(
+            flops=0, bytes_accessed=2 * shape[0] * shape[1], transcendentals=0
+        ),
+        name="blank",
+    )(after)
 
 
 def piece(code):
@@ -161,7 +183,7 @@
         def meet(a, total, b=b, j=j):
             target = (left_at(a) & (MR - 1)) * NC + j
             code = a * RCAP + b
-            wanted = kept(target)
+            wanted = kept[target] >= 0
             held = owner[target]
             fresh = jnp.logical_and(wanted, held == 0)
 
@@ -170,7 +192,7 @@
                 owner[target] = code + 1
                 slot_of[total] = code * TILES + target
 
-            @pl.when(jnp.logical_and(wanted, held != 0))
+            @pl.when(jnp.logical_and(wanted, held > 0))
             def _():
                 rows, cols = piece(held - 1)
                 more_rows, more_cols = piece(code)
@@ -215,16 +237,10 @@
 
 
 def first_kernel(
-    keep, left, r0, r1, out, prod, table,
-    zero, zero_sems, right, stage, meta_v, meta, owner, slot_of, meta_sem, out_sems,
+    keep, left, r0, r1, zero, out, prod, table,
+    right, stage, meta_v, meta, slot_of, meta_sem, out_sems,
 ):
-    zero[...] = jnp.zeros_like(zero)
-    clears = [
-        pltpu.make_async_copy(zero, out.at[pl.ds(n * ZROWS, ZROWS), :], zero_sems.at[n])
-        for n in range(out.shape[0] // ZROWS)
-    ]
-    for copy in clears:
-        copy.start()
+    del zero
     odd = lax.rem(lax.axis_index("row"), 2)
     line = lax.broadcasted_iota(jnp.int32, (META, BLK), 0)
     rows = left[pl.ds(HALF, META), :].astype(jnp.float32)
@@ -235,15 +251,15 @@
     meta_copy = pltpu.make_async_copy(meta_v, meta, meta_sem)
     meta_copy.start()
     for at in range(TILES):
-        owner[at] = 0
+        table[at] = jnp.minimum(keep[at // NC, at % NC], 1) - 1
     choose(odd, r0, r1, right)
     products(((left, 0), (left, HALF + META)), right, prod)
     meta_copy.wait()
     total = gather(
         lambda a: meta[0, a],
         lambda b: meta[1 + odd, b],
-        lambda target: keep[target >> 3, target & (NC - 1)] != 0,
-        owner,
+        table,
+        table,
         prod,
         slot_of,
     )
@@ -252,44 +268,37 @@
         rows, cols = piece(code)
         return prod[rows, cols]
 
-    for copy in clears:
-        copy.wait()
     write(total, value, slot_of, stage, out, out_sems)
-    for i in range(MR):
-        for j in range(NC):
-            table[i * NC + j] = jnp.where(keep[i, j] != 0, owner[i * NC + j], -1)
     for b in range(RCAP):
         table[TILES + b] = meta[2 - odd, b]
 
 
-def first(keep, left, r0, r1):
+def first(keep, left, r0, r1, zero):
     return pl.pallas_call(
         first_kernel,
         out_shape=(
-            jax.ShapeDtypeStruct((MR * BLK, NC * BLK), jnp.bfloat16),
+            jax.ShapeDtypeStruct(zero.shape, zero.dtype),
             jax.ShapeDtypeStruct((LROWS, RCAP * BLK), jnp.float32),
             jax.ShapeDtypeStruct((TILES + BLK,), jnp.int32),
         ),
-        in_specs=[spec(pltpu.SMEM)] + [spec(pltpu.VMEM)] * 3,
+        in_specs=[spec(pltpu.SMEM)] + [spec(pltpu.VMEM)] * 3 + [spec(pltpu.HBM)],
         out_specs=[spec(pltpu.HBM), spec(pltpu.VMEM), spec(pltpu.SMEM)],
         scratch_shapes=[
-            pltpu.VMEM((ZROWS, NC * BLK), jnp.bfloat16),
-            pltpu.SemaphoreType.DMA((MR * BLK // ZROWS,)),
             pltpu.VMEM((BLK, RCAP * BLK), jnp.bfloat16),
             pltpu.VMEM((PAIRS, BLK, BLK), jnp.bfloat16),
             pltpu.VMEM((META, BLK), jnp.int32),
             pltpu.SMEM((META, BLK), jnp.int32),
-            pltpu.SMEM((TILES,), jnp.int32),
             pltpu.SMEM((PAIRS,), jnp.int32),
             pltpu.SemaphoreType.DMA,
             pltpu.SemaphoreType.DMA((PAIRS,)),
         ],
+        input_output_aliases={4: 0},
         compiler_params=pltpu.CompilerParams(vmem_limit_bytes=32 << 20),
         cost_estimate=pl.CostEstimate(
             flops=10**10, bytes_accessed=14 << 20, transcendentals=0
         ),
         name="first",
-    )(keep, left, r0, r1)
+    )(keep, left, r0, r1, zero)
 
 
 def last_kernel(
@@ -309,7 +318,7 @@
     total = gather(
         lambda a: meta[0, a],
         lambda b: table[TILES + b],
-        lambda target: table[target] >= 0,
+        table,
         owner,
         prod,
         slot_of,
@@ -381,19 +390,20 @@
             pairs.append(((r, c), (to_r % rows_n, to_c % cols_n)))
         return send(value, pairs)
 
-    whole, half = pack_left(left_pattern, left_matrix)
+    whole, rpack = pack(left_pattern, right_pattern, left_matrix, right_matrix)
     even = moved(whole, lambda r, c: (r, c - group * (r + r % 2)))
-    roads = {at: detour(*at, cols_n, group) for at in devices}
-    between = send(half, [((r, roads[r, c][0]), (r, roads[r, c][1])) for r, c in devices])
-    rpack = pack_right(right_pattern, right_matrix, whole)
     r0 = moved(rpack, lambda r, c: (r - c // group, c))
     r1 = moved(rpack, lambda r, c: (r - c // group - 1, c))
+    roads = {at: detour(*at, cols_n, group) for at in devices}
+    half = second_half(whole, rpack)
+    between = send(half, [((r, roads[r, c][0]), (r, roads[r, c][1])) for r, c in devices])
+    zero = blank(half, (left_matrix.shape[0], right_matrix.shape[1]))
     passed = moved(
         lax.slice_in_dim(even, 0, HALF + META),
         lambda r, c: (r, c + group * (2 * (r % 2) - 1)),
     )
     more = send(between, [((r, roads[r, c][1]), (r, c)) for r, c in devices])
-    out, before, table = first(keep_mask, even, r0, r1)
+    out, before, table = first(keep_mask, even, r0, r1, zero)
     return last(table, passed, more, r0, r1, before, out)
 
 

time: 36.8 us -> 41.2 us (1.12)
  the two profiles are of different devices: /device:TPU:52 before, /device:TPU:24 now
where the time goes in v3:
time: 41.2 us; the launch traced here: 40.7 us
  starting transfers between devices  18.8 us (46%)
  Pallas kernels  14.9 us (36%)
  waiting for transfers between devices  4.77 us (12%)
  local copies, waits for them, and re-layouts  2.13 us (5%)
    ppermute x6, starting transfers between devices, send(): return lax.ppermute(value, ('row', 'col'), pairs)  18.8 us
    ppermute x6, waiting for transfers between devices, send(): return lax.ppermute(value, ('row', 'col'), pairs)  4.77 us
    pallas_call x1, Pallas kernels, first(): pl.pallas_call(first_kernel, out_shape=(jax.ShapeDtypeStruct(zero.shape,...  4.32 us
    pallas_call x1, Pallas kernels, blank(): pl.pallas_call(blank_kernel, out_shape=jax.ShapeDtypeStruct(shape, jnp.bf...  3.45 us
    pallas_call x1, Pallas kernels, last(): pl.pallas_call(last_kernel, out_shape=jax.ShapeDtypeStruct(out.shape, out...  3.24 us
    unnamed x11, local copies, waits for them, and re-layouts  2.11 us
    pallas_call x1, Pallas kernels, pack(): pl.pallas_call(pack_kernel, out_shape=(jax.ShapeDtypeStruct((LROWS + META...  2.08 us
    pallas_call x1, Pallas kernels, second_half(): pl.pallas_call(second_half_kernel, out_shape=jax.ShapeDtypeStruct((HALF,...  1.77 us
  transfers between devices with their start and end apart: 6, of which 2 were waited for; matrix products, arithmetic and copies ran while one was open for 0% of the time, Pallas kernels for 23%

profile of v3, /device:TPU:24, one launch (start us, length us, event | category | flops | bytes accessed | tf_op | source)
XLA Modules:
  0.0 40.7 jit_solution(14938486813501775322)
XLA Ops:
  0.0 0.0 copy-start.2
  0.0 0.7 %copy-done.2 = s32[8,8]{1,0:T(8,128)S(1)} copy-done((s32[8,8]{1,0:T(8,128)S(1)}, s32[8,8]{1,0:T(8,128)}, u32[]{:S(2)}) %copy-start.2) | copy-done | bytes 280
  0.7 0.0 copy-start.3
  0.7 0.7 %copy-done.3 = s32[32,4]{0,1:T(4,128)S(1)} copy-done((s32[32,4]{0,1:T(4,128)S(1)}, s32[32,4]{0,1:T(4,128)}, u32[]{:S(2)}) %copy-start.3) | copy-done | bytes 536
  1.4 0.0 copy-start.4
  1.4 2.1 %pack.1 = (bf16[2064,128]{1,0:T(8,128)(2,1)S(1)}, bf16[144,512]{1,0:T(8,128)(2,1)S(1)}) custom-call(s32[4,32]{1,0:T(4,128)S(1)} %bitcast.1, s32[8,8]{1,0:T(8,128)S(1)} %copy-done.2, bf16[4096,512]{1,0:T(8,128)(2,1)} %left.1, bf16[1024,1024]{1,0:T(8,128)(2,1)} %right.1), custom_call_target="tpu_custom_call" | custom-call | bytes 2097152 | tf_op jit(solution)/shard_map/pack/pallas_call | solution.py:90
  3.5 0.0 copy-start.1
  3.5 0.7 %copy-done.1 = bf16[144,512]{1,0:T(8,128)(2,1)} copy-done((bf16[144,512]{1,0:T(8,128)(2,1)}, bf16[144,512]{1,0:T(8,128)(2,1)S(1)}, u32[]{:S(2)}) %copy-start.1) | copy-done | bytes 147480
  4.1 0.0 copy-start
  4.1 5.8 %collective-permute-start = (bf16[2064,128]{1,0:T(8,128)(2,1)S(1)}, bf16[2064,128]{1,0:T(8,128)(2,1)S(1)}, u32[]{:S(2)}, u32[]{:S(2)}) collective-permute-start(bf16[2064,128]{1,0:T(8,128)(2,1)S(1)} %get-tuple-element.10.whole), channel_id=1, source_target_pairs={{0,0},{1,1},{2,2},{3,3},{4,4},{5,5},{6,6},{7,7},{8,8},{9,9},{10,10... | collective-permute-start | bytes 1585160 | tf_op jit(solution)/shard_map/ppermute | solution.py:382
  9.9 0.0 copy-done
  9.9 1.8 %second_half.1.after = bf16[1024,128]{1,0:T(8,128)(2,1)} custom-call(bf16[2064,128]{1,0:T(8,128)(2,1)} %copy-done, bf16[144,512]{1,0:T(8,128)(2,1)} %copy-done.1), custom_call_target="tpu_custom_call" | custom-call | bytes 524288 | tf_op jit(solution)/shard_map/second_half/pallas_call | solution.py:118
  11.7 1.5 %collective-permute-start.4 = (bf16[1024,128]{1,0:T(8,128)(2,1)}, bf16[1024,128]{1,0:T(8,128)(2,1)S(1)}, u32[]{:S(2)}, u32[]{:S(2)}) collective-permute-start(bf16[1024,128]{1,0:T(8,128)(2,1)} %second_half.1.after), channel_id=1, source_target_pairs={{2,0},{3,1},{4,2},{5,3},{6,4},{7,5},{8,6},{9,7},{10,8},{11,9},{12,... | collective-permute-start | bytes 786440 | tf_op jit(solution)/shard_map/ppermute | solution.py:382
  13.2 1.6 %collective-permute-start.1 = (bf16[144,512]{1,0:T(8,128)(2,1)}, bf16[144,512]{1,0:T(8,128)(2,1)S(1)}, u32[]{:S(2)}, u32[]{:S(2)}) collective-permute-start(bf16[144,512]{1,0:T(8,128)(2,1)} %copy-done.1), channel_id=1, source_target_pairs={{0,0},{1,1},{2,114},{3,115},{4,100},{5,101},{6,86},{7,87},{8,72},{... | collective-permute-start | bytes 442376 | tf_op jit(solution)/shard_map/ppermute | solution.py:382
  14.7 1.9 %collective-permute-start.2 = (bf16[144,512]{1,0:T(8,128)(2,1)}, bf16[144,512]{1,0:T(8,128)(2,1)S(1)}, u32[]{:S(2)}, u32[]{:S(2)}) collective-permute-start(bf16[144,512]{1,0:T(8,128)(2,1)} %copy-done.1), channel_id=1, source_target_pairs={{0,112},{1,113},{2,98},{3,99},{4,84},{5,85},{6,70},{7,71},{8,56},{... | collective-permute-start | bytes 442376 | tf_op jit(solution)/shard_map/ppermute | solution.py:382
  16.7 3.5 %blank.1.zero = bf16[4096,1024]{1,0:T(8,128)(2,1)} custom-call(bf16[1024,128]{1,0:T(8,128)(2,1)} %second_half.1.after), custom_call_target="tpu_custom_call" | custom-call | bytes 8388608 | tf_op jit(solution)/shard_map/blank/pallas_call | solution.py:144
  20.1 0.0 copy-done.4
  20.1 0.1 copy.8.keep
  20.2 0.0 collective-permute-done.4
  20.2 8.0 %collective-permute-start.5 = (bf16[1024,128]{1,0:T(8,128)(2,1)S(1)}, bf16[1024,128]{1,0:T(8,128)(2,1)S(1)}, u32[]{:S(2)}, u32[]{:S(2)}) collective-permute-start(bf16[1024,128]{1,0:T(8,128)(2,1)S(1)} %collective-permute-done.4), channel_id=1, source_target_pairs={{0,0},{1,1},{2,2},{3,3},{4,4},{5,5},{6,6},{7,7},{8,8},{9,9},{10,10... | collective-permute-start | bytes 786440 | tf_op jit(solution)/shard_map/ppermute | solution.py:382
  28.2 0.0 collective-permute-done.left
  28.2 0.1 collective-permute-start.3
  28.3 0.0 collective-permute-done.1.r0
  28.3 0.0 collective-permute-done.2.r1
  28.4 4.3 %first.1 = (bf16[4096,1024]{1,0:T(8,128)(2,1)}, f32[2048,512]{1,0:T(8,128)S(1)}, s32[384]{0:T(512)S(1)}) custom-call(s32[32,8]{1,0:T(8,128)S(1)} %copy.8.keep, bf16[2064,128]{1,0:T(8,128)(2,1)S(1)} %collective-permute-done.left, bf16[144,512]{1,0:T(8,128)(2,1)S(1)} %collective-permute-done.1.r0, ...), custom_call_target="tpu_custom_call", output_to_operand_aliasing={{0}: (4, {})} | custom-call | flops 10000000000 | bytes 14680064 | tf_op jit(solution)/shard_map/first/pallas_call | solution.py:277
  32.7 0.5 %collective-permute-done.5.more = bf16[1024,128]{1,0:T(8,128)(2,1)S(1)} collective-permute-done((bf16[1024,128]{1,0:T(8,128)(2,1)S(1)}, bf16[1024,128]{1,0:T(8,128)(2,1)S(1)}, u32[]{:S(2)}, u32[]{:S(2)}) %collective-permute-start.5) | collective-permute-done | bytes 262176 | tf_op jit(solution)/shard_map/ppermute | solution.py:382
  33.2 4.3 %collective-permute-done.3.left = bf16[1040,128]{1,0:T(8,128)(2,1)S(1)} collective-permute-done((bf16[1040,128]{1,0:T(8,128)(2,1)S(1)}, bf16[1040,128]{1,0:T(8,128)(2,1)S(1)}, u32[]{:S(2)}, u32[]{:S(2)}) %collective-permute-start.3) | collective-permute-done | bytes 266272 | tf_op jit(solution)/shard_map/ppermute | solution.py:382
  37.4 3.2 %last.1 = bf16[4096,1024]{1,0:T(8,128)(2,1)} custom-call(s32[384]{0:T(512)S(1)} %get-tuple-element.12.table, bf16[1040,128]{1,0:T(8,128)(2,1)S(1)} %collective-permute-done.3.left, bf16[1024,128]{1,0:T(8,128)(2,1)S(1)} %collective-permute-done.5.more, bf16[144,512]{1,0:T(8,128)(2,1)S(1)} %collective-permute-done.1.r0, ...), custom_call_target="tpu_custom_call", output_to_operand_aliasing={{}: (6, {})} | custom-call | flops 268435456 | bytes 4194304 | tf_op jit(solution)/shard_map/last/pallas_call | solution.py:338
  (1 shorter events, 0.0 us)
Async XLA Ops:
  0.0 0.7 %copy-start.2 = (s32[8,8]{1,0:T(8,128)S(1)}, s32[8,8]{1,0:T(8,128)}, u32[]{:S(2)}) copy-start(s32[8,8]{1,0:T(8,128)} %rpat.1) | copy-start | bytes 772
  0.7 0.7 %copy-start.3 = (s32[32,4]{0,1:T(4,128)S(1)}, s32[32,4]{0,1:T(4,128)}, u32[]{:S(2)}) copy-start(s32[32,4]{0,1:T(4,128)} %param.6) | copy-start | bytes 1540
  1.4 18.7 %copy-start.4 = (s32[32,8]{0,1:T(8,128)S(1)}, s32[32,8]{0,1:T(8,128)}, u32[]{:S(2)}) copy-start(s32[32,8]{0,1:T(8,128)} %param.9) | copy-start | bytes 3076
  3.5 0.7 %copy-start.1 = (bf16[144,512]{1,0:T(8,128)(2,1)}, bf16[144,512]{1,0:T(8,128)(2,1)S(1)}, u32[]{:S(2)}) copy-start(bf16[144,512]{1,0:T(8,128)(2,1)S(1)} %get-tuple-element.11.after) | copy-start | bytes 442372
  4.1 5.8 %copy-start = (bf16[2064,128]{1,0:T(8,128)(2,1)}, bf16[2064,128]{1,0:T(8,128)(2,1)S(1)}, u32[]{:S(2)}) copy-start(bf16[2064,128]{1,0:T(8,128)(2,1)S(1)} %get-tuple-element.10.whole) | copy-start | bytes 1585156
  4.1 24.1 %collective-permute-start = (bf16[2064,128]{1,0:T(8,128)(2,1)S(1)}, bf16[2064,128]{1,0:T(8,128)(2,1)S(1)}, u32[]{:S(2)}, u32[]{:S(2)}) collective-permute-start(bf16[2064,128]{1,0:T(8,128)(2,1)S(1)} %get-tuple-element.10.whole), channel_id=1, source_target_pairs={{0,0},{1,1},{2,2},{3,3},{4,4},{5,5},{6,6},{7,7},{8,8},{9,9},{10,10... | collective-permute-start | bytes 1585160 | tf_op jit(solution)/shard_map/ppermute | solution.py:382
  11.7 8.5 %collective-permute-start.4 = (bf16[1024,128]{1,0:T(8,128)(2,1)}, bf16[1024,128]{1,0:T(8,128)(2,1)S(1)}, u32[]{:S(2)}, u32[]{:S(2)}) collective-permute-start(bf16[1024,128]{1,0:T(8,128)(2,1)} %second_half.1.after), channel_id=1, source_target_pairs={{2,0},{3,1},{4,2},{5,3},{6,4},{7,5},{8,6},{9,7},{10,8},{11,9},{12,... | collective-permute-start | bytes 786440 | tf_op jit(solution)/shard_map/ppermute | solution.py:382
  13.2 15.2 %collective-permute-start.1 = (bf16[144,512]{1,0:T(8,128)(2,1)}, bf16[144,512]{1,0:T(8,128)(2,1)S(1)}, u32[]{:S(2)}, u32[]{:S(2)}) collective-permute-start(bf16[144,512]{1,0:T(8,128)(2,1)} %copy-done.1), channel_id=1, source_target_pairs={{0,0},{1,1},{2,114},{3,115},{4,100},{5,101},{6,86},{7,87},{8,72},{... | collective-permute-start | bytes 442376 | tf_op jit(solution)/shard_map/ppermute | solution.py:382
  14.7 13.6 %collective-permute-start.2 = (bf16[144,512]{1,0:T(8,128)(2,1)}, bf16[144,512]{1,0:T(8,128)(2,1)S(1)}, u32[]{:S(2)}, u32[]{:S(2)}) collective-permute-start(bf16[144,512]{1,0:T(8,128)(2,1)} %copy-done.1), channel_id=1, source_target_pairs={{0,112},{1,113},{2,98},{3,99},{4,84},{5,85},{6,70},{7,71},{8,56},{... | collective-permute-start | bytes 442376 | tf_op jit(solution)/shard_map/ppermute | solution.py:382
  20.2 13.0 %collective-permute-start.5 = (bf16[1024,128]{1,0:T(8,128)(2,1)S(1)}, bf16[1024,128]{1,0:T(8,128)(2,1)S(1)}, u32[]{:S(2)}, u32[]{:S(2)}) collective-permute-start(bf16[1024,128]{1,0:T(8,128)(2,1)S(1)} %collective-permute-done.4), channel_id=1, source_target_pairs={{0,0},{1,1},{2,2},{3,3},{4,4},{5,5},{6,6},{7,7},{8,8},{9,9},{10,10... | collective-permute-start | bytes 786440 | tf_op jit(solution)/shard_map/ppermute | solution.py:382
  28.2 9.2 %collective-permute-start.3 = (bf16[1040,128]{1,0:T(8,128)(2,1)S(1)}, bf16[1040,128]{1,0:T(8,128)(2,1)S(1)}, u32[]{:S(2)}, u32[]{:S(2)}) collective-permute-start(bf16[1040,128]{1,0:T(8,128)(2,1)S(1)} %slice.4), channel_id=1, source_target_pairs={{0,14},{1,15},{2,0},{3,1},{4,2},{5,3},{6,4},{7,5},{8,6},{9,7},{10,... | collective-permute-start | bytes 798728 | tf_op jit(solution)/shard_map/ppermute | solution.py:382

commit v4 on v2

--- a/solution.py
+++ b/solution.py
@@ -19,6 +19,7 @@
 PAIRS = LCAP * RCAP
 TILES = MR * NC
 ZROWS = 256
+ZFIRST = 6
 
 
 def block_of(ref, block_row, block_col):
@@ -88,7 +89,18 @@
     )(pattern.T, left)
 
 
-def pack_right_kernel(pattern, right, after, out, pos, meta, sems):
+def clear(out, zero, sems, begin, end):
+    zero[...] = jnp.zeros_like(zero)
+    copies = [
+        pltpu.make_async_copy(zero, out.at[pl.ds(n * ZROWS, ZROWS), :], sems.at[n - begin])
+        for n in range(begin, end)
+    ]
+    for copy in copies:
+        copy.start()
+    return copies
+
+
+def pack_right_kernel(pattern, right, after, out, product, pos, meta, sems, zero, zero_sems):
     del after
     part = lax.rem(lax.axis_index("col"), 2)
     count = 0
@@ -114,20 +126,26 @@
     meta[...] = row.astype(jnp.float32).astype(jnp.bfloat16)
     copies.append(pltpu.make_async_copy(meta, out.at[pl.ds(BLK, META), :], sems.at[RCAP]))
     copies[-1].start()
+    copies += clear(product, zero, zero_sems, 0, ZFIRST)
     for copy in copies:
         copy.wait()
 
 
-def pack_right(pattern, right, after):
+def pack_right(pattern, right, after, shape):
     return pl.pallas_call(
         pack_right_kernel,
-        out_shape=jax.ShapeDtypeStruct((BLK + META, RCAP * BLK), jnp.bfloat16),
+        out_shape=(
+            jax.ShapeDtypeStruct((BLK + META, RCAP * BLK), jnp.bfloat16),
+            jax.ShapeDtypeStruct(shape, jnp.bfloat16),
+        ),
         in_specs=[spec(pltpu.SMEM), spec(pltpu.HBM), spec(pl.ANY)],
-        out_specs=spec(pl.ANY),
+        out_specs=[spec(pl.ANY), spec(pltpu.HBM)],
         scratch_shapes=[
             pltpu.SMEM((RCAP + 1,), jnp.int32),
             pltpu.VMEM((META, RCAP * BLK), jnp.bfloat16),
             pltpu.SemaphoreType.DMA((RCAP + 1,)),
+            pltpu.VMEM((ZROWS, shape[1]), jnp.bfloat16),
+            pltpu.SemaphoreType.DMA((ZFIRST,)),
         ],
         compiler_params=pltpu.CompilerParams(vmem_limit_bytes=52 << 20),
         cost_estimate=pl.CostEstimate(flops=0, bytes_accessed=1 << 20, transcendentals=0),
@@ -161,7 +179,7 @@
         def meet(a, total, b=b, j=j):
             target = (left_at(a) & (MR - 1)) * NC + j
             code = a * RCAP + b
-            wanted = kept(target)
+            wanted = kept[target] >= 0
             held = owner[target]
             fresh = jnp.logical_and(wanted, held == 0)
 
@@ -170,7 +188,7 @@
                 owner[target] = code + 1
                 slot_of[total] = code * TILES + target
 
-            @pl.when(jnp.logical_and(wanted, held != 0))
+            @pl.when(jnp.logical_and(wanted, held > 0))
             def _():
                 rows, cols = piece(held - 1)
                 more_rows, more_cols = piece(code)
@@ -215,17 +233,12 @@
 
 
 def first_kernel(
-    keep, left, r0, r1, out, prod, table,
-    zero, zero_sems, right, stage, meta_v, meta, owner, slot_of, meta_sem, out_sems,
+    keep, left, r0, r1, begun, out, prod, table,
+    zero, zero_sems, right, stage, meta_v, meta, slot_of, meta_sem, out_sems,
 ):
-    zero[...] = jnp.zeros_like(zero)
-    clears = [
-        pltpu.make_async_copy(zero, out.at[pl.ds(n * ZROWS, ZROWS), :], zero_sems.at[n])
-        for n in range(out.shape[0] // ZROWS)
-    ]
-    for copy in clears:
-        copy.start()
+    del begun
     odd = lax.rem(lax.axis_index("row"), 2)
+    clears = clear(out, zero, zero_sems, ZFIRST, out.shape[0] // ZROWS)
     line = lax.broadcasted_iota(jnp.int32, (META, BLK), 0)
     rows = left[pl.ds(HALF, META), :].astype(jnp.float32)
     for n, ref in enumerate((r0, r1)):
@@ -235,15 +248,15 @@
     meta_copy = pltpu.make_async_copy(meta_v, meta, meta_sem)
     meta_copy.start()
     for at in range(TILES):
-        owner[at] = 0
+        table[at] = jnp.minimum(keep[at // NC, at % NC], 1) - 1
     choose(odd, r0, r1, right)
     products(((left, 0), (left, HALF + META)), right, prod)
     meta_copy.wait()
     total = gather(
         lambda a: meta[0, a],
         lambda b: meta[1 + odd, b],
-        lambda target: keep[target >> 3, target & (NC - 1)] != 0,
-        owner,
+        table,
+        table,
         prod,
         slot_of,
     )
@@ -255,48 +268,47 @@
     for copy in clears:
         copy.wait()
     write(total, value, slot_of, stage, out, out_sems)
-    for i in range(MR):
-        for j in range(NC):
-            table[i * NC + j] = jnp.where(keep[i, j] != 0, owner[i * NC + j], -1)
     for b in range(RCAP):
         table[TILES + b] = meta[2 - odd, b]
 
 
-def first(keep, left, r0, r1):
+def first(keep, left, r0, r1, begun):
     return pl.pallas_call(
         first_kernel,
         out_shape=(
-            jax.ShapeDtypeStruct((MR * BLK, NC * BLK), jnp.bfloat16),
+            jax.ShapeDtypeStruct(begun.shape, begun.dtype),
             jax.ShapeDtypeStruct((LROWS, RCAP * BLK), jnp.float32),
             jax.ShapeDtypeStruct((TILES + BLK,), jnp.int32),
         ),
-        in_specs=[spec(pltpu.SMEM)] + [spec(pltpu.VMEM)] * 3,
+        in_specs=[spec(pltpu.SMEM)] + [spec(pltpu.VMEM)] * 3 + [spec(pltpu.HBM)],
         out_specs=[spec(pltpu.HBM), spec(pltpu.VMEM), spec(pltpu.SMEM)],
         scratch_shapes=[
-            pltpu.VMEM((ZROWS, NC * BLK), jnp.bfloat16),
-            pltpu.SemaphoreType.DMA((MR * BLK // ZROWS,)),
+            pltpu.VMEM((ZROWS, begun.shape[1]), jnp.bfloat16),
+            pltpu.SemaphoreType.DMA((begun.shape[0] // ZROWS - ZFIRST,)),
             pltpu.VMEM((BLK, RCAP * BLK), jnp.bfloat16),
             pltpu.VMEM((PAIRS, BLK, BLK), jnp.bfloat16),
             pltpu.VMEM((META, BLK), jnp.int32),
             pltpu.SMEM((META, BLK), jnp.int32),
-            pltpu.SMEM((TILES,), jnp.int32),
             pltpu.SMEM((PAIRS,), jnp.int32),
             pltpu.SemaphoreType.DMA,
             pltpu.SemaphoreType.DMA((PAIRS,)),
         ],
+        input_output_aliases={4: 0},
         compiler_params=pltpu.CompilerParams(vmem_limit_bytes=32 << 20),
         cost_estimate=pl.CostEstimate(
             flops=10**10, bytes_accessed=14 << 20, transcendentals=0
         ),
         name="first",
-    )(keep, left, r0, r1)
+    )(keep, left, r0, r1, begun)
 
 
 def last_kernel(
-    table, left, more, r0, r1, before, zero, out,
-    right, prod, stage, meta_v, meta, owner, slot_of, meta_sem, out_sems,
+    table_in, left, more, r0, r1, before, zero, out,
+    table, table_sem, right, prod, stage, meta_v, meta, owner, slot_of, meta_sem, out_sems,
 ):
     del zero
+    table_copy = pltpu.make_async_copy(table_in, table, table_sem)
+    table_copy.start()
     odd = lax.rem(lax.axis_index("row"), 2)
     meta_v[...] = left[pl.ds(HALF, META), :].astype(jnp.float32).astype(jnp.int32)
     meta_copy = pltpu.make_async_copy(meta_v, meta, meta_sem)
@@ -306,10 +318,11 @@
     choose(odd, r1, r0, right)
     products(((left, 0), (more, 0)), right, prod)
     meta_copy.wait()
+    table_copy.wait()
     total = gather(
         lambda a: meta[0, a],
         lambda b: table[TILES + b],
-        lambda target: table[target] >= 0,
+        table,
         owner,
         prod,
         slot_of,
@@ -329,9 +342,11 @@
     return pl.pallas_call(
         last_kernel,
         out_shape=jax.ShapeDtypeStruct(out.shape, out.dtype),
-        in_specs=[spec(pltpu.SMEM)] + [spec(pltpu.VMEM)] * 5 + [spec(pltpu.HBM)],
+        in_specs=[spec(pl.ANY)] + [spec(pltpu.VMEM)] * 5 + [spec(pltpu.HBM)],
         out_specs=spec(pltpu.HBM),
         scratch_shapes=[
+            pltpu.SMEM(table.shape, jnp.int32),
+            pltpu.SemaphoreType.DMA,
             pltpu.VMEM((BLK, RCAP * BLK), jnp.bfloat16),
             pltpu.VMEM((LROWS, RCAP * BLK), jnp.float32),
             pltpu.VMEM((PAIRS, BLK, BLK), jnp.bfloat16),
@@ -385,7 +400,8 @@
     even = moved(whole, lambda r, c: (r, c - group * (r + r % 2)))
     roads = {at: detour(*at, cols_n, group) for at in devices}
     between = send(half, [((r, roads[r, c][0]), (r, roads[r, c][1])) for r, c in devices])
-    rpack = pack_right(right_pattern, right_matrix, whole)
+    shape = (left_matrix.shape[0], right_matrix.shape[1])
+    rpack, begun = pack_right(right_pattern, right_matrix, whole, shape)
     r0 = moved(rpack, lambda r, c: (r - c // group, c))
     r1 = moved(rpack, lambda r, c: (r - c // group - 1, c))
     passed = moved(
@@ -393,7 +409,7 @@
         lambda r, c: (r, c + group * (2 * (r % 2) - 1)),
     )
     more = send(between, [((r, roads[r, c][1]), (r, c)) for r, c in devices])
-    out, before, table = first(keep_mask, even, r0, r1)
+    out, before, table = first(keep_mask, even, r0, r1, begun)
     return last(table, passed, more, r0, r1, before, out)
 
 

time: 36.8 us -> 38.3 us (1.041)
  the two profiles are of different devices: /device:TPU:52 before, /device:TPU:96 now
where the time goes in v4:
time: 38.3 us; the launch traced here: 37.8 us
  starting transfers between devices  15.2 us (40%)
  Pallas kernels  13 us (34%)
  waiting for transfers between devices  7.33 us (19%)
  local copies, waits for them, and re-layouts  2.15 us (6%)
    ppermute x6, starting transfers between devices, send(): return lax.ppermute(value, ('row', 'col'), pairs)  15.2 us
    ppermute x6, waiting for transfers between devices, send(): return lax.ppermute(value, ('row', 'col'), pairs)  7.33 us
    pallas_call x1, Pallas kernels, first(): pl.pallas_call(first_kernel, out_shape=(jax.ShapeDtypeStruct(begun.shape,...  5.6 us
    pallas_call x1, Pallas kernels, last(): pl.pallas_call(last_kernel, out_shape=jax.ShapeDtypeStruct(out.shape, out...  2.67 us
    pallas_call x1, Pallas kernels, pack_right(): pl.pallas_call(pack_right_kernel, out_shape=(jax.ShapeDtypeStruct((BLK +...  2.48 us
    pallas_call x1, Pallas kernels, pack_left(): pl.pallas_call(pack_left_kernel, out_shape=(jax.ShapeDtypeStruct((LROWS +...  2.3 us
    unnamed x5, local copies, waits for them, and re-layouts  2.13 us
  transfers between devices with their start and end apart: 6, of which 1 were waited for; matrix products, arithmetic and copies ran while one was open for 2% of the time, Pallas kernels for 21%

profile of v4, /device:TPU:96, one launch (start us, length us, event | category | flops | bytes accessed | tf_op | source)
XLA Modules:
  0.0 37.8 jit_solution(7343190817556414690)
XLA Ops:
  0.0 0.0 copy-start.1
  0.0 0.7 %copy-done.1 = s32[32,4]{0,1:T(4,128)S(1)} copy-done((s32[32,4]{0,1:T(4,128)S(1)}, s32[32,4]{0,1:T(4,128)}, u32[]{:S(2)}) %copy-start.1) | copy-done | bytes 536
  0.7 2.3 %pack_left.1 = (bf16[2064,128]{1,0:T(8,128)(2,1)S(1)}, bf16[1024,128]{1,0:T(8,128)(2,1)S(1)}) custom-call(s32[4,32]{1,0:T(4,128)S(1)} %bitcast.1, bf16[4096,512]{1,0:T(8,128)(2,1)} %left.1), custom_call_target="tpu_custom_call" | custom-call | bytes 2097152 | tf_op jit(solution)/shard_map/pack_left/pallas_call | solution.py:73
  3.0 0.7 %collective-permute-start = (bf16[2064,128]{1,0:T(8,128)(2,1)S(1)}, bf16[2064,128]{1,0:T(8,128)(2,1)S(1)}, u32[]{:S(2)}, u32[]{:S(2)}) collective-permute-start(bf16[2064,128]{1,0:T(8,128)(2,1)S(1)} %get-tuple-element.12.after), channel_id=1, source_target_pairs={{0,0},{1,1},{2,2},{3,3},{4,4},{5,5},{6,6},{7,7},{8,8},{9,9},{10,10... | collective-permute-start | bytes 1585160 | tf_op jit(solution)/shard_map/ppermute | solution.py:388
  3.7 1.2 %collective-permute-start.4 = (bf16[1024,128]{1,0:T(8,128)(2,1)S(1)}, bf16[1024,128]{1,0:T(8,128)(2,1)S(1)}, u32[]{:S(2)}, u32[]{:S(2)}) collective-permute-start(bf16[1024,128]{1,0:T(8,128)(2,1)S(1)} %get-tuple-element.16), channel_id=1, source_target_pairs={{2,0},{3,1},{4,2},{5,3},{6,4},{7,5},{8,6},{9,7},{10,8},{11,9},{12,... | collective-permute-start | bytes 786440 | tf_op jit(solution)/shard_map/ppermute | solution.py:388
  4.9 0.0 copy-start
  4.9 0.7 %copy-done = s32[8,8]{1,0:T(8,128)S(1)} copy-done((s32[8,8]{1,0:T(8,128)S(1)}, s32[8,8]{1,0:T(8,128)}, u32[]{:S(2)}) %copy-start) | copy-done | bytes 280
  5.6 2.5 %pack_right.1 = (bf16[144,512]{1,0:T(8,128)(2,1)S(1)}, bf16[4096,1024]{1,0:T(8,128)(2,1)}) custom-call(s32[8,8]{1,0:T(8,128)S(1)} %copy-done, bf16[1024,1024]{1,0:T(8,128)(2,1)} %right.1, bf16[2064,128]{1,0:T(8,128)(2,1)S(1)} %get-tuple-element.12.after), custom_call_target="tpu_custom_call" | custom-call | bytes 1048576 | tf_op jit(solution)/shard_map/pack_right/pallas_call | solution.py:135
  8.1 9.1 %collective-permute-start.1 = (bf16[144,512]{1,0:T(8,128)(2,1)S(1)}, bf16[144,512]{1,0:T(8,128)(2,1)S(1)}, u32[]{:S(2)}, u32[]{:S(2)}) collective-permute-start(bf16[144,512]{1,0:T(8,128)(2,1)S(1)} %get-tuple-element.13), channel_id=1, source_target_pairs={{0,0},{1,1},{2,114},{3,115},{4,100},{5,101},{6,86},{7,87},{8,72},{... | collective-permute-start | bytes 442376 | tf_op jit(solution)/shard_map/ppermute | solution.py:388
  17.2 1.9 %collective-permute-start.2 = (bf16[144,512]{1,0:T(8,128)(2,1)S(1)}, bf16[144,512]{1,0:T(8,128)(2,1)S(1)}, u32[]{:S(2)}, u32[]{:S(2)}) collective-permute-start(bf16[144,512]{1,0:T(8,128)(2,1)S(1)} %get-tuple-element.13), channel_id=1, source_target_pairs={{0,112},{1,113},{2,98},{3,99},{4,84},{5,85},{6,70},{7,71},{8,56},{... | collective-permute-start | bytes 442376 | tf_op jit(solution)/shard_map/ppermute | solution.py:388
  19.1 0.8 %copy.8.keep = s32[32,8]{1,0:T(8,128)S(1)} copy(s32[32,8]{0,1:T(8,128)} %param.9) | data formatting | bytes 2048 | tf_op args[4]
  19.9 0.0 collective-permute-done.4
  19.9 0.7 %collective-permute-start.5 = (bf16[1024,128]{1,0:T(8,128)(2,1)S(1)}, bf16[1024,128]{1,0:T(8,128)(2,1)S(1)}, u32[]{:S(2)}, u32[]{:S(2)}) collective-permute-start(bf16[1024,128]{1,0:T(8,128)(2,1)S(1)} %collective-permute-done.4), channel_id=1, source_target_pairs={{0,0},{1,1},{2,2},{3,3},{4,4},{5,5},{6,6},{7,7},{8,8},{9,9},{10,10... | collective-permute-start | bytes 786440 | tf_op jit(solution)/shard_map/ppermute | solution.py:388
  20.6 0.0 collective-permute-done.left
  20.6 1.6 %collective-permute-start.3 = (bf16[1040,128]{1,0:T(8,128)(2,1)S(1)}, bf16[1040,128]{1,0:T(8,128)(2,1)S(1)}, u32[]{:S(2)}, u32[]{:S(2)}) collective-permute-start(bf16[1040,128]{1,0:T(8,128)(2,1)S(1)} %slice.4), channel_id=1, source_target_pairs={{0,14},{1,15},{2,0},{3,1},{4,2},{5,3},{6,4},{7,5},{8,6},{9,7},{10,... | collective-permute-start | bytes 798728 | tf_op jit(solution)/shard_map/ppermute | solution.py:388
  22.2 0.0 collective-permute-done.1.r0
  22.2 7.3 %collective-permute-done.2.r1 = bf16[144,512]{1,0:T(8,128)(2,1)S(1)} collective-permute-done((bf16[144,512]{1,0:T(8,128)(2,1)S(1)}, bf16[144,512]{1,0:T(8,128)(2,1)S(1)}, u32[]{:S(2)}, u32[]{:S(2)}) %collective-permute-start.2) | collective-permute-done | bytes 147488 | tf_op jit(solution)/shard_map/ppermute | solution.py:388
  29.5 5.6 %first.1 = (bf16[4096,1024]{1,0:T(8,128)(2,1)}, f32[2048,512]{1,0:T(8,128)S(1)}, s32[384]{0:T(512)S(1)}) custom-call(s32[32,8]{1,0:T(8,128)S(1)} %copy.8.keep, bf16[2064,128]{1,0:T(8,128)(2,1)S(1)} %collective-permute-done.left, bf16[144,512]{1,0:T(8,128)(2,1)S(1)} %collective-permute-done.1.r0, ...), custom_call_target="tpu_custom_call", output_to_operand_aliasing={{0}: (4, {})} | custom-call | flops 10000000000 | bytes 14680064 | tf_op jit(solution)/shard_map/first/pallas_call | solution.py:276
  35.1 0.0 collective-permute-done.5.more
  35.1 0.0 collective-permute-done.3.left
  35.1 2.7 %last.1 = bf16[4096,1024]{1,0:T(8,128)(2,1)} custom-call(s32[384]{0:T(512)S(1)} %get-tuple-element.15.table_in, bf16[1040,128]{1,0:T(8,128)(2,1)S(1)} %collective-permute-done.3.left, bf16[1024,128]{1,0:T(8,128)(2,1)S(1)} %collective-permute-done.5.more, bf16[144,512]{1,0:T(8,128)(2,1)S(1)} %collective-permute-done.1.r0, ...), custom_call_target="tpu_custom_call", output_to_operand_aliasing={{}: (6, {})} | custom-call | flops 268435456 | bytes 4194304 | tf_op jit(solution)/shard_map/last/pallas_call | solution.py:342
  (1 shorter events, 0.0 us)
Async XLA Ops:
  0.0 0.7 %copy-start.1 = (s32[32,4]{0,1:T(4,128)S(1)}, s32[32,4]{0,1:T(4,128)}, u32[]{:S(2)}) copy-start(s32[32,4]{0,1:T(4,128)} %param.6) | copy-start | bytes 1540
  3.0 17.6 %collective-permute-start = (bf16[2064,128]{1,0:T(8,128)(2,1)S(1)}, bf16[2064,128]{1,0:T(8,128)(2,1)S(1)}, u32[]{:S(2)}, u32[]{:S(2)}) collective-permute-start(bf16[2064,128]{1,0:T(8,128)(2,1)S(1)} %get-tuple-element.12.after), channel_id=1, source_target_pairs={{0,0},{1,1},{2,2},{3,3},{4,4},{5,5},{6,6},{7,7},{8,8},{9,9},{10,10... | collective-permute-start | bytes 1585160 | tf_op jit(solution)/shard_map/ppermute | solution.py:388
  3.7 16.2 %collective-permute-start.4 = (bf16[1024,128]{1,0:T(8,128)(2,1)S(1)}, bf16[1024,128]{1,0:T(8,128)(2,1)S(1)}, u32[]{:S(2)}, u32[]{:S(2)}) collective-permute-start(bf16[1024,128]{1,0:T(8,128)(2,1)S(1)} %get-tuple-element.16), channel_id=1, source_target_pairs={{2,0},{3,1},{4,2},{5,3},{6,4},{7,5},{8,6},{9,7},{10,8},{11,9},{12,... | collective-permute-start | bytes 786440 | tf_op jit(solution)/shard_map/ppermute | solution.py:388
  4.9 0.7 %copy-start = (s32[8,8]{1,0:T(8,128)S(1)}, s32[8,8]{1,0:T(8,128)}, u32[]{:S(2)}) copy-start(s32[8,8]{1,0:T(8,128)} %pattern.1) | copy-start | bytes 772
  8.1 14.1 %collective-permute-start.1 = (bf16[144,512]{1,0:T(8,128)(2,1)S(1)}, bf16[144,512]{1,0:T(8,128)(2,1)S(1)}, u32[]{:S(2)}, u32[]{:S(2)}) collective-permute-start(bf16[144,512]{1,0:T(8,128)(2,1)S(1)} %get-tuple-element.13), channel_id=1, source_target_pairs={{0,0},{1,1},{2,114},{3,115},{4,100},{5,101},{6,86},{7,87},{8,72},{... | collective-permute-start | bytes 442376 | tf_op jit(solution)/shard_map/ppermute | solution.py:388
  17.2 12.3 %collective-permute-start.2 = (bf16[144,512]{1,0:T(8,128)(2,1)S(1)}, bf16[144,512]{1,0:T(8,128)(2,1)S(1)}, u32[]{:S(2)}, u32[]{:S(2)}) collective-permute-start(bf16[144,512]{1,0:T(8,128)(2,1)S(1)} %get-tuple-element.13), channel_id=1, source_target_pairs={{0,112},{1,113},{2,98},{3,99},{4,84},{5,85},{6,70},{7,71},{8,56},{... | collective-permute-start | bytes 442376 | tf_op jit(solution)/shard_map/ppermute | solution.py:388
  19.9 15.2 %collective-permute-start.5 = (bf16[1024,128]{1,0:T(8,128)(2,1)S(1)}, bf16[1024,128]{1,0:T(8,128)(2,1)S(1)}, u32[]{:S(2)}, u32[]{:S(2)}) collective-permute-start(bf16[1024,128]{1,0:T(8,128)(2,1)S(1)} %collective-permute-done.4), channel_id=1, source_target_pairs={{0,0},{1,1},{2,2},{3,3},{4,4},{5,5},{6,6},{7,7},{8,8},{9,9},{10,10... | collective-permute-start | bytes 786440 | tf_op jit(solution)/shard_map/ppermute | solution.py:388
  20.6 14.5 %collective-permute-start.3 = (bf16[1040,128]{1,0:T(8,128)(2,1)S(1)}, bf16[1040,128]{1,0:T(8,128)(2,1)S(1)}, u32[]{:S(2)}, u32[]{:S(2)}) collective-permute-start(bf16[1040,128]{1,0:T(8,128)(2,1)S(1)} %slice.4), channel_id=1, source_target_pairs={{0,14},{1,15},{2,0},{3,1},{4,2},{5,3},{6,4},{7,5},{8,6},{9,7},{10,... | collective-permute-start | bytes 798728 | tf_op jit(solution)/shard_map/ppermute | solution.py:388

commit v5 on v2

--- a/solution.py
+++ b/solution.py
@@ -19,6 +19,7 @@
 PAIRS = LCAP * RCAP
 TILES = MR * NC
 ZROWS = 256
+NOTES = TILES + 64
 
 
 def block_of(ref, block_row, block_col):
@@ -161,7 +162,7 @@
         def meet(a, total, b=b, j=j):
             target = (left_at(a) & (MR - 1)) * NC + j
             code = a * RCAP + b
-            wanted = kept(target)
+            wanted = kept[target] >= 0
             held = owner[target]
             fresh = jnp.logical_and(wanted, held == 0)
 
@@ -170,7 +171,7 @@
                 owner[target] = code + 1
                 slot_of[total] = code * TILES + target
 
-            @pl.when(jnp.logical_and(wanted, held != 0))
+            @pl.when(jnp.logical_and(wanted, held > 0))
             def _():
                 rows, cols = piece(held - 1)
                 more_rows, more_cols = piece(code)
@@ -183,27 +184,6 @@
     return total
 
 
-def write(total, value, slot_of, stage, out, sems):
-    def copy_out(slot, target):
-        return pltpu.make_async_copy(
-            stage.at[slot], block_of(out, target >> 3, target & (NC - 1)), sems.at[slot]
-        )
-
-    def send(slot, carry):
-        entry = slot_of[slot]
-        target = entry & (TILES - 1)
-        stage[slot] = value(entry >> 8, target).astype(jnp.bfloat16)
-        copy_out(slot, target).start()
-        return carry
-
-    def drain(slot, carry):
-        copy_out(slot, slot_of[slot] & (TILES - 1)).wait()
-        return carry
-
-    lax.fori_loop(0, total, send, 0)
-    lax.fori_loop(0, total, drain, 0)
-
-
 def choose(flag, first, second, held):
     @pl.when(flag == 0)
     def _():
@@ -216,7 +196,7 @@
 
 def first_kernel(
     keep, left, r0, r1, out, prod, table,
-    zero, zero_sems, right, stage, meta_v, meta, owner, slot_of, meta_sem, out_sems,
+    zero, zero_sems, right, meta_v, meta, slot_of, meta_sem,
 ):
     zero[...] = jnp.zeros_like(zero)
     clears = [
@@ -235,31 +215,30 @@
     meta_copy = pltpu.make_async_copy(meta_v, meta, meta_sem)
     meta_copy.start()
     for at in range(TILES):
-        owner[at] = 0
+        table[at] = jnp.minimum(keep[at // NC, at % NC], 1) - 1
     choose(odd, r0, r1, right)
     products(((left, 0), (left, HALF + META)), right, prod)
     meta_copy.wait()
     total = gather(
         lambda a: meta[0, a],
         lambda b: meta[1 + odd, b],
-        lambda target: keep[target >> 3, target & (NC - 1)] != 0,
-        owner,
+        table,
+        table,
         prod,
         slot_of,
     )
 
-    def value(code, target):
-        rows, cols = piece(code)
-        return prod[rows, cols]
-
+    for b in range(RCAP):
+        table[TILES + b] = meta[2 - odd, b]
+    table[TILES + RCAP] = total
+
+    def note(slot, carry):
+        table[NOTES + slot] = slot_of[slot]
+        return carry
+
+    lax.fori_loop(0, total, note, 0)
     for copy in clears:
         copy.wait()
-    write(total, value, slot_of, stage, out, out_sems)
-    for i in range(MR):
-        for j in range(NC):
-            table[i * NC + j] = jnp.where(keep[i, j] != 0, owner[i * NC + j], -1)
-    for b in range(RCAP):
-        table[TILES + b] = meta[2 - odd, b]
 
 
 def first(keep, left, r0, r1):
@@ -268,7 +247,7 @@
         out_shape=(
             jax.ShapeDtypeStruct((MR * BLK, NC * BLK), jnp.bfloat16),
             jax.ShapeDtypeStruct((LROWS, RCAP * BLK), jnp.float32),
-            jax.ShapeDtypeStruct((TILES + BLK,), jnp.int32),
+            jax.ShapeDtypeStruct((NOTES + PAIRS,), jnp.int32),
         ),
         in_specs=[spec(pltpu.SMEM)] + [spec(pltpu.VMEM)] * 3,
         out_specs=[spec(pltpu.HBM), spec(pltpu.VMEM), spec(pltpu.SMEM)],
@@ -276,13 +255,10 @@
             pltpu.VMEM((ZROWS, NC * BLK), jnp.bfloat16),
             pltpu.SemaphoreType.DMA((MR * BLK // ZROWS,)),
             pltpu.VMEM((BLK, RCAP * BLK), jnp.bfloat16),
-            pltpu.VMEM((PAIRS, BLK, BLK), jnp.bfloat16),
             pltpu.VMEM((META, BLK), jnp.int32),
             pltpu.SMEM((META, BLK), jnp.int32),
-            pltpu.SMEM((TILES,), jnp.int32),
             pltpu.SMEM((PAIRS,), jnp.int32),
             pltpu.SemaphoreType.DMA,
-            pltpu.SemaphoreType.DMA((PAIRS,)),
         ],
         compiler_params=pltpu.CompilerParams(vmem_limit_bytes=32 << 20),
         cost_estimate=pl.CostEstimate(
@@ -293,10 +269,12 @@
 
 
 def last_kernel(
-    table, left, more, r0, r1, before, zero, out,
-    right, prod, stage, meta_v, meta, owner, slot_of, meta_sem, out_sems,
+    table_in, left, more, r0, r1, before, zero, out,
+    table, table_sem, right, prod, stage, meta_v, meta, owner, slot_of, meta_sem, out_sems,
 ):
     del zero
+    table_copy = pltpu.make_async_copy(table_in, table, table_sem)
+    table_copy.start()
     odd = lax.rem(lax.axis_index("row"), 2)
     meta_v[...] = left[pl.ds(HALF, META), :].astype(jnp.float32).astype(jnp.int32)
     meta_copy = pltpu.make_async_copy(meta_v, meta, meta_sem)
@@ -306,41 +284,74 @@
     choose(odd, r1, r0, right)
     products(((left, 0), (more, 0)), right, prod)
     meta_copy.wait()
+    table_copy.wait()
     total = gather(
         lambda a: meta[0, a],
         lambda b: table[TILES + b],
-        lambda target: table[target] >= 0,
+        table,
         owner,
         prod,
         slot_of,
     )
 
-    def value(code, target):
-        rows, cols = piece(code)
+    def copy_out(slot, target):
+        return pltpu.make_async_copy(
+            stage.at[slot], block_of(out, target >> 3, target & (NC - 1)), out_sems.at[slot]
+        )
+
+    def send(slot, carry):
+        entry = slot_of[slot]
+        target = entry & (TILES - 1)
+        rows, cols = piece(entry >> 8)
+        fresh = prod[rows, cols]
         held = table[target]
         old_rows, old_cols = piece(jnp.maximum(held - 1, 0))
-        fresh = prod[rows, cols]
-        return jnp.where(held > 0, fresh + before[old_rows, old_cols], fresh)
-
-    write(total, value, slot_of, stage, out, out_sems)
+        both = jnp.where(held > 0, fresh + before[old_rows, old_cols], fresh)
+        stage[slot] = both.astype(jnp.bfloat16)
+        copy_out(slot, target).start()
+        return carry
+
+    def send_old(n, slot):
+        entry = table[NOTES + n]
+        target = entry & (TILES - 1)
+        alone = owner[target] == 0
+
+        @pl.when(alone)
+        def _():
+            rows, cols = piece(entry >> 8)
+            slot_of[slot] = entry
+            stage[slot] = before[rows, cols].astype(jnp.bfloat16)
+            copy_out(slot, target).start()
+
+        return slot + alone.astype(jnp.int32)
+
+    def drain(slot, carry):
+        copy_out(slot, slot_of[slot] & (TILES - 1)).wait()
+        return carry
+
+    lax.fori_loop(0, total, send, 0)
+    slots = lax.fori_loop(0, table[TILES + RCAP], send_old, total)
+    lax.fori_loop(0, slots, drain, 0)
 
 
 def last(table, left, more, r0, r1, before, out):
     return pl.pallas_call(
         last_kernel,
         out_shape=jax.ShapeDtypeStruct(out.shape, out.dtype),
-        in_specs=[spec(pltpu.SMEM)] + [spec(pltpu.VMEM)] * 5 + [spec(pltpu.HBM)],
+        in_specs=[spec(pl.ANY)] + [spec(pltpu.VMEM)] * 5 + [spec(pltpu.HBM)],
         out_specs=spec(pltpu.HBM),
         scratch_shapes=[
+            pltpu.SMEM(table.shape, jnp.int32),
+            pltpu.SemaphoreType.DMA,
             pltpu.VMEM((BLK, RCAP * BLK), jnp.bfloat16),
             pltpu.VMEM((LROWS, RCAP * BLK), jnp.float32),
-            pltpu.VMEM((PAIRS, BLK, BLK), jnp.bfloat16),
+            pltpu.VMEM((2 * PAIRS, BLK, BLK), jnp.bfloat16),
             pltpu.VMEM((META, BLK), jnp.int32),
             pltpu.SMEM((META, BLK), jnp.int32),
             pltpu.SMEM((TILES,), jnp.int32),
-            pltpu.SMEM((PAIRS,), jnp.int32),
+            pltpu.SMEM((2 * PAIRS,), jnp.int32),
             pltpu.SemaphoreType.DMA,
-            pltpu.SemaphoreType.DMA((PAIRS,)),
+            pltpu.SemaphoreType.DMA((2 * PAIRS,)),
         ],
         input_output_aliases={6: 0},
         compiler_params=pltpu.CompilerParams(vmem_limit_bytes=32 << 20),

time: 36.8 us -> 35.9 us (0.976)
  Pallas kernels: 13.5 us -> 12.7 us
    pallas_call x1, Pallas kernels: 6.52 us -> 5.18 us  [first(): pl.pallas_call(first_kernel, out_shape=(jax.ShapeDtypeStruct((MR * BLK, N...]
    pallas_call x1, Pallas kernels: 3.35 us -> 3.9 us  [last(): pl.pallas_call(last_kernel, out_shape=jax.ShapeDtypeStruct(out.shape, out...]
  transfers between devices with their start and end apart: 6 -> 6, of which waited for: 1 -> 1; matrix products, arithmetic and copies ran while one was open for 0% -> 0% of each run, Pallas kernels for 22% -> 19%
where the time goes in v5:
time: 35.9 us; the launch traced here: 35.6 us
  starting transfers between devices  17.1 us (48%)
  Pallas kernels  12.7 us (35%)
  waiting for transfers between devices  4.97 us (14%)
  local copies, waits for them, and re-layouts  0.8 us (2%)
    ppermute x6, starting transfers between devices, send(): return lax.ppermute(value, ('row', 'col'), pairs)  17.1 us
    pallas_call x1, Pallas kernels, first(): pl.pallas_call(first_kernel, out_shape=(jax.ShapeDtypeStruct((MR * BLK, N...  5.18 us
    ppermute x6, waiting for transfers between devices, send(): return lax.ppermute(value, ('row', 'col'), pairs)  4.97 us
    pallas_call x1, Pallas kernels, last(): pl.pallas_call(last_kernel, out_shape=jax.ShapeDtypeStruct(out.shape, out...  3.9 us
    pallas_call x1, Pallas kernels, pack_left(): pl.pallas_call(pack_left_kernel, out_shape=(jax.ShapeDtypeStruct((LROWS +...  2.07 us
    pallas_call x1, Pallas kernels, pack_right(): pl.pallas_call(pack_right_kernel, out_shape=jax.ShapeDtypeStruct((BLK + M...  1.52 us
    unnamed x7, local copies, waits for them, and re-layouts  0.78 us
  transfers between devices with their start and end apart: 6, of which 1 were waited for; matrix products, arithmetic and copies ran while one was open for 0% of the time, Pallas kernels for 19%

profile of v5, /device:TPU:52, one launch (start us, length us, event | category | flops | bytes accessed | tf_op | source)
XLA Modules:
  0.0 35.6 jit_solution(2093770338956136719)
XLA Ops:
  0.0 0.0 copy-start
  0.0 0.0 copy-start.1
  0.0 0.7 %copy-done.1 = s32[32,4]{0,1:T(4,128)S(1)} copy-done((s32[32,4]{0,1:T(4,128)S(1)}, s32[32,4]{0,1:T(4,128)}, u32[]{:S(2)}) %copy-start.1) | copy-done | bytes 536
  0.7 0.0 copy-start.2
  0.7 2.1 %pack_left.1 = (bf16[2064,128]{1,0:T(8,128)(2,1)S(1)}, bf16[1024,128]{1,0:T(8,128)(2,1)S(1)}) custom-call(s32[4,32]{1,0:T(4,128)S(1)} %bitcast.1, bf16[4096,512]{1,0:T(8,128)(2,1)} %left.1), custom_call_target="tpu_custom_call" | custom-call | bytes 2097152 | tf_op jit(solution)/shard_map/pack_left/pallas_call | solution.py:73
  2.8 3.8 %collective-permute-start = (bf16[2064,128]{1,0:T(8,128)(2,1)S(1)}, bf16[2064,128]{1,0:T(8,128)(2,1)S(1)}, u32[]{:S(2)}, u32[]{:S(2)}) collective-permute-start(bf16[2064,128]{1,0:T(8,128)(2,1)S(1)} %get-tuple-element.10.after), channel_id=1, source_target_pairs={{0,0},{1,1},{2,2},{3,3},{4,4},{5,5},{6,6},{7,7},{8,8},{9,9},{10,10... | collective-permute-start | bytes 1585160 | tf_op jit(solution)/shard_map/ppermute | solution.py:384
  6.6 1.3 %collective-permute-start.4 = (bf16[1024,128]{1,0:T(8,128)(2,1)S(1)}, bf16[1024,128]{1,0:T(8,128)(2,1)S(1)}, u32[]{:S(2)}, u32[]{:S(2)}) collective-permute-start(bf16[1024,128]{1,0:T(8,128)(2,1)S(1)} %get-tuple-element.12), channel_id=1, source_target_pairs={{2,0},{3,1},{4,2},{5,3},{6,4},{7,5},{8,6},{9,7},{10,8},{11,9},{12,... | collective-permute-start | bytes 786440 | tf_op jit(solution)/shard_map/ppermute | solution.py:384
  7.9 0.0 copy-done
  7.9 1.5 %pack_right.1 = bf16[144,512]{1,0:T(8,128)(2,1)S(1)} custom-call(s32[8,8]{1,0:T(8,128)S(1)} %copy-done, bf16[1024,1024]{1,0:T(8,128)(2,1)} %right.1, bf16[2064,128]{1,0:T(8,128)(2,1)S(1)} %get-tuple-element.10.after), custom_call_target="tpu_custom_call" | custom-call | bytes 1048576 | tf_op jit(solution)/shard_map/pack_right/pallas_call | solution.py:123
  9.4 4.5 %collective-permute-start.2 = (bf16[144,512]{1,0:T(8,128)(2,1)S(1)}, bf16[144,512]{1,0:T(8,128)(2,1)S(1)}, u32[]{:S(2)}, u32[]{:S(2)}) collective-permute-start(bf16[144,512]{1,0:T(8,128)(2,1)S(1)} %pack_right.1), channel_id=1, source_target_pairs={{0,112},{1,113},{2,98},{3,99},{4,84},{5,85},{6,70},{7,71},{8,56},{... | collective-permute-start | bytes 442376 | tf_op jit(solution)/shard_map/ppermute | solution.py:384
  13.9 1.9 %collective-permute-start.1 = (bf16[144,512]{1,0:T(8,128)(2,1)S(1)}, bf16[144,512]{1,0:T(8,128)(2,1)S(1)}, u32[]{:S(2)}, u32[]{:S(2)}) collective-permute-start(bf16[144,512]{1,0:T(8,128)(2,1)S(1)} %pack_right.1), channel_id=1, source_target_pairs={{0,0},{1,1},{2,114},{3,115},{4,100},{5,101},{6,86},{7,87},{8,72},{... | collective-permute-start | bytes 442376 | tf_op jit(solution)/shard_map/ppermute | solution.py:384
  15.9 0.0 copy-done.2
  15.9 0.1 copy.7.keep
  16.0 0.0 collective-permute-done.4
  16.0 4.3 %collective-permute-start.5 = (bf16[1024,128]{1,0:T(8,128)(2,1)S(1)}, bf16[1024,128]{1,0:T(8,128)(2,1)S(1)}, u32[]{:S(2)}, u32[]{:S(2)}) collective-permute-start(bf16[1024,128]{1,0:T(8,128)(2,1)S(1)} %collective-permute-done.4), channel_id=1, source_target_pairs={{0,0},{1,1},{2,2},{3,3},{4,4},{5,5},{6,6},{7,7},{8,8},{9,9},{10,10... | collective-permute-start | bytes 786440 | tf_op jit(solution)/shard_map/ppermute | solution.py:384
  20.3 0.0 collective-permute-done.left
  20.3 1.3 %collective-permute-start.3 = (bf16[1040,128]{1,0:T(8,128)(2,1)S(1)}, bf16[1040,128]{1,0:T(8,128)(2,1)S(1)}, u32[]{:S(2)}, u32[]{:S(2)}) collective-permute-start(bf16[1040,128]{1,0:T(8,128)(2,1)S(1)} %slice.4), channel_id=1, source_target_pairs={{0,14},{1,15},{2,0},{3,1},{4,2},{5,3},{6,4},{7,5},{8,6},{9,7},{10,... | collective-permute-start | bytes 798728 | tf_op jit(solution)/shard_map/ppermute | solution.py:384
  21.6 0.0 collective-permute-done.2.r1
  21.6 5.0 %collective-permute-done.1.r0 = bf16[144,512]{1,0:T(8,128)(2,1)S(1)} collective-permute-done((bf16[144,512]{1,0:T(8,128)(2,1)S(1)}, bf16[144,512]{1,0:T(8,128)(2,1)S(1)}, u32[]{:S(2)}, u32[]{:S(2)}) %collective-permute-start.1) | collective-permute-done | bytes 147488 | tf_op jit(solution)/shard_map/ppermute | solution.py:384
  26.5 5.2 %first.1 = (bf16[4096,1024]{1,0:T(8,128)(2,1)}, f32[2048,512]{1,0:T(8,128)S(1)}, s32[384]{0:T(512)S(1)}) custom-call(s32[32,8]{1,0:T(8,128)S(1)} %copy.7.keep, bf16[2064,128]{1,0:T(8,128)(2,1)S(1)} %collective-permute-done.left, bf16[144,512]{1,0:T(8,128)(2,1)S(1)} %collective-permute-done.1.r0, bf16[144,512]{1,0:T(8,128)(2,1)S(1)} %collective-permute-done.2.r1), custom_call_target="tpu_custom_call" | custom-call | flops 10000000000 | bytes 14680064 | tf_op jit(solution)/shard_map/first/pallas_call | solution.py:245
  31.7 0.0 collective-permute-done.5.more
  31.7 0.0 collective-permute-done.3.left
  31.7 3.9 %last.1 = bf16[4096,1024]{1,0:T(8,128)(2,1)} custom-call(s32[384]{0:T(512)S(1)} %get-tuple-element.11.table_in, bf16[1040,128]{1,0:T(8,128)(2,1)S(1)} %collective-permute-done.3.left, bf16[1024,128]{1,0:T(8,128)(2,1)S(1)} %collective-permute-done.5.more, bf16[144,512]{1,0:T(8,128)(2,1)S(1)} %collective-permute-done.1.r0, ...), custom_call_target="tpu_custom_call", output_to_operand_aliasing={{}: (6, {})} | custom-call | flops 268435456 | bytes 4194304 | tf_op jit(solution)/shard_map/last/pallas_call | solution.py:338
  (1 shorter events, 0.0 us)
Async XLA Ops:
  0.0 7.9 %copy-start = (s32[8,8]{1,0:T(8,128)S(1)}, s32[8,8]{1,0:T(8,128)}, u32[]{:S(2)}) copy-start(s32[8,8]{1,0:T(8,128)} %pattern.1) | copy-start | bytes 772
  0.0 0.7 %copy-start.1 = (s32[32,4]{0,1:T(4,128)S(1)}, s32[32,4]{0,1:T(4,128)}, u32[]{:S(2)}) copy-start(s32[32,4]{0,1:T(4,128)} %param.6) | copy-start | bytes 1540
  0.7 15.2 %copy-start.2 = (s32[32,8]{0,1:T(8,128)S(1)}, s32[32,8]{0,1:T(8,128)}, u32[]{:S(2)}) copy-start(s32[32,8]{0,1:T(8,128)} %param.9) | copy-start | bytes 3076
  2.8 17.5 %collective-permute-start = (bf16[2064,128]{1,0:T(8,128)(2,1)S(1)}, bf16[2064,128]{1,0:T(8,128)(2,1)S(1)}, u32[]{:S(2)}, u32[]{:S(2)}) collective-permute-start(bf16[2064,128]{1,0:T(8,128)(2,1)S(1)} %get-tuple-element.10.after), channel_id=1, source_target_pairs={{0,0},{1,1},{2,2},{3,3},{4,4},{5,5},{6,6},{7,7},{8,8},{9,9},{10,10... | collective-permute-start | bytes 1585160 | tf_op jit(solution)/shard_map/ppermute | solution.py:384
  6.6 9.3 %collective-permute-start.4 = (bf16[1024,128]{1,0:T(8,128)(2,1)S(1)}, bf16[1024,128]{1,0:T(8,128)(2,1)S(1)}, u32[]{:S(2)}, u32[]{:S(2)}) collective-permute-start(bf16[1024,128]{1,0:T(8,128)(2,1)S(1)} %get-tuple-element.12), channel_id=1, source_target_pairs={{2,0},{3,1},{4,2},{5,3},{6,4},{7,5},{8,6},{9,7},{10,8},{11,9},{12,... | collective-permute-start | bytes 786440 | tf_op jit(solution)/shard_map/ppermute | solution.py:384
  9.4 12.1 %collective-permute-start.2 = (bf16[144,512]{1,0:T(8,128)(2,1)S(1)}, bf16[144,512]{1,0:T(8,128)(2,1)S(1)}, u32[]{:S(2)}, u32[]{:S(2)}) collective-permute-start(bf16[144,512]{1,0:T(8,128)(2,1)S(1)} %pack_right.1), channel_id=1, source_target_pairs={{0,112},{1,113},{2,98},{3,99},{4,84},{5,85},{6,70},{7,71},{8,56},{... | collective-permute-start | bytes 442376 | tf_op jit(solution)/shard_map/ppermute | solution.py:384
  13.9 12.6 %collective-permute-start.1 = (bf16[144,512]{1,0:T(8,128)(2,1)S(1)}, bf16[144,512]{1,0:T(8,128)(2,1)S(1)}, u32[]{:S(2)}, u32[]{:S(2)}) collective-permute-start(bf16[144,512]{1,0:T(8,128)(2,1)S(1)} %pack_right.1), channel_id=1, source_target_pairs={{0,0},{1,1},{2,114},{3,115},{4,100},{5,101},{6,86},{7,87},{8,72},{... | collective-permute-start | bytes 442376 | tf_op jit(solution)/shard_map/ppermute | solution.py:384
  16.0 15.8 %collective-permute-start.5 = (bf16[1024,128]{1,0:T(8,128)(2,1)S(1)}, bf16[1024,128]{1,0:T(8,128)(2,1)S(1)}, u32[]{:S(2)}, u32[]{:S(2)}) collective-permute-start(bf16[1024,128]{1,0:T(8,128)(2,1)S(1)} %collective-permute-done.4), channel_id=1, source_target_pairs={{0,0},{1,1},{2,2},{3,3},{4,4},{5,5},{6,6},{7,7},{8,8},{9,9},{10,10... | collective-permute-start | bytes 786440 | tf_op jit(solution)/shard_map/ppermute | solution.py:384
  20.3 11.4 %collective-permute-start.3 = (bf16[1040,128]{1,0:T(8,128)(2,1)S(1)}, bf16[1040,128]{1,0:T(8,128)(2,1)S(1)}, u32[]{:S(2)}, u32[]{:S(2)}) collective-permute-start(bf16[1040,128]{1,0:T(8,128)(2,1)S(1)} %slice.4), channel_id=1, source_target_pairs={{0,14},{1,15},{2,0},{3,1},{4,2},{5,3},{6,4},{7,5},{8,6},{9,7},{10,... | collective-permute-start | bytes 798728 | tf_op jit(solution)/shard_map/ppermute | solution.py:384

commit v6 on v2

--- a/solution.py
+++ b/solution.py
@@ -161,7 +161,7 @@
         def meet(a, total, b=b, j=j):
             target = (left_at(a) & (MR - 1)) * NC + j
             code = a * RCAP + b
-            wanted = kept(target)
+            wanted = kept[target] >= 0
             held = owner[target]
             fresh = jnp.logical_and(wanted, held == 0)
 
@@ -170,7 +170,7 @@
                 owner[target] = code + 1
                 slot_of[total] = code * TILES + target
 
-            @pl.when(jnp.logical_and(wanted, held != 0))
+            @pl.when(jnp.logical_and(wanted, held > 0))
             def _():
                 rows, cols = piece(held - 1)
                 more_rows, more_cols = piece(code)
@@ -216,15 +216,8 @@
 
 def first_kernel(
     keep, left, r0, r1, out, prod, table,
-    zero, zero_sems, right, stage, meta_v, meta, owner, slot_of, meta_sem, out_sems,
+    zero, zero_sems, right, stage, meta_v, meta, slot_of, meta_sem, out_sems,
 ):
-    zero[...] = jnp.zeros_like(zero)
-    clears = [
-        pltpu.make_async_copy(zero, out.at[pl.ds(n * ZROWS, ZROWS), :], zero_sems.at[n])
-        for n in range(out.shape[0] // ZROWS)
-    ]
-    for copy in clears:
-        copy.start()
     odd = lax.rem(lax.axis_index("row"), 2)
     line = lax.broadcasted_iota(jnp.int32, (META, BLK), 0)
     rows = left[pl.ds(HALF, META), :].astype(jnp.float32)
@@ -234,32 +227,37 @@
     meta_v[...] = rows.astype(jnp.int32)
     meta_copy = pltpu.make_async_copy(meta_v, meta, meta_sem)
     meta_copy.start()
+    zero[...] = jnp.zeros_like(zero)
+    clears = [
+        pltpu.make_async_copy(zero, out.at[pl.ds(n * ZROWS, ZROWS), :], zero_sems.at[n])
+        for n in range(out.shape[0] // ZROWS)
+    ]
+    for copy in clears:
+        copy.start()
     for at in range(TILES):
-        owner[at] = 0
+        table[at] = jnp.minimum(keep[at // NC, at % NC], 1) - 1
     choose(odd, r0, r1, right)
     products(((left, 0), (left, HALF + META)), right, prod)
     meta_copy.wait()
     total = gather(
         lambda a: meta[0, a],
         lambda b: meta[1 + odd, b],
-        lambda target: keep[target >> 3, target & (NC - 1)] != 0,
-        owner,
+        table,
+        table,
         prod,
         slot_of,
     )
 
+    for b in range(RCAP):
+        table[TILES + b] = meta[2 - odd, b]
+    for copy in clears:
+        copy.wait()
+
     def value(code, target):
         rows, cols = piece(code)
         return prod[rows, cols]
 
-    for copy in clears:
-        copy.wait()
     write(total, value, slot_of, stage, out, out_sems)
-    for i in range(MR):
-        for j in range(NC):
-            table[i * NC + j] = jnp.where(keep[i, j] != 0, owner[i * NC + j], -1)
-    for b in range(RCAP):
-        table[TILES + b] = meta[2 - odd, b]
 
 
 def first(keep, left, r0, r1):
@@ -279,7 +277,6 @@
             pltpu.VMEM((PAIRS, BLK, BLK), jnp.bfloat16),
             pltpu.VMEM((META, BLK), jnp.int32),
             pltpu.SMEM((META, BLK), jnp.int32),
-            pltpu.SMEM((TILES,), jnp.int32),
             pltpu.SMEM((PAIRS,), jnp.int32),
             pltpu.SemaphoreType.DMA,
             pltpu.SemaphoreType.DMA((PAIRS,)),
@@ -293,10 +290,12 @@
 
 
 def last_kernel(
-    table, left, more, r0, r1, before, zero, out,
-    right, prod, stage, meta_v, meta, owner, slot_of, meta_sem, out_sems,
+    table_in, left, more, r0, r1, before, zero, out,
+    table, table_sem, right, prod, stage, meta_v, meta, owner, slot_of, meta_sem, out_sems,
 ):
     del zero
+    table_copy = pltpu.make_async_copy(table_in, table, table_sem)
+    table_copy.start()
     odd = lax.rem(lax.axis_index("row"), 2)
     meta_v[...] = left[pl.ds(HALF, META), :].astype(jnp.float32).astype(jnp.int32)
     meta_copy = pltpu.make_async_copy(meta_v, meta, meta_sem)
@@ -306,10 +305,11 @@
     choose(odd, r1, r0, right)
     products(((left, 0), (more, 0)), right, prod)
     meta_copy.wait()
+    table_copy.wait()
     total = gather(
         lambda a: meta[0, a],
         lambda b: table[TILES + b],
-        lambda target: table[target] >= 0,
+        table,
         owner,
         prod,
         slot_of,
@@ -317,9 +317,9 @@
 
     def value(code, target):
         rows, cols = piece(code)
+        fresh = prod[rows, cols]
         held = table[target]
         old_rows, old_cols = piece(jnp.maximum(held - 1, 0))
-        fresh = prod[rows, cols]
         return jnp.where(held > 0, fresh + before[old_rows, old_cols], fresh)
 
     write(total, value, slot_of, stage, out, out_sems)
@@ -329,9 +329,11 @@
     return pl.pallas_call(
         last_kernel,
         out_shape=jax.ShapeDtypeStruct(out.shape, out.dtype),
-        in_specs=[spec(pltpu.SMEM)] + [spec(pltpu.VMEM)] * 5 + [spec(pltpu.HBM)],
+        in_specs=[spec(pl.ANY)] + [spec(pltpu.VMEM)] * 5 + [spec(pltpu.HBM)],
         out_specs=spec(pltpu.HBM),
         scratch_shapes=[
+            pltpu.SMEM(table.shape, jnp.int32),
+            pltpu.SemaphoreType.DMA,
             pltpu.VMEM((BLK, RCAP * BLK), jnp.bfloat16),
             pltpu.VMEM((LROWS, RCAP * BLK), jnp.float32),
             pltpu.VMEM((PAIRS, BLK, BLK), jnp.bfloat16),

time: 36.8 us -> 36.3 us (0.986)
  Pallas kernels: 13.5 us -> 13.1 us
    pallas_call x1, Pallas kernels: 3.35 us -> 2.87 us  [last(): pl.pallas_call(last_kernel, out_shape=jax.ShapeDtypeStruct(out.shape, out...]
where the time goes in v6:
time: 36.3 us; the launch traced here: 36 us
  starting transfers between devices  17.1 us (47%)
  Pallas kernels  13.1 us (36%)
  waiting for transfers between devices  4.95 us (14%)
  local copies, waits for them, and re-layouts  0.8 us (2%)
    ppermute x6, starting transfers between devices, send(): return lax.ppermute(value, ('row', 'col'), pairs)  17.1 us
    pallas_call x1, Pallas kernels, first(): pl.pallas_call(first_kernel, out_shape=(jax.ShapeDtypeStruct((MR * BLK, N...  6.54 us
    ppermute x6, waiting for transfers between devices, send(): return lax.ppermute(value, ('row', 'col'), pairs)  4.95 us
    pallas_call x1, Pallas kernels, last(): pl.pallas_call(last_kernel, out_shape=jax.ShapeDtypeStruct(out.shape, out...  2.87 us
    pallas_call x1, Pallas kernels, pack_left(): pl.pallas_call(pack_left_kernel, out_shape=(jax.ShapeDtypeStruct((LROWS +...  2.17 us
    pallas_call x1, Pallas kernels, pack_right(): pl.pallas_call(pack_right_kernel, out_shape=jax.ShapeDtypeStruct((BLK + M...  1.52 us
    unnamed x7, local copies, waits for them, and re-layouts  0.78 us
  transfers between devices with their start and end apart: 6, of which 1 were waited for; matrix products, arithmetic and copies ran while one was open for 0% of the time, Pallas kernels for 22%

profile of v6, /device:TPU:52, one launch (start us, length us, event | category | flops | bytes accessed | tf_op | source)
XLA Modules:
  0.0 36.0 jit_solution(9911482649742981616)
XLA Ops:
  0.0 0.0 copy-start
  0.0 0.0 copy-start.1
  0.0 0.7 %copy-done.1 = s32[32,4]{0,1:T(4,128)S(1)} copy-done((s32[32,4]{0,1:T(4,128)S(1)}, s32[32,4]{0,1:T(4,128)}, u32[]{:S(2)}) %copy-start.1) | copy-done | bytes 536
  0.7 0.0 copy-start.2
  0.7 2.2 %pack_left.1 = (bf16[2064,128]{1,0:T(8,128)(2,1)S(1)}, bf16[1024,128]{1,0:T(8,128)(2,1)S(1)}) custom-call(s32[4,32]{1,0:T(4,128)S(1)} %bitcast.1, bf16[4096,512]{1,0:T(8,128)(2,1)} %left.1), custom_call_target="tpu_custom_call" | custom-call | bytes 2097152 | tf_op jit(solution)/shard_map/pack_left/pallas_call | solution.py:72
  2.9 3.7 %collective-permute-start = (bf16[2064,128]{1,0:T(8,128)(2,1)S(1)}, bf16[2064,128]{1,0:T(8,128)(2,1)S(1)}, u32[]{:S(2)}, u32[]{:S(2)}) collective-permute-start(bf16[2064,128]{1,0:T(8,128)(2,1)S(1)} %get-tuple-element.10.after), channel_id=1, source_target_pairs={{0,0},{1,1},{2,2},{3,3},{4,4},{5,5},{6,6},{7,7},{8,8},{9,9},{10,10... | collective-permute-start | bytes 1585160 | tf_op jit(solution)/shard_map/ppermute | solution.py:375
  6.6 1.3 %collective-permute-start.4 = (bf16[1024,128]{1,0:T(8,128)(2,1)S(1)}, bf16[1024,128]{1,0:T(8,128)(2,1)S(1)}, u32[]{:S(2)}, u32[]{:S(2)}) collective-permute-start(bf16[1024,128]{1,0:T(8,128)(2,1)S(1)} %get-tuple-element.12), channel_id=1, source_target_pairs={{2,0},{3,1},{4,2},{5,3},{6,4},{7,5},{8,6},{9,7},{10,8},{11,9},{12,... | collective-permute-start | bytes 786440 | tf_op jit(solution)/shard_map/ppermute | solution.py:375
  7.9 0.0 copy-done
  7.9 1.5 %pack_right.1 = bf16[144,512]{1,0:T(8,128)(2,1)S(1)} custom-call(s32[8,8]{1,0:T(8,128)S(1)} %copy-done, bf16[1024,1024]{1,0:T(8,128)(2,1)} %right.1, bf16[2064,128]{1,0:T(8,128)(2,1)S(1)} %get-tuple-element.10.after), custom_call_target="tpu_custom_call" | custom-call | bytes 1048576 | tf_op jit(solution)/shard_map/pack_right/pallas_call | solution.py:122
  9.4 4.6 %collective-permute-start.2 = (bf16[144,512]{1,0:T(8,128)(2,1)S(1)}, bf16[144,512]{1,0:T(8,128)(2,1)S(1)}, u32[]{:S(2)}, u32[]{:S(2)}) collective-permute-start(bf16[144,512]{1,0:T(8,128)(2,1)S(1)} %pack_right.1), channel_id=1, source_target_pairs={{0,112},{1,113},{2,98},{3,99},{4,84},{5,85},{6,70},{7,71},{8,56},{... | collective-permute-start | bytes 442376 | tf_op jit(solution)/shard_map/ppermute | solution.py:375
  14.0 1.9 %collective-permute-start.1 = (bf16[144,512]{1,0:T(8,128)(2,1)S(1)}, bf16[144,512]{1,0:T(8,128)(2,1)S(1)}, u32[]{:S(2)}, u32[]{:S(2)}) collective-permute-start(bf16[144,512]{1,0:T(8,128)(2,1)S(1)} %pack_right.1), channel_id=1, source_target_pairs={{0,0},{1,1},{2,114},{3,115},{4,100},{5,101},{6,86},{7,87},{8,72},{... | collective-permute-start | bytes 442376 | tf_op jit(solution)/shard_map/ppermute | solution.py:375
  15.9 0.0 copy-done.2
  15.9 0.1 copy.7.keep
  16.0 0.0 collective-permute-done.4
  16.0 4.3 %collective-permute-start.5 = (bf16[1024,128]{1,0:T(8,128)(2,1)S(1)}, bf16[1024,128]{1,0:T(8,128)(2,1)S(1)}, u32[]{:S(2)}, u32[]{:S(2)}) collective-permute-start(bf16[1024,128]{1,0:T(8,128)(2,1)S(1)} %collective-permute-done.4), channel_id=1, source_target_pairs={{0,0},{1,1},{2,2},{3,3},{4,4},{5,5},{6,6},{7,7},{8,8},{9,9},{10,10... | collective-permute-start | bytes 786440 | tf_op jit(solution)/shard_map/ppermute | solution.py:375
  20.3 0.0 collective-permute-done.left
  20.3 1.3 %collective-permute-start.3 = (bf16[1040,128]{1,0:T(8,128)(2,1)S(1)}, bf16[1040,128]{1,0:T(8,128)(2,1)S(1)}, u32[]{:S(2)}, u32[]{:S(2)}) collective-permute-start(bf16[1040,128]{1,0:T(8,128)(2,1)S(1)} %slice.4), channel_id=1, source_target_pairs={{0,14},{1,15},{2,0},{3,1},{4,2},{5,3},{6,4},{7,5},{8,6},{9,7},{10,... | collective-permute-start | bytes 798728 | tf_op jit(solution)/shard_map/ppermute | solution.py:375
  21.6 0.0 collective-permute-done.2.r1
  21.6 4.9 %collective-permute-done.1.r0 = bf16[144,512]{1,0:T(8,128)(2,1)S(1)} collective-permute-done((bf16[144,512]{1,0:T(8,128)(2,1)S(1)}, bf16[144,512]{1,0:T(8,128)(2,1)S(1)}, u32[]{:S(2)}, u32[]{:S(2)}) %collective-permute-start.1) | collective-permute-done | bytes 147488 | tf_op jit(solution)/shard_map/ppermute | solution.py:375
  26.6 6.5 %first.1 = (bf16[4096,1024]{1,0:T(8,128)(2,1)}, f32[2048,512]{1,0:T(8,128)S(1)}, s32[384]{0:T(512)S(1)}) custom-call(s32[32,8]{1,0:T(8,128)S(1)} %copy.7.keep, bf16[2064,128]{1,0:T(8,128)(2,1)S(1)} %collective-permute-done.left, bf16[144,512]{1,0:T(8,128)(2,1)S(1)} %collective-permute-done.1.r0, bf16[144,512]{1,0:T(8,128)(2,1)S(1)} %collective-permute-done.2.r1), custom_call_target="tpu_custom_call" | custom-call | flops 10000000000 | bytes 14680064 | tf_op jit(solution)/shard_map/first/pallas_call | solution.py:264
  33.1 0.0 collective-permute-done.5.more
  33.1 0.0 collective-permute-done.3.left
  33.1 2.9 %last.1 = bf16[4096,1024]{1,0:T(8,128)(2,1)} custom-call(s32[384]{0:T(512)S(1)} %get-tuple-element.11.table_in, bf16[1040,128]{1,0:T(8,128)(2,1)S(1)} %collective-permute-done.3.left, bf16[1024,128]{1,0:T(8,128)(2,1)S(1)} %collective-permute-done.5.more, bf16[144,512]{1,0:T(8,128)(2,1)S(1)} %collective-permute-done.1.r0, ...), custom_call_target="tpu_custom_call", output_to_operand_aliasing={{}: (6, {})} | custom-call | flops 268435456 | bytes 4194304 | tf_op jit(solution)/shard_map/last/pallas_call | solution.py:329
  (1 shorter events, 0.0 us)
Async XLA Ops:
  0.0 7.9 %copy-start = (s32[8,8]{1,0:T(8,128)S(1)}, s32[8,8]{1,0:T(8,128)}, u32[]{:S(2)}) copy-start(s32[8,8]{1,0:T(8,128)} %pattern.1) | copy-start | bytes 772
  0.0 0.7 %copy-start.1 = (s32[32,4]{0,1:T(4,128)S(1)}, s32[32,4]{0,1:T(4,128)}, u32[]{:S(2)}) copy-start(s32[32,4]{0,1:T(4,128)} %param.6) | copy-start | bytes 1540
  0.7 15.2 %copy-start.2 = (s32[32,8]{0,1:T(8,128)S(1)}, s32[32,8]{0,1:T(8,128)}, u32[]{:S(2)}) copy-start(s32[32,8]{0,1:T(8,128)} %param.9) | copy-start | bytes 3076
  2.9 17.4 %collective-permute-start = (bf16[2064,128]{1,0:T(8,128)(2,1)S(1)}, bf16[2064,128]{1,0:T(8,128)(2,1)S(1)}, u32[]{:S(2)}, u32[]{:S(2)}) collective-permute-start(bf16[2064,128]{1,0:T(8,128)(2,1)S(1)} %get-tuple-element.10.after), channel_id=1, source_target_pairs={{0,0},{1,1},{2,2},{3,3},{4,4},{5,5},{6,6},{7,7},{8,8},{9,9},{10,10... | collective-permute-start | bytes 1585160 | tf_op jit(solution)/shard_map/ppermute | solution.py:375
  6.6 9.4 %collective-permute-start.4 = (bf16[1024,128]{1,0:T(8,128)(2,1)S(1)}, bf16[1024,128]{1,0:T(8,128)(2,1)S(1)}, u32[]{:S(2)}, u32[]{:S(2)}) collective-permute-start(bf16[1024,128]{1,0:T(8,128)(2,1)S(1)} %get-tuple-element.12), channel_id=1, source_target_pairs={{2,0},{3,1},{4,2},{5,3},{6,4},{7,5},{8,6},{9,7},{10,8},{11,9},{12,... | collective-permute-start | bytes 786440 | tf_op jit(solution)/shard_map/ppermute | solution.py:375
  9.4 12.2 %collective-permute-start.2 = (bf16[144,512]{1,0:T(8,128)(2,1)S(1)}, bf16[144,512]{1,0:T(8,128)(2,1)S(1)}, u32[]{:S(2)}, u32[]{:S(2)}) collective-permute-start(bf16[144,512]{1,0:T(8,128)(2,1)S(1)} %pack_right.1), channel_id=1, source_target_pairs={{0,112},{1,113},{2,98},{3,99},{4,84},{5,85},{6,70},{7,71},{8,56},{... | collective-permute-start | bytes 442376 | tf_op jit(solution)/shard_map/ppermute | solution.py:375
  14.0 12.6 %collective-permute-start.1 = (bf16[144,512]{1,0:T(8,128)(2,1)S(1)}, bf16[144,512]{1,0:T(8,128)(2,1)S(1)}, u32[]{:S(2)}, u32[]{:S(2)}) collective-permute-start(bf16[144,512]{1,0:T(8,128)(2,1)S(1)} %pack_right.1), channel_id=1, source_target_pairs={{0,0},{1,1},{2,114},{3,115},{4,100},{5,101},{6,86},{7,87},{8,72},{... | collective-permute-start | bytes 442376 | tf_op jit(solution)/shard_map/ppermute | solution.py:375
  16.0 17.1 %collective-permute-start.5 = (bf16[1024,128]{1,0:T(8,128)(2,1)S(1)}, bf16[1024,128]{1,0:T(8,128)(2,1)S(1)}, u32[]{:S(2)}, u32[]{:S(2)}) collective-permute-start(bf16[1024,128]{1,0:T(8,128)(2,1)S(1)} %collective-permute-done.4), channel_id=1, source_target_pairs={{0,0},{1,1},{2,2},{3,3},{4,4},{5,5},{6,6},{7,7},{8,8},{9,9},{10,10... | collective-permute-start | bytes 786440 | tf_op jit(solution)/shard_map/ppermute | solution.py:375
  20.3 12.8 %collective-permute-start.3 = (bf16[1040,128]{1,0:T(8,128)(2,1)S(1)}, bf16[1040,128]{1,0:T(8,128)(2,1)S(1)}, u32[]{:S(2)}, u32[]{:S(2)}) collective-permute-start(bf16[1040,128]{1,0:T(8,128)(2,1)S(1)} %slice.4), channel_id=1, source_target_pairs={{0,14},{1,15},{2,0},{3,1},{4,2},{5,3},{6,4},{7,5},{8,6},{9,7},{10,... | collective-permute-start | bytes 798728 | tf_op jit(solution)/shard_map/ppermute | solution.py:375

commit v7 on v6

--- a/solution.py
+++ b/solution.py
@@ -18,7 +18,6 @@
 HALF = LROWS // 2
 PAIRS = LCAP * RCAP
 TILES = MR * NC
-ZROWS = 256
 
 
 def block_of(ref, block_row, block_col):
@@ -135,6 +134,38 @@
     )(pattern, right, after)
 
 
+def blank_kernel(after, out, zero, sems):
+    del after
+    zero[...] = jnp.zeros_like(zero)
+    rows = zero.shape[0]
+    copies = [
+        pltpu.make_async_copy(zero, out.at[pl.ds(n * rows, rows), :], sems.at[n])
+        for n in range(out.shape[0] // rows)
+    ]
+    for copy in copies:
+        copy.start()
+    for copy in copies:
+        copy.wait()
+
+
+def blank(after, shape):
+    rows = 256
+    return pl.pallas_call(
+        blank_kernel,
+        out_shape=jax.ShapeDtypeStruct(shape, jnp.bfloat16),
+        in_specs=[spec(pl.ANY)],
+        out_specs=spec(pltpu.HBM),
+        scratch_shapes=[
+            pltpu.VMEM((rows, shape[1]), jnp.bfloat16),
+            pltpu.SemaphoreType.DMA((shape[0] // rows,)),
+        ],
+        cost_estimate=pl.CostEstimate(
+            flops=0, bytes_accessed=2 * shape[0] * shape[1], transcendentals=0
+        ),
+        name="blank",
+    )(after)
+
+
 def piece(code):
     return (
         pl.ds(pl.multiple_of((code >> 2) * BLK, BLK), BLK),
@@ -215,9 +246,10 @@
 
 
 def first_kernel(
-    keep, left, r0, r1, out, prod, table,
-    zero, zero_sems, right, stage, meta_v, meta, slot_of, meta_sem, out_sems,
+    keep, left, r0, r1, zero, out, prod, table,
+    right, stage, meta_v, meta, slot_of, meta_sem, out_sems,
 ):
+    del zero
     odd = lax.rem(lax.axis_index("row"), 2)
     line = lax.broadcasted_iota(jnp.int32, (META, BLK), 0)
     rows = left[pl.ds(HALF, META), :].astype(jnp.float32)
@@ -227,13 +259,6 @@
     meta_v[...] = rows.astype(jnp.int32)
     meta_copy = pltpu.make_async_copy(meta_v, meta, meta_sem)
     meta_copy.start()
-    zero[...] = jnp.zeros_like(zero)
-    clears = [
-        pltpu.make_async_copy(zero, out.at[pl.ds(n * ZROWS, ZROWS), :], zero_sems.at[n])
-        for n in range(out.shape[0] // ZROWS)
-    ]
-    for copy in clears:
-        copy.start()
     for at in range(TILES):
         table[at] = jnp.minimum(keep[at // NC, at % NC], 1) - 1
     choose(odd, r0, r1, right)
@@ -250,8 +275,6 @@
 
     for b in range(RCAP):
         table[TILES + b] = meta[2 - odd, b]
-    for copy in clears:
-        copy.wait()
 
     def value(code, target):
         rows, cols = piece(code)
@@ -260,19 +283,17 @@
     write(total, value, slot_of, stage, out, out_sems)
 
 
-def first(keep, left, r0, r1):
+def first(keep, left, r0, r1, zero):
     return pl.pallas_call(
         first_kernel,
         out_shape=(
-            jax.ShapeDtypeStruct((MR * BLK, NC * BLK), jnp.bfloat16),
+            jax.ShapeDtypeStruct(zero.shape, zero.dtype),
             jax.ShapeDtypeStruct((LROWS, RCAP * BLK), jnp.float32),
             jax.ShapeDtypeStruct((TILES + BLK,), jnp.int32),
         ),
-        in_specs=[spec(pltpu.SMEM)] + [spec(pltpu.VMEM)] * 3,
+        in_specs=[spec(pltpu.SMEM)] + [spec(pltpu.VMEM)] * 3 + [spec(pltpu.HBM)],
         out_specs=[spec(pltpu.HBM), spec(pltpu.VMEM), spec(pltpu.SMEM)],
         scratch_shapes=[
-            pltpu.VMEM((ZROWS, NC * BLK), jnp.bfloat16),
-            pltpu.SemaphoreType.DMA((MR * BLK // ZROWS,)),
             pltpu.VMEM((BLK, RCAP * BLK), jnp.bfloat16),
             pltpu.VMEM((PAIRS, BLK, BLK), jnp.bfloat16),
             pltpu.VMEM((META, BLK), jnp.int32),
@@ -281,12 +302,13 @@
             pltpu.SemaphoreType.DMA,
             pltpu.SemaphoreType.DMA((PAIRS,)),
         ],
+        input_output_aliases={4: 0},
         compiler_params=pltpu.CompilerParams(vmem_limit_bytes=32 << 20),
         cost_estimate=pl.CostEstimate(
             flops=10**10, bytes_accessed=14 << 20, transcendentals=0
         ),
         name="first",
-    )(keep, left, r0, r1)
+    )(keep, left, r0, r1, zero)
 
 
 def last_kernel(
@@ -390,12 +412,12 @@
     rpack = pack_right(right_pattern, right_matrix, whole)
     r0 = moved(rpack, lambda r, c: (r - c // group, c))
     r1 = moved(rpack, lambda r, c: (r - c // group - 1, c))
-    passed = moved(
-        lax.slice_in_dim(even, 0, HALF + META),
-        lambda r, c: (r, c + group * (2 * (r % 2) - 1)),
-    )
+    zero = blank(rpack, (left_matrix.shape[0], right_matrix.shape[1]))
+    part = lax.slice_in_dim(even, 0, HALF + META)
+    part, between = lax.optimization_barrier((part, between))
+    passed = moved(part, lambda r, c: (r, c + group * (2 * (r % 2) - 1)))
     more = send(between, [((r, roads[r, c][1]), (r, c)) for r, c in devices])
-    out, before, table = first(keep_mask, even, r0, r1)
+    out, before, table = first(keep_mask, even, r0, r1, zero)
     return last(table, passed, more, r0, r1, before, out)
 
 

time: 36.3 us -> 38.5 us (1.061)
  the two profiles are of different devices: /device:TPU:52 before, /device:TPU:26 now
where the time goes in v7:
time: 38.5 us; the launch traced here: 37.9 us
  starting transfers between devices  19.9 us (52%)
  Pallas kernels  13.9 us (36%)
  waiting for transfers between devices  2.52 us (7%)
  local copies, waits for them, and re-layouts  1.47 us (4%)
    ppermute x6, starting transfers between devices, send(): return lax.ppermute(value, ('row', 'col'), pairs)  19.9 us
    pallas_call x1, Pallas kernels, first(): pl.pallas_call(first_kernel, out_shape=(jax.ShapeDtypeStruct(zero.shape,...  4.33 us
    pallas_call x1, Pallas kernels, blank(): pl.pallas_call(blank_kernel, out_shape=jax.ShapeDtypeStruct(shape, jnp.bf...  3.45 us
    ppermute x6, waiting for transfers between devices, send(): return lax.ppermute(value, ('row', 'col'), pairs)  2.52 us
    pallas_call x1, Pallas kernels, last(): pl.pallas_call(last_kernel, out_shape=jax.ShapeDtypeStruct(out.shape, out...  2.49 us
    pallas_call x1, Pallas kernels, pack_left(): pl.pallas_call(pack_left_kernel, out_shape=(jax.ShapeDtypeStruct((LROWS +...  2.11 us
    pallas_call x1, Pallas kernels, pack_right(): pl.pallas_call(pack_right_kernel, out_shape=jax.ShapeDtypeStruct((BLK + M...  1.52 us
    unnamed x9, local copies, waits for them, and re-layouts  1.45 us
  transfers between devices with their start and end apart: 6, of which 2 were waited for; matrix products, arithmetic and copies ran while one was open for 0% of the time, Pallas kernels for 25%

profile of v7, /device:TPU:26, one launch (start us, length us, event | category | flops | bytes accessed | tf_op | source)
XLA Modules:
  0.0 37.9 jit_solution(5065494223336298734)
XLA Ops:
  0.0 0.0 copy-start.2
  0.0 0.7 %copy-done.2 = s32[32,4]{0,1:T(4,128)S(1)} copy-done((s32[32,4]{0,1:T(4,128)S(1)}, s32[32,4]{0,1:T(4,128)}, u32[]{:S(2)}) %copy-start.2) | copy-done | bytes 536
  0.7 0.0 copy-start.3
  0.7 2.1 %pack_left.1 = (bf16[2064,128]{1,0:T(8,128)(2,1)S(1)}, bf16[1024,128]{1,0:T(8,128)(2,1)S(1)}) custom-call(s32[4,32]{1,0:T(4,128)S(1)} %bitcast.1, bf16[4096,512]{1,0:T(8,128)(2,1)} %left.1), custom_call_target="tpu_custom_call" | custom-call | bytes 2097152 | tf_op jit(solution)/shard_map/pack_left/pallas_call | solution.py:71
  2.8 5.8 %collective-permute-start = (bf16[2064,128]{1,0:T(8,128)(2,1)S(1)}, bf16[2064,128]{1,0:T(8,128)(2,1)S(1)}, u32[]{:S(2)}, u32[]{:S(2)}) collective-permute-start(bf16[2064,128]{1,0:T(8,128)(2,1)S(1)} %get-tuple-element.12.after), channel_id=1, source_target_pairs={{0,0},{1,1},{2,2},{3,3},{4,4},{5,5},{6,6},{7,7},{8,8},{9,9},{10,10... | collective-permute-start | bytes 1585160 | tf_op jit(solution)/shard_map/ppermute | solution.py:397
  8.6 0.6 %collective-permute-start.3 = (bf16[1024,128]{1,0:T(8,128)(2,1)S(1)}, bf16[1024,128]{1,0:T(8,128)(2,1)S(1)}, u32[]{:S(2)}, u32[]{:S(2)}) collective-permute-start(bf16[1024,128]{1,0:T(8,128)(2,1)S(1)} %get-tuple-element.14), channel_id=1, source_target_pairs={{2,0},{3,1},{4,2},{5,3},{6,4},{7,5},{8,6},{9,7},{10,8},{11,9},{12,... | collective-permute-start | bytes 786440 | tf_op jit(solution)/shard_map/ppermute | solution.py:397
  9.2 0.0 copy-start.1
  9.2 0.7 %copy-done.1 = s32[8,8]{1,0:T(8,128)S(1)} copy-done((s32[8,8]{1,0:T(8,128)S(1)}, s32[8,8]{1,0:T(8,128)}, u32[]{:S(2)}) %copy-start.1) | copy-done | bytes 280
  9.9 1.5 %pack_right.1.after = bf16[144,512]{1,0:T(8,128)(2,1)S(1)} custom-call(s32[8,8]{1,0:T(8,128)S(1)} %copy-done.1, bf16[1024,1024]{1,0:T(8,128)(2,1)} %right.1, bf16[2064,128]{1,0:T(8,128)(2,1)S(1)} %get-tuple-element.12.after), custom_call_target="tpu_custom_call" | custom-call | bytes 1048576 | tf_op jit(solution)/shard_map/pack_right/pallas_call | solution.py:121
  11.4 0.0 copy-start
  11.4 2.8 %collective-permute-start.1 = (bf16[144,512]{1,0:T(8,128)(2,1)S(1)}, bf16[144,512]{1,0:T(8,128)(2,1)S(1)}, u32[]{:S(2)}, u32[]{:S(2)}) collective-permute-start(bf16[144,512]{1,0:T(8,128)(2,1)S(1)} %pack_right.1.after), channel_id=1, source_target_pairs={{0,0},{1,1},{2,114},{3,115},{4,100},{5,101},{6,86},{7,87},{8,72},{... | collective-permute-start | bytes 442376 | tf_op jit(solution)/shard_map/ppermute | solution.py:397
  14.2 2.5 %collective-permute-start.2 = (bf16[144,512]{1,0:T(8,128)(2,1)S(1)}, bf16[144,512]{1,0:T(8,128)(2,1)S(1)}, u32[]{:S(2)}, u32[]{:S(2)}) collective-permute-start(bf16[144,512]{1,0:T(8,128)(2,1)S(1)} %pack_right.1.after), channel_id=1, source_target_pairs={{0,112},{1,113},{2,98},{3,99},{4,84},{5,85},{6,70},{7,71},{8,56},{... | collective-permute-start | bytes 442376 | tf_op jit(solution)/shard_map/ppermute | solution.py:397
  16.7 0.0 copy-done
  16.7 3.5 %blank.1.zero = bf16[4096,1024]{1,0:T(8,128)(2,1)} custom-call(bf16[144,512]{1,0:T(8,128)(2,1)} %copy-done), custom_call_target="tpu_custom_call" | custom-call | bytes 8388608 | tf_op jit(solution)/shard_map/blank/pallas_call | solution.py:153
  20.1 0.0 copy-done.3
  20.1 0.1 copy.8.keep
  20.2 0.3 collective-permute-done.left
  20.6 0.0 collective-permute-done.3
  20.6 4.8 %collective-permute-start.4 = (bf16[1040,128]{1,0:T(8,128)(2,1)S(1)}, bf16[1040,128]{1,0:T(8,128)(2,1)S(1)}, u32[]{:S(2)}, u32[]{:S(2)}) collective-permute-start(bf16[1040,128]{1,0:T(8,128)(2,1)S(1)} %slice.4), channel_id=1, source_target_pairs={{0,14},{1,15},{2,0},{3,1},{4,2},{5,3},{6,4},{7,5},{8,6},{9,7},{10,... | collective-permute-start | bytes 798728 | tf_op jit(solution)/shard_map/ppermute | solution.py:397
  25.4 3.5 %collective-permute-start.5 = (bf16[1024,128]{1,0:T(8,128)(2,1)S(1)}, bf16[1024,128]{1,0:T(8,128)(2,1)S(1)}, u32[]{:S(2)}, u32[]{:S(2)}) collective-permute-start(bf16[1024,128]{1,0:T(8,128)(2,1)S(1)} %collective-permute-done.3), channel_id=1, source_target_pairs={{0,0},{1,1},{2,2},{3,3},{4,4},{5,5},{6,6},{7,7},{8,8},{9,9},{10,10... | collective-permute-start | bytes 786440 | tf_op jit(solution)/shard_map/ppermute | solution.py:397
  28.9 0.0 collective-permute-done.1.r0
  28.9 0.0 collective-permute-done.2.r1
  28.9 4.3 %first.1 = (bf16[4096,1024]{1,0:T(8,128)(2,1)}, f32[2048,512]{1,0:T(8,128)S(1)}, s32[384]{0:T(512)S(1)}) custom-call(s32[32,8]{1,0:T(8,128)S(1)} %copy.8.keep, bf16[2064,128]{1,0:T(8,128)(2,1)S(1)} %collective-permute-done.left, bf16[144,512]{1,0:T(8,128)(2,1)S(1)} %collective-permute-done.1.r0, ...), custom_call_target="tpu_custom_call", output_to_operand_aliasing={{0}: (4, {})} | custom-call | flops 10000000000 | bytes 14680064 | tf_op jit(solution)/shard_map/first/pallas_call | solution.py:287
  33.3 2.2 %collective-permute-done.5.more = bf16[1024,128]{1,0:T(8,128)(2,1)S(1)} collective-permute-done((bf16[1024,128]{1,0:T(8,128)(2,1)S(1)}, bf16[1024,128]{1,0:T(8,128)(2,1)S(1)}, u32[]{:S(2)}, u32[]{:S(2)}) %collective-permute-start.5) | collective-permute-done | bytes 262176 | tf_op jit(solution)/shard_map/ppermute | solution.py:397
  35.5 0.0 collective-permute-done.4.left
  35.5 2.5 %last.1 = bf16[4096,1024]{1,0:T(8,128)(2,1)} custom-call(s32[384]{0:T(512)S(1)} %get-tuple-element.13.table_in, bf16[1040,128]{1,0:T(8,128)(2,1)S(1)} %collective-permute-done.4.left, bf16[1024,128]{1,0:T(8,128)(2,1)S(1)} %collective-permute-done.5.more, bf16[144,512]{1,0:T(8,128)(2,1)S(1)} %collective-permute-done.1.r0, ...), custom_call_target="tpu_custom_call", output_to_operand_aliasing={{}: (6, {})} | custom-call | flops 268435456 | bytes 4194304 | tf_op jit(solution)/shard_map/last/pallas_call | solution.py:351
  (1 shorter events, 0.0 us)
Async XLA Ops:
  0.0 0.7 %copy-start.2 = (s32[32,4]{0,1:T(4,128)S(1)}, s32[32,4]{0,1:T(4,128)}, u32[]{:S(2)}) copy-start(s32[32,4]{0,1:T(4,128)} %param.6) | copy-start | bytes 1540
  0.7 19.5 %copy-start.3 = (s32[32,8]{0,1:T(8,128)S(1)}, s32[32,8]{0,1:T(8,128)}, u32[]{:S(2)}) copy-start(s32[32,8]{0,1:T(8,128)} %param.9) | copy-start | bytes 3076
  2.8 17.7 %collective-permute-start = (bf16[2064,128]{1,0:T(8,128)(2,1)S(1)}, bf16[2064,128]{1,0:T(8,128)(2,1)S(1)}, u32[]{:S(2)}, u32[]{:S(2)}) collective-permute-start(bf16[2064,128]{1,0:T(8,128)(2,1)S(1)} %get-tuple-element.12.after), channel_id=1, source_target_pairs={{0,0},{1,1},{2,2},{3,3},{4,4},{5,5},{6,6},{7,7},{8,8},{9,9},{10,10... | collective-permute-start | bytes 1585160 | tf_op jit(solution)/shard_map/ppermute | solution.py:397
  8.6 12.0 %collective-permute-start.3 = (bf16[1024,128]{1,0:T(8,128)(2,1)S(1)}, bf16[1024,128]{1,0:T(8,128)(2,1)S(1)}, u32[]{:S(2)}, u32[]{:S(2)}) collective-permute-start(bf16[1024,128]{1,0:T(8,128)(2,1)S(1)} %get-tuple-element.14), channel_id=1, source_target_pairs={{2,0},{3,1},{4,2},{5,3},{6,4},{7,5},{8,6},{9,7},{10,8},{11,9},{12,... | collective-permute-start | bytes 786440 | tf_op jit(solution)/shard_map/ppermute | solution.py:397
  9.2 0.7 %copy-start.1 = (s32[8,8]{1,0:T(8,128)S(1)}, s32[8,8]{1,0:T(8,128)}, u32[]{:S(2)}) copy-start(s32[8,8]{1,0:T(8,128)} %pattern.1) | copy-start | bytes 772
  11.4 5.2 %copy-start = (bf16[144,512]{1,0:T(8,128)(2,1)}, bf16[144,512]{1,0:T(8,128)(2,1)S(1)}, u32[]{:S(2)}) copy-start(bf16[144,512]{1,0:T(8,128)(2,1)S(1)} %pack_right.1.after) | copy-start | bytes 442372
  11.4 17.5 %collective-permute-start.1 = (bf16[144,512]{1,0:T(8,128)(2,1)S(1)}, bf16[144,512]{1,0:T(8,128)(2,1)S(1)}, u32[]{:S(2)}, u32[]{:S(2)}) collective-permute-start(bf16[144,512]{1,0:T(8,128)(2,1)S(1)} %pack_right.1.after), channel_id=1, source_target_pairs={{0,0},{1,1},{2,114},{3,115},{4,100},{5,101},{6,86},{7,87},{8,72},{... | collective-permute-start | bytes 442376 | tf_op jit(solution)/shard_map/ppermute | solution.py:397
  14.2 14.7 %collective-permute-start.2 = (bf16[144,512]{1,0:T(8,128)(2,1)S(1)}, bf16[144,512]{1,0:T(8,128)(2,1)S(1)}, u32[]{:S(2)}, u32[]{:S(2)}) collective-permute-start(bf16[144,512]{1,0:T(8,128)(2,1)S(1)} %pack_right.1.after), channel_id=1, source_target_pairs={{0,112},{1,113},{2,98},{3,99},{4,84},{5,85},{6,70},{7,71},{8,56},{... | collective-permute-start | bytes 442376 | tf_op jit(solution)/shard_map/ppermute | solution.py:397
  20.6 14.9 %collective-permute-start.4 = (bf16[1040,128]{1,0:T(8,128)(2,1)S(1)}, bf16[1040,128]{1,0:T(8,128)(2,1)S(1)}, u32[]{:S(2)}, u32[]{:S(2)}) collective-permute-start(bf16[1040,128]{1,0:T(8,128)(2,1)S(1)} %slice.4), channel_id=1, source_target_pairs={{0,14},{1,15},{2,0},{3,1},{4,2},{5,3},{6,4},{7,5},{8,6},{9,7},{10,... | collective-permute-start | bytes 798728 | tf_op jit(solution)/shard_map/ppermute | solution.py:397
  25.4 10.0 %collective-permute-start.5 = (bf16[1024,128]{1,0:T(8,128)(2,1)S(1)}, bf16[1024,128]{1,0:T(8,128)(2,1)S(1)}, u32[]{:S(2)}, u32[]{:S(2)}) collective-permute-start(bf16[1024,128]{1,0:T(8,128)(2,1)S(1)} %collective-permute-done.3), channel_id=1, source_target_pairs={{0,0},{1,1},{2,2},{3,3},{4,4},{5,5},{6,6},{7,7},{8,8},{9,9},{10,10... | collective-permute-start | bytes 786440 | tf_op jit(solution)/shard_map/ppermute | solution.py:397

commit v8 on v5

--- a/solution.py
+++ b/solution.py
@@ -15,7 +15,9 @@
 RCAP = 4
 META = 16
 LROWS = LCAP * BLK
-HALF = LROWS // 2
+ACAP = 6
+HALF = ACAP * BLK
+REST = LROWS - HALF
 PAIRS = LCAP * RCAP
 TILES = MR * NC
 ZROWS = 256
@@ -52,7 +54,7 @@
         if a * BLK >= HALF:
             copies.append(
                 pltpu.make_async_copy(
-                    block, more.at[pl.ds(a * BLK - HALF, BLK), :], sems.at[LCAP + a - LCAP // 2]
+                    block, more.at[pl.ds(a * BLK - HALF, BLK), :], sems.at[LCAP + a - ACAP]
                 )
             )
             copies[-1].start()
@@ -63,7 +65,7 @@
     for k in range(KS + 1):
         row = jnp.where(lane == LCAP + k, starts[k], row)
     meta[...] = row.astype(jnp.float32).astype(jnp.bfloat16)
-    copies.append(pltpu.make_async_copy(meta, out.at[pl.ds(HALF, META), :], sems.at[LCAP + LCAP // 2]))
+    copies.append(pltpu.make_async_copy(meta, out.at[pl.ds(HALF, META), :], sems.at[2 * LCAP - ACAP]))
     copies[-1].start()
     for copy in copies:
         copy.wait()
@@ -74,14 +76,14 @@
         pack_left_kernel,
         out_shape=(
             jax.ShapeDtypeStruct((LROWS + META, BLK), jnp.bfloat16),
-            jax.ShapeDtypeStruct((HALF, BLK), jnp.bfloat16),
+            jax.ShapeDtypeStruct((REST, BLK), jnp.bfloat16),
         ),
         in_specs=[spec(pltpu.SMEM), spec(pltpu.HBM)],
         out_specs=[spec(pl.ANY)] * 2,
         scratch_shapes=[
             pltpu.SMEM((LCAP + 1,), jnp.int32),
             pltpu.VMEM((META, BLK), jnp.bfloat16),
-            pltpu.SemaphoreType.DMA((LCAP + LCAP // 2 + 1,)),
+            pltpu.SemaphoreType.DMA((2 * LCAP - ACAP + 1,)),
         ],
         compiler_params=pltpu.CompilerParams(vmem_limit_bytes=52 << 20),
         cost_estimate=pl.CostEstimate(flops=0, bytes_accessed=2 << 20, transcendentals=0),
@@ -143,13 +145,13 @@
     )
 
 
-def products(halves, right, prod):
-    chunk = 512
+def products(left, more, begin, right, prod):
+    chunk = 256
     rhs = right[...]
-    for n, (ref, begin) in enumerate(halves):
-        for first in range(0, HALF, chunk):
-            prod[pl.ds(n * HALF + first, chunk), :] = jnp.dot(
-                ref[pl.ds(begin + first, chunk), :], rhs, preferred_element_type=jnp.float32
+    for ref, at, place, size in ((left, 0, 0, HALF), (more, begin, HALF, REST)):
+        for first in range(0, size, chunk):
+            prod[pl.ds(place + first, chunk), :] = jnp.dot(
+                ref[pl.ds(at + first, chunk), :], rhs, preferred_element_type=jnp.float32
             )
 
 
@@ -217,7 +219,7 @@
     for at in range(TILES):
         table[at] = jnp.minimum(keep[at // NC, at % NC], 1) - 1
     choose(odd, r0, r1, right)
-    products(((left, 0), (left, HALF + META)), right, prod)
+    products(left, left, HALF + META, right, prod)
     meta_copy.wait()
     total = gather(
         lambda a: meta[0, a],
@@ -282,7 +284,7 @@
     for at in range(TILES):
         owner[at] = 0
     choose(odd, r1, r0, right)
-    products(((left, 0), (more, 0)), right, prod)
+    products(left, more, 0, right, prod)
     meta_copy.wait()
     table_copy.wait()
     total = gather(

time: 35.9 us -> 35.9 us (level)
  starting transfers between devices: 17.1 us -> 15.7 us
  waiting for transfers between devices: 4.97 us -> 6.33 us
    ppermute x6, starting transfers between devices: 17.1 us -> 15.7 us  [send(): return lax.ppermute(value, ('row', 'col'), pairs)]
    ppermute x6, waiting for transfers between devices: 4.97 us -> 6.33 us  [send(): return lax.ppermute(value, ('row', 'col'), pairs)]
  transfers between devices with their start and end apart: 6 -> 6, of which waited for: 1 -> 2; matrix products, arithmetic and copies ran while one was open for 0% -> 0% of each run, Pallas kernels for 19% -> 19%
where the time goes in v8:
time: 35.9 us; the launch traced here: 35.5 us
  starting transfers between devices  15.7 us (44%)
  Pallas kernels  12.6 us (35%)
  waiting for transfers between devices  6.33 us (18%)
  local copies, waits for them, and re-layouts  0.79 us (2%)
    ppermute x6, starting transfers between devices, send(): return lax.ppermute(value, ('row', 'col'), pairs)  15.7 us
    ppermute x6, waiting for transfers between devices, send(): return lax.ppermute(value, ('row', 'col'), pairs)  6.33 us
    pallas_call x1, Pallas kernels, first(): pl.pallas_call(first_kernel, out_shape=(jax.ShapeDtypeStruct((MR * BLK, N...  5.18 us
    pallas_call x1, Pallas kernels, last(): pl.pallas_call(last_kernel, out_shape=jax.ShapeDtypeStruct(out.shape, out...  3.76 us
    pallas_call x1, Pallas kernels, pack_left(): pl.pallas_call(pack_left_kernel, out_shape=(jax.ShapeDtypeStruct((LROWS +...  2.11 us
    pallas_call x1, Pallas kernels, pack_right(): pl.pallas_call(pack_right_kernel, out_shape=jax.ShapeDtypeStruct((BLK + M...  1.52 us
    unnamed x7, local copies, waits for them, and re-layouts  0.78 us
  transfers between devices with their start and end apart: 6, of which 2 were waited for; matrix products, arithmetic and copies ran while one was open for 0% of the time, Pallas kernels for 19%

profile of v8, /device:TPU:52, one launch (start us, length us, event | category | flops | bytes accessed | tf_op | source)
XLA Modules:
  0.0 35.5 jit_solution(12490541201187748159)
XLA Ops:
  0.0 0.0 copy-start
  0.0 0.0 copy-start.1
  0.0 0.7 %copy-done.1 = s32[32,4]{0,1:T(4,128)S(1)} copy-done((s32[32,4]{0,1:T(4,128)S(1)}, s32[32,4]{0,1:T(4,128)}, u32[]{:S(2)}) %copy-start.1) | copy-done | bytes 536
  0.7 0.0 copy-start.2
  0.7 2.1 %pack_left.1 = (bf16[2064,128]{1,0:T(8,128)(2,1)S(1)}, bf16[1280,128]{1,0:T(8,128)(2,1)S(1)}) custom-call(s32[4,32]{1,0:T(4,128)S(1)} %bitcast.1, bf16[4096,512]{1,0:T(8,128)(2,1)} %left.1), custom_call_target="tpu_custom_call" | custom-call | bytes 2097152 | tf_op jit(solution)/shard_map/pack_left/pallas_call | solution.py:75
  2.8 3.8 %collective-permute-start = (bf16[2064,128]{1,0:T(8,128)(2,1)S(1)}, bf16[2064,128]{1,0:T(8,128)(2,1)S(1)}, u32[]{:S(2)}, u32[]{:S(2)}) collective-permute-start(bf16[2064,128]{1,0:T(8,128)(2,1)S(1)} %get-tuple-element.10.after), channel_id=1, source_target_pairs={{0,0},{1,1},{2,2},{3,3},{4,4},{5,5},{6,6},{7,7},{8,8},{9,9},{10,10... | collective-permute-start | bytes 1585160 | tf_op jit(solution)/shard_map/ppermute | solution.py:386
  6.7 1.3 %collective-permute-start.4 = (bf16[1280,128]{1,0:T(8,128)(2,1)S(1)}, bf16[1280,128]{1,0:T(8,128)(2,1)S(1)}, u32[]{:S(2)}, u32[]{:S(2)}) collective-permute-start(bf16[1280,128]{1,0:T(8,128)(2,1)S(1)} %get-tuple-element.12), channel_id=1, source_target_pairs={{2,0},{3,1},{4,2},{5,3},{6,4},{7,5},{8,6},{9,7},{10,8},{11,9},{12,... | collective-permute-start | bytes 983048 | tf_op jit(solution)/shard_map/ppermute | solution.py:386
  8.0 0.0 copy-done
  8.0 1.5 %pack_right.1 = bf16[144,512]{1,0:T(8,128)(2,1)S(1)} custom-call(s32[8,8]{1,0:T(8,128)S(1)} %copy-done, bf16[1024,1024]{1,0:T(8,128)(2,1)} %right.1, bf16[2064,128]{1,0:T(8,128)(2,1)S(1)} %get-tuple-element.10.after), custom_call_target="tpu_custom_call" | custom-call | bytes 1048576 | tf_op jit(solution)/shard_map/pack_right/pallas_call | solution.py:125
  9.5 4.4 %collective-permute-start.2 = (bf16[144,512]{1,0:T(8,128)(2,1)S(1)}, bf16[144,512]{1,0:T(8,128)(2,1)S(1)}, u32[]{:S(2)}, u32[]{:S(2)}) collective-permute-start(bf16[144,512]{1,0:T(8,128)(2,1)S(1)} %pack_right.1), channel_id=1, source_target_pairs={{0,112},{1,113},{2,98},{3,99},{4,84},{5,85},{6,70},{7,71},{8,56},{... | collective-permute-start | bytes 442376 | tf_op jit(solution)/shard_map/ppermute | solution.py:386
  13.9 1.9 %collective-permute-start.1 = (bf16[144,512]{1,0:T(8,128)(2,1)S(1)}, bf16[144,512]{1,0:T(8,128)(2,1)S(1)}, u32[]{:S(2)}, u32[]{:S(2)}) collective-permute-start(bf16[144,512]{1,0:T(8,128)(2,1)S(1)} %pack_right.1), channel_id=1, source_target_pairs={{0,0},{1,1},{2,114},{3,115},{4,100},{5,101},{6,86},{7,87},{8,72},{... | collective-permute-start | bytes 442376 | tf_op jit(solution)/shard_map/ppermute | solution.py:386
  15.9 0.0 copy-done.2
  15.9 0.1 copy.7.keep
  16.0 1.4 %collective-permute-done.4 = bf16[1280,128]{1,0:T(8,128)(2,1)S(1)} collective-permute-done((bf16[1280,128]{1,0:T(8,128)(2,1)S(1)}, bf16[1280,128]{1,0:T(8,128)(2,1)S(1)}, u32[]{:S(2)}, u32[]{:S(2)}) %collective-permute-start.4) | collective-permute-done | bytes 327712 | tf_op jit(solution)/shard_map/ppermute | solution.py:386
  17.4 3.6 %collective-permute-start.5 = (bf16[1280,128]{1,0:T(8,128)(2,1)S(1)}, bf16[1280,128]{1,0:T(8,128)(2,1)S(1)}, u32[]{:S(2)}, u32[]{:S(2)}) collective-permute-start(bf16[1280,128]{1,0:T(8,128)(2,1)S(1)} %collective-permute-done.4), channel_id=1, source_target_pairs={{0,0},{1,1},{2,2},{3,3},{4,4},{5,5},{6,6},{7,7},{8,8},{9,9},{10,10... | collective-permute-start | bytes 983048 | tf_op jit(solution)/shard_map/ppermute | solution.py:386
  21.0 0.0 collective-permute-done.left
  21.0 0.6 %collective-permute-start.3 = (bf16[784,128]{1,0:T(8,128)(2,1)S(1)}, bf16[784,128]{1,0:T(8,128)(2,1)S(1)}, u32[]{:S(2)}, u32[]{:S(2)}) collective-permute-start(bf16[784,128]{1,0:T(8,128)(2,1)S(1)} %slice.4), channel_id=1, source_target_pairs={{0,14},{1,15},{2,0},{3,1},{4,2},{5,3},{6,4},{7,5},{8,6},{9,7},{10,... | collective-permute-start | bytes 602120 | tf_op jit(solution)/shard_map/ppermute | solution.py:386
  21.6 0.0 collective-permute-done.2.r1
  21.6 4.9 %collective-permute-done.1.r0 = bf16[144,512]{1,0:T(8,128)(2,1)S(1)} collective-permute-done((bf16[144,512]{1,0:T(8,128)(2,1)S(1)}, bf16[144,512]{1,0:T(8,128)(2,1)S(1)}, u32[]{:S(2)}, u32[]{:S(2)}) %collective-permute-start.1) | collective-permute-done | bytes 147488 | tf_op jit(solution)/shard_map/ppermute | solution.py:386
  26.5 5.2 %first.1 = (bf16[4096,1024]{1,0:T(8,128)(2,1)}, f32[2048,512]{1,0:T(8,128)S(1)}, s32[384]{0:T(512)S(1)}) custom-call(s32[32,8]{1,0:T(8,128)S(1)} %copy.7.keep, bf16[2064,128]{1,0:T(8,128)(2,1)S(1)} %collective-permute-done.left, bf16[144,512]{1,0:T(8,128)(2,1)S(1)} %collective-permute-done.1.r0, bf16[144,512]{1,0:T(8,128)(2,1)S(1)} %collective-permute-done.2.r1), custom_call_target="tpu_custom_call" | custom-call | flops 10000000000 | bytes 14680064 | tf_op jit(solution)/shard_map/first/pallas_call | solution.py:247
  31.7 0.0 collective-permute-done.5.more
  31.7 0.0 collective-permute-done.3.left
  31.7 3.8 %last.1 = bf16[4096,1024]{1,0:T(8,128)(2,1)} custom-call(s32[384]{0:T(512)S(1)} %get-tuple-element.11.table_in, bf16[784,128]{1,0:T(8,128)(2,1)S(1)} %collective-permute-done.3.left, bf16[1280,128]{1,0:T(8,128)(2,1)S(1)} %collective-permute-done.5.more, bf16[144,512]{1,0:T(8,128)(2,1)S(1)} %collective-permute-done.1.r0, ...), custom_call_target="tpu_custom_call", output_to_operand_aliasing={{}: (6, {})} | custom-call | flops 268435456 | bytes 4194304 | tf_op jit(solution)/shard_map/last/pallas_call | solution.py:340
  (1 shorter events, 0.0 us)
Async XLA Ops:
  0.0 8.0 %copy-start = (s32[8,8]{1,0:T(8,128)S(1)}, s32[8,8]{1,0:T(8,128)}, u32[]{:S(2)}) copy-start(s32[8,8]{1,0:T(8,128)} %pattern.1) | copy-start | bytes 772
  0.0 0.7 %copy-start.1 = (s32[32,4]{0,1:T(4,128)S(1)}, s32[32,4]{0,1:T(4,128)}, u32[]{:S(2)}) copy-start(s32[32,4]{0,1:T(4,128)} %param.6) | copy-start | bytes 1540
  0.7 15.2 %copy-start.2 = (s32[32,8]{0,1:T(8,128)S(1)}, s32[32,8]{0,1:T(8,128)}, u32[]{:S(2)}) copy-start(s32[32,8]{0,1:T(8,128)} %param.9) | copy-start | bytes 3076
  2.8 18.1 %collective-permute-start = (bf16[2064,128]{1,0:T(8,128)(2,1)S(1)}, bf16[2064,128]{1,0:T(8,128)(2,1)S(1)}, u32[]{:S(2)}, u32[]{:S(2)}) collective-permute-start(bf16[2064,128]{1,0:T(8,128)(2,1)S(1)} %get-tuple-element.10.after), channel_id=1, source_target_pairs={{0,0},{1,1},{2,2},{3,3},{4,4},{5,5},{6,6},{7,7},{8,8},{9,9},{10,10... | collective-permute-start | bytes 1585160 | tf_op jit(solution)/shard_map/ppermute | solution.py:386
  6.7 10.7 %collective-permute-start.4 = (bf16[1280,128]{1,0:T(8,128)(2,1)S(1)}, bf16[1280,128]{1,0:T(8,128)(2,1)S(1)}, u32[]{:S(2)}, u32[]{:S(2)}) collective-permute-start(bf16[1280,128]{1,0:T(8,128)(2,1)S(1)} %get-tuple-element.12), channel_id=1, source_target_pairs={{2,0},{3,1},{4,2},{5,3},{6,4},{7,5},{8,6},{9,7},{10,8},{11,9},{12,... | collective-permute-start | bytes 983048 | tf_op jit(solution)/shard_map/ppermute | solution.py:386
  9.5 12.1 %collective-permute-start.2 = (bf16[144,512]{1,0:T(8,128)(2,1)S(1)}, bf16[144,512]{1,0:T(8,128)(2,1)S(1)}, u32[]{:S(2)}, u32[]{:S(2)}) collective-permute-start(bf16[144,512]{1,0:T(8,128)(2,1)S(1)} %pack_right.1), channel_id=1, source_target_pairs={{0,112},{1,113},{2,98},{3,99},{4,84},{5,85},{6,70},{7,71},{8,56},{... | collective-permute-start | bytes 442376 | tf_op jit(solution)/shard_map/ppermute | solution.py:386
  13.9 12.6 %collective-permute-start.1 = (bf16[144,512]{1,0:T(8,128)(2,1)S(1)}, bf16[144,512]{1,0:T(8,128)(2,1)S(1)}, u32[]{:S(2)}, u32[]{:S(2)}) collective-permute-start(bf16[144,512]{1,0:T(8,128)(2,1)S(1)} %pack_right.1), channel_id=1, source_target_pairs={{0,0},{1,1},{2,114},{3,115},{4,100},{5,101},{6,86},{7,87},{8,72},{... | collective-permute-start | bytes 442376 | tf_op jit(solution)/shard_map/ppermute | solution.py:386
  17.4 14.4 %collective-permute-start.5 = (bf16[1280,128]{1,0:T(8,128)(2,1)S(1)}, bf16[1280,128]{1,0:T(8,128)(2,1)S(1)}, u32[]{:S(2)}, u32[]{:S(2)}) collective-permute-start(bf16[1280,128]{1,0:T(8,128)(2,1)S(1)} %collective-permute-done.4), channel_id=1, source_target_pairs={{0,0},{1,1},{2,2},{3,3},{4,4},{5,5},{6,6},{7,7},{8,8},{9,9},{10,10... | collective-permute-start | bytes 983048 | tf_op jit(solution)/shard_map/ppermute | solution.py:386
  21.0 10.7 %collective-permute-start.3 = (bf16[784,128]{1,0:T(8,128)(2,1)S(1)}, bf16[784,128]{1,0:T(8,128)(2,1)S(1)}, u32[]{:S(2)}, u32[]{:S(2)}) collective-permute-start(bf16[784,128]{1,0:T(8,128)(2,1)S(1)} %slice.4), channel_id=1, source_target_pairs={{0,14},{1,15},{2,0},{3,1},{4,2},{5,3},{6,4},{7,5},{8,6},{9,7},{10,... | collective-permute-start | bytes 602120 | tf_op jit(solution)/shard_map/ppermute | solution.py:386

commit v9 on v8

--- a/solution.py
+++ b/solution.py
@@ -20,7 +20,6 @@
 REST = LROWS - HALF
 PAIRS = LCAP * RCAP
 TILES = MR * NC
-ZROWS = 256
 NOTES = TILES + 64
 
 
@@ -138,6 +137,38 @@
     )(pattern, right, after)
 
 
+def blank_kernel(after, out, zero, sems):
+    del after
+    zero[...] = jnp.zeros_like(zero)
+    rows = zero.shape[0]
+    copies = [
+        pltpu.make_async_copy(zero, out.at[pl.ds(n * rows, rows), :], sems.at[n])
+        for n in range(out.shape[0] // rows)
+    ]
+    for copy in copies:
+        copy.start()
+    for copy in copies:
+        copy.wait()
+
+
+def blank(after, shape):
+    rows = 256
+    return pl.pallas_call(
+        blank_kernel,
+        out_shape=jax.ShapeDtypeStruct(shape, jnp.bfloat16),
+        in_specs=[spec(pl.ANY)],
+        out_specs=spec(pltpu.HBM),
+        scratch_shapes=[
+            pltpu.VMEM((rows, shape[1]), jnp.bfloat16),
+            pltpu.SemaphoreType.DMA((shape[0] // rows,)),
+        ],
+        cost_estimate=pl.CostEstimate(
+            flops=10**10, bytes_accessed=2 * shape[0] * shape[1], transcendentals=0
+        ),
+        name="blank",
+    )(after)
+
+
 def piece(code):
     return (
         pl.ds(pl.multiple_of((code >> 2) * BLK, BLK), BLK),
@@ -197,16 +228,9 @@
 
 
 def first_kernel(
-    keep, left, r0, r1, out, prod, table,
-    zero, zero_sems, right, meta_v, meta, slot_of, meta_sem,
+    keep, left, r0, r1, prod, table,
+    right, meta_v, meta, slot_of, meta_sem,
 ):
-    zero[...] = jnp.zeros_like(zero)
-    clears = [
-        pltpu.make_async_copy(zero, out.at[pl.ds(n * ZROWS, ZROWS), :], zero_sems.at[n])
-        for n in range(out.shape[0] // ZROWS)
-    ]
-    for copy in clears:
-        copy.start()
     odd = lax.rem(lax.axis_index("row"), 2)
     line = lax.broadcasted_iota(jnp.int32, (META, BLK), 0)
     rows = left[pl.ds(HALF, META), :].astype(jnp.float32)
@@ -239,23 +263,18 @@
         return carry
 
     lax.fori_loop(0, total, note, 0)
-    for copy in clears:
-        copy.wait()
 
 
 def first(keep, left, r0, r1):
     return pl.pallas_call(
         first_kernel,
         out_shape=(
-            jax.ShapeDtypeStruct((MR * BLK, NC * BLK), jnp.bfloat16),
             jax.ShapeDtypeStruct((LROWS, RCAP * BLK), jnp.float32),
             jax.ShapeDtypeStruct((NOTES + PAIRS,), jnp.int32),
         ),
         in_specs=[spec(pltpu.SMEM)] + [spec(pltpu.VMEM)] * 3,
-        out_specs=[spec(pltpu.HBM), spec(pltpu.VMEM), spec(pltpu.SMEM)],
+        out_specs=[spec(pltpu.VMEM), spec(pltpu.SMEM)],
         scratch_shapes=[
-            pltpu.VMEM((ZROWS, NC * BLK), jnp.bfloat16),
-            pltpu.SemaphoreType.DMA((MR * BLK // ZROWS,)),
             pltpu.VMEM((BLK, RCAP * BLK), jnp.bfloat16),
             pltpu.VMEM((META, BLK), jnp.int32),
             pltpu.SMEM((META, BLK), jnp.int32),
@@ -264,7 +283,7 @@
         ],
         compiler_params=pltpu.CompilerParams(vmem_limit_bytes=32 << 20),
         cost_estimate=pl.CostEstimate(
-            flops=10**10, bytes_accessed=14 << 20, transcendentals=0
+            flops=2 * PAIRS * BLK**3, bytes_accessed=14 << 20, transcendentals=0
         ),
         name="first",
     )(keep, left, r0, r1)
@@ -406,8 +425,9 @@
         lambda r, c: (r, c + group * (2 * (r % 2) - 1)),
     )
     more = send(between, [((r, roads[r, c][1]), (r, c)) for r, c in devices])
-    out, before, table = first(keep_mask, even, r0, r1)
-    return last(table, passed, more, r0, r1, before, out)
+    zero = blank(even, (left_matrix.shape[0], right_matrix.shape[1]))
+    before, table = first(keep_mask, even, r0, r1)
+    return last(table, passed, more, r0, r1, before, zero)
 
 
 def solution(mesh):

time: 35.9 us -> 38.5 us (1.072)
  the two profiles are of different devices: /device:TPU:52 before, /device:TPU:16 now
where the time goes in v9:
time: 38.5 us; the launch traced here: 37.9 us
  starting transfers between devices  19.2 us (50%)
  Pallas kernels  13.6 us (35%)
  waiting for transfers between devices  3.06 us (8%)
  local copies, waits for them, and re-layouts  1.83 us (5%)
    ppermute x6, starting transfers between devices, send(): return lax.ppermute(value, ('row', 'col'), pairs)  19.2 us
    pallas_call x1, Pallas kernels, last(): pl.pallas_call(last_kernel, out_shape=jax.ShapeDtypeStruct(out.shape, out...  3.56 us
    pallas_call x1, Pallas kernels, blank(): pl.pallas_call(blank_kernel, out_shape=jax.ShapeDtypeStruct(shape, jnp.bf...  3.45 us
    ppermute x6, waiting for transfers between devices, send(): return lax.ppermute(value, ('row', 'col'), pairs)  3.06 us
    pallas_call x1, Pallas kernels, first(): pl.pallas_call(first_kernel, out_shape=(jax.ShapeDtypeStruct((LROWS, RCAP...  2.89 us
    pallas_call x1, Pallas kernels, pack_left(): pl.pallas_call(pack_left_kernel, out_shape=(jax.ShapeDtypeStruct((LROWS +...  2.15 us
    unnamed x11, local copies, waits for them, and re-layouts  1.82 us
    pallas_call x1, Pallas kernels, pack_right(): pl.pallas_call(pack_right_kernel, out_shape=jax.ShapeDtypeStruct((BLK + M...  1.52 us
  transfers between devices with their start and end apart: 6, of which 1 were waited for; matrix products, arithmetic and copies ran while one was open for 0% of the time, Pallas kernels for 21%

profile of v9, /device:TPU:16, one launch (start us, length us, event | category | flops | bytes accessed | tf_op | source)
XLA Modules:
  0.0 37.9 jit_solution(593053792424792403)
XLA Ops:
  0.0 0.0 copy-start.2
  0.0 0.0 copy-start.3
  0.0 0.7 %copy-done.3 = s32[32,4]{0,1:T(4,128)S(1)} copy-done((s32[32,4]{0,1:T(4,128)S(1)}, s32[32,4]{0,1:T(4,128)}, u32[]{:S(2)}) %copy-start.3) | copy-done | bytes 536
  0.7 0.0 copy-start.4
  0.7 2.1 %pack_left.1 = (bf16[2064,128]{1,0:T(8,128)(2,1)S(1)}, bf16[1280,128]{1,0:T(8,128)(2,1)S(1)}) custom-call(s32[4,32]{1,0:T(4,128)S(1)} %bitcast.1, bf16[4096,512]{1,0:T(8,128)(2,1)} %left.1), custom_call_target="tpu_custom_call" | custom-call | bytes 2097152 | tf_op jit(solution)/shard_map/pack_left/pallas_call | solution.py:74
  2.9 5.9 %collective-permute-start = (bf16[2064,128]{1,0:T(8,128)(2,1)S(1)}, bf16[2064,128]{1,0:T(8,128)(2,1)S(1)}, u32[]{:S(2)}, u32[]{:S(2)}) collective-permute-start(bf16[2064,128]{1,0:T(8,128)(2,1)S(1)} %get-tuple-element.9.after), channel_id=1, source_target_pairs={{0,0},{1,1},{2,2},{3,3},{4,4},{5,5},{6,6},{7,7},{8,8},{9,9},{10,10... | collective-permute-start | bytes 1585160 | tf_op jit(solution)/shard_map/ppermute | solution.py:405
  8.8 0.1 collective-permute-start.4
  8.9 0.0 copy-done.2
  8.9 1.5 %pack_right.1 = bf16[144,512]{1,0:T(8,128)(2,1)S(1)} custom-call(s32[8,8]{1,0:T(8,128)S(1)} %copy-done.2, bf16[1024,1024]{1,0:T(8,128)(2,1)} %right.1, bf16[2064,128]{1,0:T(8,128)(2,1)S(1)} %get-tuple-element.9.after), custom_call_target="tpu_custom_call" | custom-call | bytes 1048576 | tf_op jit(solution)/shard_map/pack_right/pallas_call | solution.py:124
  10.4 3.8 %collective-permute-start.2 = (bf16[144,512]{1,0:T(8,128)(2,1)S(1)}, bf16[144,512]{1,0:T(8,128)(2,1)S(1)}, u32[]{:S(2)}, u32[]{:S(2)}) collective-permute-start(bf16[144,512]{1,0:T(8,128)(2,1)S(1)} %pack_right.1), channel_id=1, source_target_pairs={{0,112},{1,113},{2,98},{3,99},{4,84},{5,85},{6,70},{7,71},{8,56},{... | collective-permute-start | bytes 442376 | tf_op jit(solution)/shard_map/ppermute | solution.py:405
  14.2 0.7 %collective-permute-start.1 = (bf16[144,512]{1,0:T(8,128)(2,1)S(1)}, bf16[144,512]{1,0:T(8,128)(2,1)S(1)}, u32[]{:S(2)}, u32[]{:S(2)}) collective-permute-start(bf16[144,512]{1,0:T(8,128)(2,1)S(1)} %pack_right.1), channel_id=1, source_target_pairs={{0,0},{1,1},{2,114},{3,115},{4,100},{5,101},{6,86},{7,87},{8,72},{... | collective-permute-start | bytes 442376 | tf_op jit(solution)/shard_map/ppermute | solution.py:405
  14.9 0.0 copy-done.4
  14.9 0.1 copy.7.keep
  15.0 3.0 %collective-permute-done.4 = bf16[1280,128]{1,0:T(8,128)(2,1)S(1)} collective-permute-done((bf16[1280,128]{1,0:T(8,128)(2,1)S(1)}, bf16[1280,128]{1,0:T(8,128)(2,1)S(1)}, u32[]{:S(2)}, u32[]{:S(2)}) %collective-permute-start.4) | collective-permute-done | bytes 327712 | tf_op jit(solution)/shard_map/ppermute | solution.py:405
  18.0 4.1 %collective-permute-start.5 = (bf16[1280,128]{1,0:T(8,128)(2,1)S(1)}, bf16[1280,128]{1,0:T(8,128)(2,1)S(1)}, u32[]{:S(2)}, u32[]{:S(2)}) collective-permute-start(bf16[1280,128]{1,0:T(8,128)(2,1)S(1)} %collective-permute-done.4), channel_id=1, source_target_pairs={{0,0},{1,1},{2,2},{3,3},{4,4},{5,5},{6,6},{7,7},{8,8},{9,9},{10,10... | collective-permute-start | bytes 983048 | tf_op jit(solution)/shard_map/ppermute | solution.py:405
  22.1 0.0 collective-permute-done.left.after
  22.2 0.0 copy-start
  22.2 4.7 %collective-permute-start.3 = (bf16[784,128]{1,0:T(8,128)(2,1)S(1)}, bf16[784,128]{1,0:T(8,128)(2,1)S(1)}, u32[]{:S(2)}, u32[]{:S(2)}) collective-permute-start(bf16[784,128]{1,0:T(8,128)(2,1)S(1)} %slice.4), channel_id=1, source_target_pairs={{0,14},{1,15},{2,0},{3,1},{4,2},{5,3},{6,4},{7,5},{8,6},{9,7},{10,... | collective-permute-start | bytes 602120 | tf_op jit(solution)/shard_map/ppermute | solution.py:405
  26.9 0.0 copy-done
  26.9 3.4 %blank.1.zero = bf16[4096,1024]{1,0:T(8,128)(2,1)} custom-call(bf16[2064,128]{1,0:T(8,128)(2,1)} %copy-done), custom_call_target="tpu_custom_call" | custom-call | flops 10000000000 | bytes 8388608 | tf_op jit(solution)/shard_map/blank/pallas_call | solution.py:156
  30.3 0.0 collective-permute-done.2.r1
  30.3 0.0 collective-permute-done.1.r0
  30.3 0.0 copy-start.1
  30.3 1.0 %copy-done.1 = bf16[2064,128]{1,0:T(8,128)(2,1)S(1)} copy-done((bf16[2064,128]{1,0:T(8,128)(2,1)S(1)}, bf16[2064,128]{1,0:T(8,128)(2,1)}, u32[]{:S(2)}) %copy-start.1) | copy-done | bytes 528408
  31.4 2.9 %first.1 = (f32[2048,512]{1,0:T(8,128)S(1)}, s32[384]{0:T(512)S(1)}) custom-call(s32[32,8]{1,0:T(8,128)S(1)} %copy.7.keep, bf16[2064,128]{1,0:T(8,128)(2,1)S(1)} %copy-done.1, bf16[144,512]{1,0:T(8,128)(2,1)S(1)} %collective-permute-done.1.r0, bf16[144,512]{1,0:T(8,128)(2,1)S(1)} %collective-permute-done.2.r1), custom_call_target="tpu_custom_call" | custom-call | flops 268435456 | bytes 14680064 | tf_op jit(solution)/shard_map/first/pallas_call | solution.py:269
  34.3 0.0 collective-permute-done.5.more
  34.3 0.0 collective-permute-done.3.left
  34.3 3.6 %last.1 = bf16[4096,1024]{1,0:T(8,128)(2,1)} custom-call(s32[384]{0:T(512)S(1)} %get-tuple-element.10.table_in, bf16[784,128]{1,0:T(8,128)(2,1)S(1)} %collective-permute-done.3.left, bf16[1280,128]{1,0:T(8,128)(2,1)S(1)} %collective-permute-done.5.more, bf16[144,512]{1,0:T(8,128)(2,1)S(1)} %collective-permute-done.1.r0, ...), custom_call_target="tpu_custom_call", output_to_operand_aliasing={{}: (6, {})} | custom-call | flops 268435456 | bytes 4194304 | tf_op jit(solution)/shard_map/last/pallas_call | solution.py:359
  (1 shorter events, 0.0 us)
Async XLA Ops:
  0.0 8.9 %copy-start.2 = (s32[8,8]{1,0:T(8,128)S(1)}, s32[8,8]{1,0:T(8,128)}, u32[]{:S(2)}) copy-start(s32[8,8]{1,0:T(8,128)} %pattern.1) | copy-start | bytes 772
  0.0 0.7 %copy-start.3 = (s32[32,4]{0,1:T(4,128)S(1)}, s32[32,4]{0,1:T(4,128)}, u32[]{:S(2)}) copy-start(s32[32,4]{0,1:T(4,128)} %param.6) | copy-start | bytes 1540
  0.7 14.2 %copy-start.4 = (s32[32,8]{0,1:T(8,128)S(1)}, s32[32,8]{0,1:T(8,128)}, u32[]{:S(2)}) copy-start(s32[32,8]{0,1:T(8,128)} %param.9) | copy-start | bytes 3076
  2.9 19.3 %collective-permute-start = (bf16[2064,128]{1,0:T(8,128)(2,1)S(1)}, bf16[2064,128]{1,0:T(8,128)(2,1)S(1)}, u32[]{:S(2)}, u32[]{:S(2)}) collective-permute-start(bf16[2064,128]{1,0:T(8,128)(2,1)S(1)} %get-tuple-element.9.after), channel_id=1, source_target_pairs={{0,0},{1,1},{2,2},{3,3},{4,4},{5,5},{6,6},{7,7},{8,8},{9,9},{10,10... | collective-permute-start | bytes 1585160 | tf_op jit(solution)/shard_map/ppermute | solution.py:405
  8.8 9.3 %collective-permute-start.4 = (bf16[1280,128]{1,0:T(8,128)(2,1)S(1)}, bf16[1280,128]{1,0:T(8,128)(2,1)S(1)}, u32[]{:S(2)}, u32[]{:S(2)}) collective-permute-start(bf16[1280,128]{1,0:T(8,128)(2,1)S(1)} %get-tuple-element.11), channel_id=1, source_target_pairs={{2,0},{3,1},{4,2},{5,3},{6,4},{7,5},{8,6},{9,7},{10,8},{11,9},{12,... | collective-permute-start | bytes 983048 | tf_op jit(solution)/shard_map/ppermute | solution.py:405
  10.4 19.9 %collective-permute-start.2 = (bf16[144,512]{1,0:T(8,128)(2,1)S(1)}, bf16[144,512]{1,0:T(8,128)(2,1)S(1)}, u32[]{:S(2)}, u32[]{:S(2)}) collective-permute-start(bf16[144,512]{1,0:T(8,128)(2,1)S(1)} %pack_right.1), channel_id=1, source_target_pairs={{0,112},{1,113},{2,98},{3,99},{4,84},{5,85},{6,70},{7,71},{8,56},{... | collective-permute-start | bytes 442376 | tf_op jit(solution)/shard_map/ppermute | solution.py:405
  14.2 16.1 %collective-permute-start.1 = (bf16[144,512]{1,0:T(8,128)(2,1)S(1)}, bf16[144,512]{1,0:T(8,128)(2,1)S(1)}, u32[]{:S(2)}, u32[]{:S(2)}) collective-permute-start(bf16[144,512]{1,0:T(8,128)(2,1)S(1)} %pack_right.1), channel_id=1, source_target_pairs={{0,0},{1,1},{2,114},{3,115},{4,100},{5,101},{6,86},{7,87},{8,72},{... | collective-permute-start | bytes 442376 | tf_op jit(solution)/shard_map/ppermute | solution.py:405
  18.0 16.3 %collective-permute-start.5 = (bf16[1280,128]{1,0:T(8,128)(2,1)S(1)}, bf16[1280,128]{1,0:T(8,128)(2,1)S(1)}, u32[]{:S(2)}, u32[]{:S(2)}) collective-permute-start(bf16[1280,128]{1,0:T(8,128)(2,1)S(1)} %collective-permute-done.4), channel_id=1, source_target_pairs={{0,0},{1,1},{2,2},{3,3},{4,4},{5,5},{6,6},{7,7},{8,8},{9,9},{10,10... | collective-permute-start | bytes 983048 | tf_op jit(solution)/shard_map/ppermute | solution.py:405
  22.2 4.7 %copy-start = (bf16[2064,128]{1,0:T(8,128)(2,1)}, bf16[2064,128]{1,0:T(8,128)(2,1)S(1)}, u32[]{:S(2)}) copy-start(bf16[2064,128]{1,0:T(8,128)(2,1)S(1)} %collective-permute-done.left.after) | copy-start | bytes 1585156
  22.2 12.1 %collective-permute-start.3 = (bf16[784,128]{1,0:T(8,128)(2,1)S(1)}, bf16[784,128]{1,0:T(8,128)(2,1)S(1)}, u32[]{:S(2)}, u32[]{:S(2)}) collective-permute-start(bf16[784,128]{1,0:T(8,128)(2,1)S(1)} %slice.4), channel_id=1, source_target_pairs={{0,14},{1,15},{2,0},{3,1},{4,2},{5,3},{6,4},{7,5},{8,6},{9,7},{10,... | collective-permute-start | bytes 602120 | tf_op jit(solution)/shard_map/ppermute | solution.py:405
  30.3 1.0 %copy-start.1 = (bf16[2064,128]{1,0:T(8,128)(2,1)S(1)}, bf16[2064,128]{1,0:T(8,128)(2,1)}, u32[]{:S(2)}) copy-start(bf16[2064,128]{1,0:T(8,128)(2,1)} %copy-done) | copy-start | bytes 1585156
